TPU v7x, 32 devices: a whole 2x2x4 slice. The times are simulated.
32 devices in a mesh: dp: 8 (over z, x), tensor: 4 (over y, core).
Axes of the slice: x: 2, y: 2, z: 4, core: 2. Of those that a mesh axis runs over, the one named last changes fastest.
Arguments:
- inputs: bfloat16 [2, 1024, 2560], P(None, 'dp'), may hold values from -6 to 6
- cotangent: bfloat16 [2, 1024, 2560], P(None, 'dp'), may hold values from -6 to 6
- prefix: int32 [2], replicated, may hold values from 102 to 512
- gain_attn: bfloat16 [2560], P('dp'), may hold values from 0.099609375 to 1.8984375
- w_query: bfloat16 [2560, 2560], P('dp', 'tensor'), may hold values from -0.15625 to 0.15625
- w_key: bfloat16 [2560, 640], P('dp', 'tensor'), may hold values from -0.15625 to 0.15625
- w_value: bfloat16 [2560, 640], P('dp', 'tensor'), may hold values from -0.125 to 0.125
- w_out: bfloat16 [2560, 2560], P('tensor', 'dp'), may hold values from -1 to 1
- gain_mlp: bfloat16 [2560], P('dp'), may hold values from 0.099609375 to 1.8984375
- w_gate: bfloat16 [2560, 7168], P('dp', 'tensor'), may hold values from -0.125 to 0.125
- w_up: bfloat16 [2560, 7168], P('dp', 'tensor'), may hold values from -0.125 to 0.125
- w_down: bfloat16 [7168, 2560], P('tensor', 'dp'), may hold values from -0.0625 to 0.0625
Outputs:
- result: float32 [2, 1024, 2560], P(None, 'dp')
- input_grad: float32 [2, 1024, 2560], P(None, 'dp')
- gain_attn_grad: float32 [2560], P('dp')
- w_query_grad: float32 [2560, 2560], P('dp', 'tensor')
- w_key_grad: float32 [2560, 640], P('dp', 'tensor')
- w_value_grad: float32 [2560, 640], P('dp', 'tensor')
- w_out_grad: float32 [2560, 2560], P('tensor', 'dp')
- gain_mlp_grad: float32 [2560], P('dp')
- w_gate_grad: float32 [2560, 7168], P('dp', 'tensor')
- w_up_grad: float32 [2560, 7168], P('dp', 'tensor')
- w_down_grad: float32 [7168, 2560], P('tensor', 'dp')
Inputs may be any that keep to these rules, and one draw needn't show every extreme that they name: Every position of sequence s sees the first prefix[s] positions of that sequence.
All inputs are finite; a program needn't handle non-finite values.
Results may differ from a plain program's by a relative error of at most 0.014.
The roundings to bfloat16 on the way count: a program that leaves them out, or rounds other values in their place, can miss the bound.
Values may be sent and summed in bfloat16 or wider, within the bound.
No kernel may reach another device: no remote copies, remote signals or barrier semaphores. Data moves between devices by JAX's collectives and lax.ppermute only.
A program may use at most 176 MiB of HBM per device.

v0:
```python
import jax
import jax.numpy as jnp
from jax import lax
from jax.sharding import PartitionSpec as P

HEAD_DIM = 80


EPSILON = 1e-05
NEGATIVE = -1e30


def batch_groups(number):
    groups = []
    first = 0
    while number - first > 2:
        groups.append((first, 2))
        first = first + 2
    while first < number:
        groups.append((first, 1))
        first = first + 1
    return groups


def contract_last(left, right):
    return lax.dot_general(
        left, right, (((1,), (1,)), ((), ())), preferred_element_type=jnp.float32
    )


def contract_first(left, right):
    return lax.dot_general(
        left, right, (((0,), (0,)), ((), ())), preferred_element_type=jnp.float32
    )


def fetch_weights(w_query, w_key, w_value, w_out, w_gate, w_up, w_down, gain_attn, gain_mlp):
    row_parts = (
        lax.all_gather(w_query, "dp", axis=0, tiled=True),
        lax.all_gather(w_key, "dp", axis=0, tiled=True),
        lax.all_gather(w_value, "dp", axis=0, tiled=True),
        lax.all_gather(w_gate, "dp", axis=0, tiled=True),
        lax.all_gather(w_up, "dp", axis=0, tiled=True),
        lax.all_gather(gain_attn, "dp", axis=0, tiled=True),
        lax.all_gather(gain_mlp, "dp", axis=0, tiled=True),
    )
    column_parts = (
        lax.all_gather(w_out, "dp", axis=1, tiled=True),
        lax.all_gather(w_down, "dp", axis=1, tiled=True),
    )
    return tuple(row_parts) + tuple(column_parts)


def visible_mask(prefix_part, first_row, rows, length):
    query_pos = first_row + lax.iota(jnp.int32, rows)
    key_pos = lax.iota(jnp.int32, length)
    causal = key_pos[None, None, :] <= query_pos[None, :, None]
    shared = key_pos[None, None, :] < prefix_part[:, None, None]
    return (causal | shared)[:, None, None, :, :]


def attention_scores(query_heads, keys_all, allowed, scale):
    scores = (
        jnp.einsum("nqkgd,ntkd->nkgqt", query_heads, keys_all, preferred_element_type=jnp.float32)
        * scale
    )
    return jnp.where(allowed, scores, NEGATIVE)


def run_batch(x_part, cot_part, prefix_part, copies, first_row):
    w_query, w_key, w_value, w_gate, w_up, gain_attn, gain_mlp, w_out, w_down = copies
    seqs, rows, width = x_part.shape
    tokens = seqs * rows
    kv_local = w_key.shape[1] // HEAD_DIM
    group = w_query.shape[1] // w_key.shape[1]
    scale = HEAD_DIM ** (-0.5)
    gain_one = gain_attn.astype(jnp.float32)
    gain_two = gain_mlp.astype(jnp.float32)
    flat = x_part.astype(jnp.float32).reshape(tokens, width)
    recip_one = lax.rsqrt(jnp.mean(flat * flat, -1, keepdims=True) + EPSILON)
    normal_one = flat * recip_one
    attn_in = (normal_one * gain_one).astype(jnp.bfloat16)
    queries = jnp.dot(attn_in, w_query, preferred_element_type=jnp.float32).astype(jnp.bfloat16)
    keys_own = jnp.dot(attn_in, w_key, preferred_element_type=jnp.float32).astype(jnp.bfloat16)
    values_own = jnp.dot(attn_in, w_value, preferred_element_type=jnp.float32).astype(jnp.bfloat16)
    keys_all, values_all = (
        lax.all_gather(keys_own.reshape(seqs, rows, -1), "dp", axis=1, tiled=True),
        lax.all_gather(values_own.reshape(seqs, rows, -1), "dp", axis=1, tiled=True),
    )
    length = keys_all.shape[1]
    keys_all = keys_all.reshape(seqs, length, kv_local, HEAD_DIM)
    values_all = values_all.reshape(seqs, length, kv_local, HEAD_DIM)
    query_heads = queries.reshape(seqs, rows, kv_local, group, HEAD_DIM)
    allowed = visible_mask(prefix_part, first_row, rows, length)
    scores = attention_scores(query_heads, keys_all, allowed, scale)
    top = jnp.max(scores, -1, keepdims=True)
    expo = jnp.exp(scores - top)
    total = jnp.sum(expo, -1, keepdims=True)
    probs = expo / total
    log_parts = top + jnp.log(total)
    mixed_parts = jnp.einsum(
        "nkgqt,ntkd->nqkgd",
        probs.astype(jnp.bfloat16),
        values_all,
        preferred_element_type=jnp.float32,
    )
    heads = mixed_parts.astype(jnp.bfloat16).reshape(tokens, -1)
    attn_out = lax.psum(jnp.dot(heads, w_out, preferred_element_type=jnp.float32), "tensor")
    hidden = flat + attn_out
    recip_two = lax.rsqrt(jnp.mean(hidden * hidden, -1, keepdims=True) + EPSILON)
    normal_two = hidden * recip_two
    mlp_in = (normal_two * gain_two).astype(jnp.bfloat16)
    gate = jnp.dot(mlp_in, w_gate, preferred_element_type=jnp.float32)
    up = jnp.dot(mlp_in, w_up, preferred_element_type=jnp.float32)
    sigma = jax.nn.sigmoid(gate)
    product = (gate * sigma * up).astype(jnp.bfloat16)
    mlp_out = lax.psum(
        jnp.dot(product, w_down, preferred_element_type=jnp.float32).astype(jnp.bfloat16), "tensor"
    ).astype(jnp.float32)
    result = hidden + mlp_out
    out_grad = cot_part.astype(jnp.float32).reshape(tokens, width)
    mlp_grad = out_grad.astype(jnp.bfloat16)
    product_grad = contract_last(mlp_grad, w_down)
    up_grad = (product_grad * gate * sigma).astype(jnp.bfloat16)
    gate_grad = (product_grad * up * sigma * (1.0 + gate * (1.0 - sigma))).astype(jnp.bfloat16)
    mlp_in_grad = lax.psum(
        contract_last(gate_grad, w_gate) + contract_last(up_grad, w_up), "tensor"
    )
    scaled_two = mlp_in_grad * gain_two
    hidden_grad = out_grad + recip_two * (
        scaled_two - normal_two * jnp.mean(scaled_two * normal_two, -1, keepdims=True)
    )
    gain_two_term = jnp.sum(mlp_in_grad * normal_two, 0)
    attn_grad = hidden_grad.astype(jnp.bfloat16)
    heads_grad = (
        contract_last(attn_grad, w_out)
        .astype(jnp.bfloat16)
        .reshape(seqs, rows, kv_local, group, HEAD_DIM)
    )
    scores = attention_scores(query_heads, keys_all, allowed, scale)
    probs = jnp.exp(scores - log_parts)
    probs_low = probs.astype(jnp.bfloat16)
    prob_grad = jnp.einsum(
        "nqkgd,ntkd->nkgqt", heads_grad, values_all, preferred_element_type=jnp.float32
    )
    score_grad = (probs * (prob_grad - jnp.sum(probs * prob_grad, -1, keepdims=True))).astype(
        jnp.bfloat16
    )
    query_parts = (
        jnp.einsum("nkgqt,ntkd->nqkgd", score_grad, keys_all, preferred_element_type=jnp.float32)
        * scale
    )
    key_parts = (
        jnp.einsum("nkgqt,nqkgd->ntkd", score_grad, query_heads, preferred_element_type=jnp.float32)
        * scale
    )
    value_parts = jnp.einsum(
        "nkgqt,nqkgd->ntkd", probs_low, heads_grad, preferred_element_type=jnp.float32
    )
    query_grad = query_parts.astype(jnp.bfloat16).reshape(tokens, -1)
    key_sum, value_sum = (
        lax.psum_scatter(
            key_parts.reshape(seqs, length, -1), "dp", scatter_dimension=1, tiled=True
        ),
        lax.psum_scatter(
            value_parts.reshape(seqs, length, -1), "dp", scatter_dimension=1, tiled=True
        ),
    )
    key_grad = key_sum.astype(jnp.bfloat16).reshape(tokens, -1)
    value_grad = value_sum.astype(jnp.bfloat16).reshape(tokens, -1)
    attn_in_grad = lax.psum(
        contract_last(query_grad, w_query)
        + contract_last(key_grad, w_key)
        + contract_last(value_grad, w_value),
        "tensor",
    )
    scaled_one = attn_in_grad * gain_one
    input_grad = hidden_grad + recip_one * (
        scaled_one - normal_one * jnp.mean(scaled_one * normal_one, -1, keepdims=True)
    )
    gain_one_term = jnp.sum(attn_in_grad * normal_one, 0)
    factors = (
        attn_in,
        jnp.concatenate([query_grad, key_grad, value_grad], 1),
        mlp_in,
        jnp.concatenate([gate_grad, up_grad], 1),
        attn_grad,
        heads,
        mlp_grad,
        product,
    )
    gains = jnp.stack([gain_one_term, gain_two_term])
    return (
        result.reshape(seqs, rows, width),
        input_grad.reshape(seqs, rows, width),
        factors,
        gains,
    )


def reduce_grads(factors, gains):
    attn_in, attn_in_grads, mlp_in, mlp_in_grads, attn_grad, heads, mlp_grad, product = factors
    left_attn = attn_in
    left_mlp = mlp_in
    row_sum = lax.psum_scatter(
        jnp.concatenate(
            [contract_first(left_attn, attn_in_grads), contract_first(left_mlp, mlp_in_grads)], 1
        ),
        "dp",
        scatter_dimension=0,
        tiled=True,
    )
    left_attn = attn_grad
    left_mlp = mlp_grad
    column_sum = lax.psum_scatter(
        jnp.concatenate([contract_first(left_attn, heads), contract_first(left_mlp, product)], 1),
        "dp",
        scatter_dimension=0,
        tiled=True,
    )
    gain_sum = lax.psum_scatter(gains, "dp", scatter_dimension=1, tiled=True)
    return (row_sum, column_sum, gain_sum)


def per_device(
    inputs,
    cotangent,
    prefix,
    gain_attn,
    w_query,
    w_key,
    w_value,
    w_out,
    gain_mlp,
    w_gate,
    w_up,
    w_down,
):
    seqs, rows, width = inputs.shape
    first_row = lax.axis_index("dp") * rows
    outputs = []
    input_grads = []
    kept = []
    gain_terms = []
    totals = None
    for first, number in batch_groups(seqs):
        copies = fetch_weights(
            w_query, w_key, w_value, w_out, w_gate, w_up, w_down, gain_attn, gain_mlp
        )
        result, input_grad, factors, gains = run_batch(
            inputs[first : first + number],
            cotangent[first : first + number],
            prefix[first : first + number],
            copies,
            first_row,
        )
        outputs.append(result)
        input_grads.append(input_grad)
        kept.append(factors)
        gain_terms.append(gains)
    joined = tuple(
        (jnp.concatenate([factors[index] for factors in kept], 0) for index in range(len(kept[0])))
    )
    totals = reduce_grads(joined, sum(gain_terms))
    row_sum, column_sum, gain_sum = totals
    head_cols = w_query.shape[1]
    kv_cols = w_key.shape[1]
    ff_cols = w_gate.shape[1]
    query_wgrad = row_sum[:, :head_cols]
    key_wgrad = row_sum[:, head_cols : head_cols + kv_cols]
    value_wgrad = row_sum[:, head_cols + kv_cols : head_cols + 2 * kv_cols]
    gate_wgrad = row_sum[:, head_cols + 2 * kv_cols : head_cols + 2 * kv_cols + ff_cols]
    up_wgrad = row_sum[:, head_cols + 2 * kv_cols + ff_cols :]
    out_wgrad = column_sum[:, :head_cols].T
    down_wgrad = column_sum[:, head_cols:].T
    return (
        jnp.concatenate(outputs, 0),
        jnp.concatenate(input_grads, 0),
        gain_sum[0],
        query_wgrad,
        key_wgrad,
        value_wgrad,
        out_wgrad,
        gain_sum[1],
        gate_wgrad,
        up_wgrad,
        down_wgrad,
    )


def solution(mesh):
    return jax.shard_map(
        per_device,
        mesh=mesh,
        in_specs=(
            P(None, "dp", None),
            P(None, "dp", None),
            P(),
            P("dp"),
            P("dp", "tensor"),
            P("dp", "tensor"),
            P("dp", "tensor"),
            P("tensor", "dp"),
            P("dp"),
            P("dp", "tensor"),
            P("dp", "tensor"),
            P("tensor", "dp"),
        ),
        out_specs=(
            P(None, "dp", None),
            P(None, "dp", None),
            P("dp"),
            P("dp", "tensor"),
            P("dp", "tensor"),
            P("dp", "tensor"),
            P("tensor", "dp"),
            P("dp"),
            P("dp", "tensor"),
            P("dp", "tensor"),
            P("tensor", "dp"),
        ),
        check_vma=False,
    )
```

profile of v0, /device:TPU:0, one launch (start us, length us, event | category | flops | bytes accessed | tf_op | source)
XLA Modules:
  0.0 2441.5 jit_solution(389851777984547737)
XLA Ops:
  12.4 39.3 %all-reduce.5 = (bf16[2560]{0:T(1024)(128)(2,1)S(1)}, bf16[2560]{0:T(1024)(128)(2,1)S(1)}) all-reduce(bf16[2560]{0:T(1024)(128)(2,1)S(1)} %dynamic-update-slice, bf16[2560]{0:T(1024)(128)(2,1)S(1)} %dynamic-update-slice.1), channel_id=1, replica_groups=mesh['dp'=8,'tensor'=4] {'dp'}, use_global_device_ids=true, to_apply=%add | all-reduce | flops 5120 | bytes 20480
  53.4 35.4 %all-gather.4 = bf16[8,320,160]{1,2,0:T(8,128)(2,1)S(1)} all-gather(bf16[1,320,160]{1,2,0:T(8,128)(2,1)S(1)} %bitcast.322), channel_id=1, replica_groups=mesh['dp'=8,'tensor'=4] {'dp'}, dimensions={0}, use_global_device_ids=true | all-gather | bytes 921600 | tf_op jit(solution)/shard_map/all_gather | solution.py:41
  89.8 34.2 %all-gather.5 = bf16[8,320,160]{1,2,0:T(8,128)(2,1)S(1)} all-gather(bf16[1,320,160]{1,2,0:T(8,128)(2,1)S(1)} %bitcast.323), channel_id=1, replica_groups=mesh['dp'=8,'tensor'=4] {'dp'}, dimensions={0}, use_global_device_ids=true | all-gather | bytes 921600 | tf_op jit(solution)/shard_map/all_gather | solution.py:40
  130.0 29.9 %all-gather.2 = bf16[1024,160]{0,1:T(8,128)(2,1)} all-gather(bf16[128,160]{0,1:T(8,128)(2,1)S(1)} %convolution_convert_fusion.7), channel_id=4, replica_groups=mesh['dp'=8,'tensor'=4] {'dp'}, dimensions={0}, use_global_device_ids=true | all-gather | bytes 368640 | tf_op jit(solution)/shard_map/all_gather | solution.py:88
  160.2 28.5 %all-gather.3 = bf16[1024,160]{0,1:T(8,128)(2,1)} all-gather(bf16[128,160]{0,1:T(8,128)(2,1)S(1)} %convolution_convert_fusion.6), channel_id=5, replica_groups=mesh['dp'=8,'tensor'=4] {'dp'}, dimensions={0}, use_global_device_ids=true | all-gather | bytes 368640 | tf_op jit(solution)/shard_map/all_gather | solution.py:87
  189.1 27.8 %all-gather = bf16[1024,160]{0,1:T(8,128)(2,1)} all-gather(bf16[128,160]{0,1:T(8,128)(2,1)S(1)} %convolution_convert_fusion.9), channel_id=2, replica_groups=mesh['dp'=8,'tensor'=4] {'dp'}, dimensions={0}, use_global_device_ids=true | all-gather | bytes 368640 | tf_op jit(solution)/shard_map/all_gather | solution.py:88
  217.3 27.9 %all-gather.1 = bf16[1024,160]{0,1:T(8,128)(2,1)} all-gather(bf16[128,160]{0,1:T(8,128)(2,1)S(1)} %convolution_convert_fusion.8), channel_id=3, replica_groups=mesh['dp'=8,'tensor'=4] {'dp'}, dimensions={0}, use_global_device_ids=true | all-gather | bytes 368640 | tf_op jit(solution)/shard_map/all_gather | solution.py:87
  270.7 55.4 %all-reduce.16.cloned.1.call-done = (f32[128,2560]{1,0:T(8,128)}, f32[128,2560]{1,0:T(8,128)}) async-done(((f32[128,2560]{1,0:T(8,128)}, f32[128,2560]{1,0:T(8,128)}), (f32[128,2560]{1,0:T(8,128)}, f32[128,2560]{1,0:T(8,128)})) %all-reduce.16.cloned.1.call-update) | async-done | bytes 2621456 | tf_op jit(solution)/shard_map/psum | solution.py:108
  331.5 131.6 %all-gather.16.cloned.1.call-done = bf16[2560,1792]{1,0:T(8,128)(2,1)} async-done(((bf16[320,1792]{1,0:T(8,128)(2,1)}), bf16[2560,1792]{1,0:T(8,128)(2,1)}) %all-gather.16.cloned.1.call-update) | async-done | bytes 9175056 | tf_op jit(solution)/shard_map/all_gather | solution.py:42
  469.2 129.0 %all-gather.18.cloned.1.call-done = bf16[2560,1792]{1,0:T(8,128)(2,1)} async-done(((bf16[320,1792]{1,0:T(8,128)(2,1)}), bf16[2560,1792]{1,0:T(8,128)(2,1)}) %all-gather.18.cloned.1.call-update) | async-done | bytes 9175056 | tf_op jit(solution)/shard_map/all_gather | solution.py:43
  611.8 121.5 %all-gather.20.cloned.1.call-done = bf16[1792,2560]{0,1:T(8,128)(2,1)} async-done(((bf16[1792,320]{0,1:T(8,128)(2,1)}), bf16[1792,2560]{0,1:T(8,128)(2,1)}) %all-gather.20.cloned.1.call-update) | async-done | bytes 9175056 | tf_op jit(solution)/shard_map/all_gather | solution.py:49
  782.5 42.8 %all-reduce.14.cloned.1.call-done = (f32[128,2560]{1,0:T(8,128)}, f32[128,2560]{1,0:T(8,128)}) async-done(((f32[128,2560]{1,0:T(8,128)}, f32[128,2560]{1,0:T(8,128)}), (f32[128,2560]{1,0:T(8,128)}, f32[128,2560]{1,0:T(8,128)})) %all-reduce.14.cloned.1.call-update) | async-done | bytes 2621456 | tf_op jit(solution)/shard_map/psum | solution.py:126
  829.2 38.4 %all-reduce.18.cloned.1.call-done = (bf16[128,2560]{1,0:T(8,128)(2,1)}, bf16[128,2560]{1,0:T(8,128)(2,1)}) async-done(((bf16[128,2560]{1,0:T(8,128)(2,1)}, bf16[128,2560]{1,0:T(8,128)(2,1)}), (bf16[128,2560]{1,0:T(8,128)(2,1)}, bf16[128,2560]{1,0:T(8,128)(2,1)})) %all-reduce.18.cloned.1.call-update) | async-done | bytes 1310736 | tf_op jit(solution)/shard_map/psum | solution.py:117
  913.9 33.5 %reduce-scatter.16.cloned.1.call-done = f32[1,128,160]{1,2,0:T(8,128)} async-done(((f32[1,1024,160]{1,2,0:T(8,128)}), f32[1,128,160]{1,2,0:T(8,128)}) %reduce-scatter.16.cloned.1.call-update) | async-done | bytes 81936 | tf_op jit(solution)/shard_map/reduce_scatter | solution.py:162
  948.3 64.4 %reduce-scatter.18.cloned.1.call-done = f32[1,128,160]{1,2,0:T(8,128)} async-done(((f32[1,1024,160]{1,2,0:T(8,128)}), f32[1,128,160]{1,2,0:T(8,128)}) %reduce-scatter.18.cloned.1.call-update) | async-done | bytes 81936 | tf_op jit(solution)/shard_map/reduce_scatter | solution.py:165
  1013.5 64.3 %reduce-scatter.12.cloned.1.call-done = f32[1,128,160]{1,2,0:T(8,128)} async-done(((f32[1,1024,160]{1,2,0:T(8,128)}), f32[1,128,160]{1,2,0:T(8,128)}) %reduce-scatter.12.cloned.1.call-update) | async-done | bytes 81936 | tf_op jit(solution)/shard_map/reduce_scatter | solution.py:162
  1083.1 60.1 %reduce-scatter.14.cloned.1.call-done = f32[1,128,160]{1,2,0:T(8,128)} async-done(((f32[1,1024,160]{1,2,0:T(8,128)}), f32[1,128,160]{1,2,0:T(8,128)}) %reduce-scatter.14.cloned.1.call-update) | async-done | bytes 81936 | tf_op jit(solution)/shard_map/reduce_scatter | solution.py:165
  1160.4 45.0 %all-reduce.12.cloned.1.call-done = (f32[128,2560]{1,0:T(8,128)}, f32[128,2560]{1,0:T(8,128)}) async-done(((f32[128,2560]{1,0:T(8,128)}, f32[128,2560]{1,0:T(8,128)}), (f32[128,2560]{1,0:T(8,128)}, f32[128,2560]{1,0:T(8,128)})) %all-reduce.12.cloned.1.call-update) | async-done | bytes 2621456 | tf_op jit(solution)/shard_map/psum | solution.py:171
  1210.1 18.4 pad_maximum_fusion.1
  1228.4 27.0 %copy.101 = f32[2560,2432]{1,0:T(8,128)} copy(f32[2560,2432]{0,1:T(8,128)} %pad_maximum_fusion.1) | data formatting | bytes 49807360
  1256.7 16.0 fusion.32
  1278.3 31.6 %pad_maximum_fusion = f32[2560,4544]{1,0:T(8,128)} fusion(f32[2560,3584]{1,0:T(8,128)} %fusion.32, f32[2560,960]{1,0:T(8,128)} %fusion.56), kind=kLoop, calls=%fused_computation | loop fusion | flops 11632640 | bytes 93061120 | tf_op jit(solution)/shard_map/concatenate | solution.py:206
  1322.1 355.3 %reduce-scatter.24.cloned.1.call-done = f32[320,2432]{1,0:T(8,128)} async-done(((f32[2560,2432]{1,0:T(8,128)}), f32[320,2432]{1,0:T(8,128)}) %reduce-scatter.24.cloned.1.call-update) | async-done | bytes 3112976
  1682.7 741.0 %reduce-scatter.20.cloned.1.call-done = f32[320,4544]{1,0:T(8,128)} async-done(((f32[2560,4544]{1,0:T(8,128)}), f32[320,4544]{1,0:T(8,128)}) %reduce-scatter.20.cloned.1.call-update) | async-done | bytes 5816336 | tf_op jit(solution)/shard_map/reduce_scatter | solution.py:205
  (325 shorter events, 227.2 us)
Async XLA Ops:
  7.2 239.0 %all-gather.12.cloned.1.call-start = ((), (), s32[]{:S(2)}) async-start(), calls=%async_computation.7 | async-start | bytes 3686400 | tf_op jit(solution)/shard_map/all_gather | solution.py:39
  7.9 253.9 %all-gather.14.cloned.1.call-start = ((), (), s32[]{:S(2)}) async-start(), calls=%async_computation.8 | async-start | bytes 3686400 | tf_op jit(solution)/shard_map/all_gather | solution.py:48
  8.7 317.4 %all-reduce.16.cloned.1.call-start = ((), (), s32[]{:S(2)}) async-start(), calls=%async_computation.21 | async-start | bytes 5242880 | tf_op jit(solution)/shard_map/psum | solution.py:108
  89.8 98.9 %copy-start.15 = (bf16[2560,160]{0,1:T(8,128)(2,1)}, bf16[2560,160]{0,1:T(8,128)(2,1)S(1)}, u32[]{:S(2)}) copy-start(bf16[2560,160]{0,1:T(8,128)(2,1)S(1)} %reshape.499) | copy-start | bytes 2457604
  127.1 89.8 %copy-start.17 = (bf16[2560,160]{0,1:T(8,128)(2,1)}, bf16[2560,160]{0,1:T(8,128)(2,1)S(1)}, u32[]{:S(2)}) copy-start(bf16[2560,160]{0,1:T(8,128)(2,1)S(1)} %reshape.501) | copy-start | bytes 2457604
  129.6 59.2 %copy-start.27 = (bf16[128,2560]{1,0:T(8,128)(2,1)}, bf16[128,2560]{1,0:T(8,128)(2,1)S(1)}, u32[]{:S(2)}) copy-start(bf16[128,2560]{1,0:T(8,128)(2,1)S(1)} %get-tuple-element.85) | copy-start | bytes 1966084
  129.6 87.3 %copy-start.25 = (bf16[128,2560]{1,0:T(8,128)(2,1)}, bf16[128,2560]{1,0:T(8,128)(2,1)S(1)}, u32[]{:S(2)}) copy-start(bf16[128,2560]{1,0:T(8,128)(2,1)S(1)} %get-tuple-element.84) | copy-start | bytes 1966084
  268.5 194.6 %all-gather.16.cloned.1.call-start = ((), (), s32[]{:S(2)}) async-start(), calls=%async_computation.9 | async-start | bytes 10321920 | tf_op jit(solution)/shard_map/all_gather | solution.py:42
  269.1 329.1 %all-gather.18.cloned.1.call-start = ((), (), s32[]{:S(2)}) async-start(), calls=%async_computation.10 | async-start | bytes 10321920 | tf_op jit(solution)/shard_map/all_gather | solution.py:43
  269.7 463.7 %all-gather.20.cloned.1.call-start = ((), (), s32[]{:S(2)}) async-start(), calls=%async_computation.11 | async-start | bytes 10321920 | tf_op jit(solution)/shard_map/all_gather | solution.py:49
  270.3 555.1 %all-reduce.14.cloned.1.call-start = ((), (), s32[]{:S(2)}) async-start(), calls=%async_computation.20 | async-start | bytes 5242880 | tf_op jit(solution)/shard_map/psum | solution.py:126
  766.9 100.7 %all-reduce.18.cloned.1.call-start = ((), (), s32[]{:S(2)}) async-start(), calls=%async_computation.22 | async-start | bytes 2621440 | tf_op jit(solution)/shard_map/psum | solution.py:117
  782.5 164.9 %reduce-scatter.16.cloned.1.call-start = ((), (), s32[]{:S(2)}) async-start(), calls=%async_computation.14 | async-start | bytes 737280 | tf_op jit(solution)/shard_map/reduce_scatter | solution.py:162
  884.3 128.3 %reduce-scatter.18.cloned.1.call-start = ((), (), s32[]{:S(2)}) async-start(), calls=%async_computation.15 | async-start | bytes 737280 | tf_op jit(solution)/shard_map/reduce_scatter | solution.py:165
  888.4 189.4 %reduce-scatter.12.cloned.1.call-start = ((), (), s32[]{:S(2)}) async-start(), calls=%async_computation.12 | async-start | bytes 737280 | tf_op jit(solution)/shard_map/reduce_scatter | solution.py:162
  901.3 241.8 %reduce-scatter.14.cloned.1.call-start = ((), (), s32[]{:S(2)}) async-start(), calls=%async_computation.13 | async-start | bytes 737280 | tf_op jit(solution)/shard_map/reduce_scatter | solution.py:165
  909.3 296.1 %all-reduce.12.cloned.1.call-start = ((), (), s32[]{:S(2)}) async-start(), calls=%async_computation.19 | async-start | bytes 5242880 | tf_op jit(solution)/shard_map/psum | solution.py:171
  948.3 132.4 %copy-start.16 = (bf16[2560,160]{0,1:T(8,128)(2,1)S(1)}, bf16[2560,160]{0,1:T(8,128)(2,1)}, u32[]{:S(2)}) copy-start(bf16[2560,160]{0,1:T(8,128)(2,1)} %copy-done.15) | copy-start | bytes 2457604
  1146.1 174.2 %reduce-scatter.22.cloned.1.call-start = ((), (), s32[]{:S(2)}) async-start(), calls=%async_computation.17 | async-start | bytes 1474560
  1156.6 48.8 %copy-start.10 = (bf16[2,128,2560]{2,1,0:T(8,128)(2,1)S(1)}, bf16[2,128,2560]{2,1,0:T(8,128)(2,1)}, u32[]{:S(2)}) copy-start(bf16[2,128,2560]{2,1,0:T(8,128)(2,1)} %param.12) | copy-start | bytes 3932164
  1156.6 48.8 %copy-start.70 = (f32[128]{0:T(128)S(1)}, f32[128]{0:T(128)}, u32[]{:S(2)}) copy-start(f32[128]{0:T(128)} %copy-done.69) | copy-start | bytes 1540
  1156.6 48.8 %copy-start.73 = (f32[128]{0:T(128)S(1)}, f32[128]{0:T(128)}, u32[]{:S(2)}) copy-start(f32[128]{0:T(128)} %copy-done.72) | copy-start | bytes 1540
  1210.0 467.4 %reduce-scatter.24.cloned.1.call-start = ((), (), s32[]{:S(2)}) async-start(), calls=%async_computation.18 | async-start | bytes 28016640
  1255.4 1168.3 %reduce-scatter.20.cloned.1.call-start = ((), (), s32[]{:S(2)}) async-start(), calls=%async_computation.16 | async-start | bytes 53084160 | tf_op jit(solution)/shard_map/reduce_scatter | solution.py:205
  (83 other events, 536.4 us)
Sparse Core Ops, SparseCore 0:
  10.2 86.1 all-gather.11
  98.6 67.7 all-gather.13
  268.6 57.4 all-reduce.15
  328.1 134.9 all-gather.15
  465.1 133.0 all-gather.17
  600.3 133.0 all-gather.19
  767.0 58.2 all-reduce.13
  828.3 39.2 all-reduce.17
  884.5 62.8 reduce-scatter.15
  950.9 61.6 reduce-scatter.17
  1015.9 61.8 reduce-scatter.11
  1081.3 61.7 reduce-scatter.13
  1146.2 59.1 all-reduce.11
  1210.1 64.3 reduce-scatter.21
  1278.3 399.0 reduce-scatter.23
  1681.1 742.4 reduce-scatter.19
where the time goes:
time: 2450 us; the launch traced here: 2440 us
  waiting for transfers between devices  1890 us (77%)
  blocking collectives  223 us (9%)
  matrix products  155 us (6%)
  other arithmetic  83.9 us (3%)
  local copies, waits for them, and re-layouts  77 us (3%)
    reduce_scatter x1, waiting for transfers between devices, reduce_grads(): lax.psum_scatter(jnp.concatenate([contract_first(left_attn, attn_in_grads...  741 us
    unnamed x18, waiting for transfers between devices  358 us
    all_gather x1, waiting for transfers between devices, fetch_weights(): lax.all_gather(w_gate, 'dp', axis=0, tiled=True)  132 us
    all_gather x1, waiting for transfers between devices, fetch_weights(): lax.all_gather(w_up, 'dp', axis=0, tiled=True)  129 us
    reduce_scatter x2, waiting for transfers between devices, run_batch(): lax.psum_scatter(value_parts.reshape(seqs, length, -1), 'dp', scatter_dim...  124 us
    all_gather x1, waiting for transfers between devices, fetch_weights(): lax.all_gather(w_down, 'dp', axis=1, tiled=True)  122 us
    reduce_scatter x2, waiting for transfers between devices, run_batch(): lax.psum_scatter(key_parts.reshape(seqs, length, -1), 'dp', scatter_dimen...  97.8 us
    all_gather x2, blocking collectives, run_batch(): lax.all_gather(values_own.reshape(seqs, rows, -1), 'dp', axis=1, tiled=True)  57.7 us
  transfers between devices with their start and end apart: 16, of which 13 were waited for; matrix products, arithmetic and copies ran while one was open for 9% of the time, Pallas kernels for 0%

commit v1 on v0

v1 whole, which is shorter than its diff:
```python
import jax
import jax.numpy as jnp
from jax import lax
from jax.sharding import PartitionSpec as P

HEAD_DIM = 80
EPSILON = 1e-05
NEGATIVE = -1e30
BF16 = jnp.bfloat16
F32 = jnp.float32
AXES = ("dp", "tensor")


def dot(left, right):
    return jnp.dot(left, right, preferred_element_type=F32)


def contract_last(left, right):
    return lax.dot_general(left, right, (((1,), (1,)), ((), ())), preferred_element_type=F32)


def contract_first(left, right):
    return lax.dot_general(left, right, (((0,), (0,)), ((), ())), preferred_element_type=F32)


def pick(stack, index):
    return lax.dynamic_index_in_dim(stack, index, 0, keepdims=False)


def place(parts, indices):
    total = jnp.zeros((len(parts),) + parts[0].shape, parts[0].dtype)
    for part, index in zip(parts, indices):
        total = lax.dynamic_update_index_in_dim(total, part, index, 0)
    return total


class Grid:
    def __init__(self, dp, tensor, seqs, kv_local):
        self.Y = seqs
        self.C = tensor // seqs
        self.U = kv_local
        self.Z = seqs * kv_local
        self.X = dp // self.Z
        assert self.C * self.Y == tensor and self.X * self.Z == dp
        i, j = lax.axis_index("dp"), lax.axis_index("tensor")
        self.z, self.x = i // self.X, i % self.X
        self.y, self.c = j // self.C, j % self.C
        order = list(range(0, self.Z, 2)) + list(range(1, self.Z, 2))[::-1]
        self.order = order
        self.ring = [order.index(z) for z in range(self.Z)]

    def move(self, value, target):
        pairs = []
        for z in range(self.Z):
            for x in range(self.X):
                for y in range(self.Y):
                    for c in range(self.C):
                        tz, tx, ty, tc = target(z, x, y, c)
                        here = ((z * self.X + x) * self.Y + y) * self.C + c
                        there = ((tz * self.X + tx) * self.Y + ty) * self.C + tc
                        pairs.append((here, there))
        return lax.ppermute(value, AXES, pairs)

    def to_z(self, value, k):
        return self.move(value, lambda z, x, y, c: ((z + k) % self.Z, x, y, c))

    def to_x(self, value, k):
        return self.move(value, lambda z, x, y, c: (z, (x + k) % self.X, y, c))

    def to_y(self, value, k):
        return self.move(value, lambda z, x, y, c: (z, x, (y + k) % self.Y, c))

    def to_c(self, value, k):
        return self.move(value, lambda z, x, y, c: (z, x, y, (c + k) % self.C))

    def along_ring(self, value, k):
        return self.move(
            value, lambda z, x, y, c: (self.order[(self.ring[z] + k) % self.Z], x, y, c)
        )

    def slot_z(self, s):
        place_of = jnp.array(self.ring, jnp.int32)[self.z]
        return jnp.array(self.order, jnp.int32)[(place_of - s) % self.Z]

    def gather_tokens(self, own):
        blocks = [own]
        for _ in range(self.Z - 1):
            blocks.append(self.along_ring(blocks[-1], 1))
        mine = jnp.concatenate(blocks, 0)
        return jnp.concatenate([mine] + [self.to_c(mine, k) for k in range(1, self.C)], 0)

    def scatter_tokens(self, partial):
        tokens = partial.shape[0] // self.C
        low = partial[tokens:].astype(BF16)
        mine = partial[:tokens]
        for h in range(1, self.C):
            part = low[(h - 1) * tokens : h * tokens]
            mine = mine + self.to_c(part, -h).astype(F32)
        own = tokens // self.Z
        total = mine[(self.Z - 1) * own :].astype(BF16)
        for s in range(self.Z - 2, -1, -1):
            total = self.along_ring(total, -1).astype(F32) + mine[s * own : (s + 1) * own]
            if s > 0:
                total = total.astype(BF16)
        return total

    def exchange_z(self, pick_for):
        parts = [pick_for(self.z)]
        for k in range(1, self.Z):
            parts.append(self.to_z(pick_for((self.z + k) % self.Z), k))
        return parts

    def from_z(self, k):
        return (self.z - k) % self.Z

    def spread_x(self, unit):
        parts = [unit] + [self.to_x(unit, k) for k in range(1, self.X)]
        return place(parts, [(self.x - k) % self.X for k in range(self.X)])

    def fetch_hidden(self, weight, x_first):
        rows, cols = weight.shape
        n = cols // self.Z
        pack = jnp.stack([weight[:, s * n : (s + 1) * n] for s in range(self.Z)], 0)
        parts = self.exchange_z(lambda zd: pick(pack, zd))
        unit = place(parts, [self.from_z(k) for k in range(self.Z)])

        def spread(value):
            return self.spread_x(value).transpose(1, 0, 2, 3).reshape(-1, n)

        if x_first:
            whole = spread(unit)
            return [whole] + [self.to_y(whole, k) for k in range(1, self.Y)]
        return [spread(unit)] + [spread(self.to_y(unit, k)) for k in range(1, self.Y)]

    def fetch_heads(self, packs, x_first):
        rows, n = packs[0].shape
        half = rows // self.Y
        pack = jnp.stack(packs, 0).reshape(self.U, self.Y, half, n).transpose(1, 0, 2, 3)
        near = [pick(pack, self.y)]
        for k in range(1, self.Y):
            near.append(self.to_y(pick(pack, (self.y + k) % self.Y), k))
        near = jnp.concatenate(near, 0)

        def for_z(zd):
            return pick(near, ((self.y - zd // self.U) % self.Y) * self.U + zd % self.U)

        parts = self.exchange_z(for_z)
        unit = place(parts, [self.from_z(k) for k in range(self.Z)])
        if x_first:
            unit = self.spread_x(unit)
            ys = [unit] + [self.to_y(unit, k) for k in range(1, self.Y)]
            both = place(ys, [(self.y - k) % self.Y for k in range(self.Y)])
            return both.transpose(2, 1, 0, 3, 4).reshape(-1, n)
        ys = [unit] + [self.to_y(unit, k) for k in range(1, self.Y)]
        unit = place(ys, [(self.y - k) % self.Y for k in range(self.Y)])
        both = self.spread_x(unit)
        return both.transpose(2, 0, 1, 3, 4).reshape(-1, n)

    def sum_x(self, total):
        out = pick(total, self.x).astype(F32)
        for k in range(1, self.X):
            out = out + self.to_x(pick(total, (self.x + k) % self.X), k).astype(F32)
        return out

    def return_hidden(self, grads, x_first):
        n = grads[0].shape[1]
        shaped = [
            g.reshape(self.Z, self.X, -1, n).transpose(1, 0, 2, 3) for g in grads
        ]
        if x_first:
            units = [self.sum_x(g) for g in shaped]
            total = units[0]
            for k in range(1, self.Y):
                total = total + self.to_y(units[k].astype(BF16), -k).astype(F32)
        else:
            total = shaped[0].astype(F32)
            for k in range(1, self.Y):
                total = total + self.to_y(shaped[k], -k).astype(F32)
            total = self.sum_x(total.astype(BF16))
        total = total.astype(BF16)
        parts = jnp.stack(self.exchange_z(lambda zd: pick(total, zd)), 0)
        return jnp.concatenate(
            [pick(parts, (self.z - s) % self.Z) for s in range(self.Z)], 1
        ).astype(F32)

    def return_heads(self, grad, x_first):
        n = grad.shape[1]
        shaped = grad.reshape(self.Z, self.X, self.Y, -1, n).transpose(2, 1, 0, 3, 4)
        total = pick(shaped, self.y).astype(F32)
        for k in range(1, self.Y):
            total = total + self.to_y(pick(shaped, (self.y + k) % self.Y), k).astype(F32)
        total = self.sum_x(total.astype(BF16)).astype(BF16)
        parts = jnp.stack(self.exchange_z(lambda zd: pick(total, zd)), 0)
        parts = jnp.stack([pick(parts, (self.z - s) % self.Z) for s in range(self.Z)], 0)
        parts = parts.reshape((self.Y, self.U) + parts.shape[1:])
        halves = [pick(parts, self.y)]
        for k in range(1, self.Y):
            halves.append(self.to_y(pick(parts, (self.y + k) % self.Y), k))
        rows = place(halves, [(self.y - k) % self.Y for k in range(self.Y)])
        return [rows[:, u].reshape(-1, n).astype(F32) for u in range(self.U)]

    def gather_gains(self, gains):
        xs = self.spread_x(gains)
        parts = [xs] + [self.to_z(xs, k) for k in range(1, self.Z)]
        whole = place(parts, [self.from_z(k) for k in range(self.Z)])
        return whole.transpose(2, 0, 1, 3).reshape(gains.shape[0], -1)

    def sum_gains(self, terms):
        number = terms.shape[0]
        part = terms
        for k in range(1, self.C):
            part = part + self.to_c(terms, k)
        terms = part
        for k in range(1, self.Y):
            part = part + self.to_y(terms, k)
        part = part.reshape(number, self.Z, self.X, -1).transpose(2, 1, 0, 3)
        out = pick(part, self.x)
        for k in range(1, self.X):
            out = out + self.to_x(pick(part, (self.x + k) % self.X), k)
        return sum(self.exchange_z(lambda zd: pick(out, zd)))

    def spread_rows(self, own):
        cs = [own] + [self.to_c(own, k) for k in range(1, self.C)]
        rows = place(cs, [(self.c - k) % self.C for k in range(self.C)])
        rows = rows.reshape(-1, own.shape[1])
        ys = [rows] + [self.to_y(rows, k) for k in range(1, self.Y)]
        return place(ys, [(self.y - k) % self.Y for k in range(self.Y)])


def per_device(
    dp,
    tensor,
    inputs,
    cotangent,
    prefix,
    gain_attn,
    w_query,
    w_key,
    w_value,
    w_out,
    gain_mlp,
    w_gate,
    w_up,
    w_down,
):
    seqs, rows, width = inputs.shape
    kv_local = w_key.shape[1] // HEAD_DIM
    group = w_query.shape[1] // w_key.shape[1]
    grid = Grid(dp, tensor, seqs, kv_local)
    own = rows // grid.C
    scale = HEAD_DIM ** (-0.5)
    q_cols = group * HEAD_DIM

    gains = grid.gather_gains(jnp.stack([gain_attn, gain_mlp], 0)).astype(F32)
    gain_one, gain_two = gains[0:1], gains[1:2]

    def heads_of(weight, u):
        size = weight.shape[1] // kv_local
        return weight[:, u * size : (u + 1) * size]

    w_qkv = grid.fetch_heads(
        [
            jnp.concatenate([heads_of(w_query, u), heads_of(w_key, u), heads_of(w_value, u)], 1)
            for u in range(kv_local)
        ],
        True,
    )
    w_out_t = w_out.T
    w_o = grid.fetch_heads([heads_of(w_out_t, u) for u in range(kv_local)], False)

    def own_rows(value):
        return lax.dynamic_slice(value, (grid.y, grid.c * own, 0), (1, own, width))[0]

    flat = own_rows(inputs).astype(F32)
    cot_own = own_rows(cotangent)
    recip_one = lax.rsqrt(jnp.mean(flat * flat, -1, keepdims=True) + EPSILON)
    normal_one = flat * recip_one
    attn_in = grid.gather_tokens((normal_one * gain_one).astype(BF16))

    w_g = grid.fetch_hidden(w_gate, True)
    w_u = grid.fetch_hidden(w_up, False)
    w_d = grid.fetch_hidden(w_down.T, True)
    mlp_grad = grid.gather_tokens(cot_own)

    qkv = dot(attn_in, w_qkv).astype(BF16)
    tokens = qkv.shape[0]
    queries = qkv[:, :q_cols].reshape(tokens, group, HEAD_DIM)
    kv_own = qkv[:, q_cols:]
    kv_all = jnp.concatenate([kv_own] + [grid.to_x(kv_own, k) for k in range(1, grid.X)], 0)
    keys, values = kv_all[:, :HEAD_DIM], kv_all[:, HEAD_DIM:]

    inner = lax.iota(jnp.int32, own)
    base = [
        grid.slot_z(s) * (grid.X * rows) + ((grid.c - h) % grid.C) * own
        for h in range(grid.C)
        for s in range(grid.Z)
    ]
    base = jnp.concatenate([b + inner for b in base])
    key_pos = jnp.concatenate([base + ((grid.x - k) % grid.X) * rows for k in range(grid.X)])
    query_pos = base + grid.x * rows
    seq_prefix = prefix[grid.y]
    allowed = (key_pos[None, :] <= query_pos[:, None]) | (key_pos[None, :] < seq_prefix)

    scores = jnp.einsum("qgd,td->gqt", queries, keys, preferred_element_type=F32) * scale
    scores = jnp.where(allowed[None], scores, NEGATIVE)
    top = jnp.max(scores, -1, keepdims=True)
    expo = jnp.exp(scores - top)
    probs = expo / jnp.sum(expo, -1, keepdims=True)
    probs_low = probs.astype(BF16)
    heads = (
        jnp.einsum("gqt,td->qgd", probs_low, values, preferred_element_type=F32)
        .astype(BF16)
        .reshape(tokens, -1)
    )
    attn_out = grid.scatter_tokens(contract_last(heads, w_o))
    hidden = flat + attn_out
    recip_two = lax.rsqrt(jnp.mean(hidden * hidden, -1, keepdims=True) + EPSILON)
    normal_two = hidden * recip_two
    mlp_in = grid.gather_tokens((normal_two * gain_two).astype(BF16))

    mlp_partial = 0.0
    in_partial = 0.0
    gate_grads, up_grads, products = [], [], []
    for wg, wu, wd in zip(w_g, w_u, w_d):
        gate = dot(mlp_in, wg)
        up = dot(mlp_in, wu)
        sigma = jax.nn.sigmoid(gate)
        product = (gate * sigma * up).astype(BF16)
        mlp_partial = mlp_partial + contract_last(product, wd)
        product_grad = dot(mlp_grad, wd)
        up_grad = (product_grad * gate * sigma).astype(BF16)
        gate_grad = (product_grad * up * sigma * (1.0 + gate * (1.0 - sigma))).astype(BF16)
        in_partial = in_partial + contract_last(gate_grad, wg) + contract_last(up_grad, wu)
        products.append(product)
        gate_grads.append(gate_grad)
        up_grads.append(up_grad)

    mlp_in_grad = grid.scatter_tokens(in_partial)
    result = grid.spread_rows(hidden + grid.scatter_tokens(mlp_partial))

    down_wgrad = grid.return_hidden(
        [contract_first(mlp_grad, p).astype(BF16) for p in products], True
    ).T
    gate_wgrad = grid.return_hidden(
        [contract_first(mlp_in, g).astype(BF16) for g in gate_grads], False
    )
    up_wgrad = grid.return_hidden(
        [contract_first(mlp_in, g).astype(BF16) for g in up_grads], True
    )

    out_grad = cot_own.astype(F32)
    scaled_two = mlp_in_grad * gain_two
    hidden_grad = out_grad + recip_two * (
        scaled_two - normal_two * jnp.mean(scaled_two * normal_two, -1, keepdims=True)
    )
    gain_two_term = jnp.sum(mlp_in_grad * normal_two, 0, keepdims=True)
    attn_grad = grid.gather_tokens(hidden_grad.astype(BF16))
    heads_grad = dot(attn_grad, w_o).astype(BF16)
    out_wgrad = grid.return_heads(contract_first(attn_grad, heads).astype(BF16), False)

    heads_grad = heads_grad.reshape(tokens, group, HEAD_DIM)
    prob_grad = jnp.einsum("qgd,td->gqt", heads_grad, values, preferred_element_type=F32)
    score_grad = (probs * (prob_grad - jnp.sum(probs * prob_grad, -1, keepdims=True))).astype(BF16)
    query_grad = jnp.einsum("gqt,td->qgd", score_grad, keys, preferred_element_type=F32) * scale
    key_parts = jnp.einsum("gqt,qgd->td", score_grad, queries, preferred_element_type=F32) * scale
    value_parts = jnp.einsum("gqt,qgd->td", probs_low, heads_grad, preferred_element_type=F32)
    kv_parts = jnp.concatenate([key_parts, value_parts], 1)
    kv_grad = kv_parts[:tokens]
    for k in range(1, grid.X):
        kv_grad = kv_grad + grid.to_x(kv_parts[k * tokens : (k + 1) * tokens], -k)
    qkv_grad = jnp.concatenate(
        [query_grad.astype(BF16).reshape(tokens, -1), kv_grad.astype(BF16)], 1
    )
    attn_in_grad = grid.scatter_tokens(contract_last(qkv_grad, w_qkv))
    qkv_wgrad = grid.return_heads(contract_first(attn_in, qkv_grad).astype(BF16), True)

    scaled_one = attn_in_grad * gain_one
    input_grad = hidden_grad + recip_one * (
        scaled_one - normal_one * jnp.mean(scaled_one * normal_one, -1, keepdims=True)
    )
    input_grad = grid.spread_rows(input_grad)
    gain_one_term = jnp.sum(attn_in_grad * normal_one, 0, keepdims=True)
    gain_sum = grid.sum_gains(jnp.concatenate([gain_one_term, gain_two_term], 0))

    return (
        result,
        input_grad,
        gain_sum[0],
        jnp.concatenate([w[:, :q_cols] for w in qkv_wgrad], 1),
        jnp.concatenate([w[:, q_cols : q_cols + HEAD_DIM] for w in qkv_wgrad], 1),
        jnp.concatenate([w[:, q_cols + HEAD_DIM :] for w in qkv_wgrad], 1),
        jnp.concatenate(out_wgrad, 1).T,
        gain_sum[1],
        gate_wgrad,
        up_wgrad,
        down_wgrad,
    )


def solution(mesh):
    dp, tensor = mesh.shape["dp"], mesh.shape["tensor"]

    def step(*args):
        return per_device(dp, tensor, *args)

    return jax.shard_map(
        step,
        mesh=mesh,
        in_specs=(
            P(None, "dp", None),
            P(None, "dp", None),
            P(),
            P("dp"),
            P("dp", "tensor"),
            P("dp", "tensor"),
            P("dp", "tensor"),
            P("tensor", "dp"),
            P("dp"),
            P("dp", "tensor"),
            P("dp", "tensor"),
            P("tensor", "dp"),
        ),
        out_specs=(
            P(None, "dp", None),
            P(None, "dp", None),
            P("dp"),
            P("dp", "tensor"),
            P("dp", "tensor"),
            P("dp", "tensor"),
            P("tensor", "dp"),
            P("dp"),
            P("dp", "tensor"),
            P("dp", "tensor"),
            P("tensor", "dp"),
        ),
        check_vma=False,
    )
```

time: 2450 us -> 937 us (0.38)
  waiting for transfers between devices: 1890 us -> 461 us
  blocking collectives: 223 us -> 0 us
  starting transfers between devices: 1.52 us -> 147 us
  local copies, waits for them, and re-layouts: 77 us -> 153 us
  matrix products: 155 us -> 103 us
  other arithmetic: 83.9 us -> 53.6 us
    reduce_scatter x5 -> x0, waiting for transfers between devices: 963 us -> none  [the longest x1 741 us: reduce_grads(): lax.psum_scatter(jnp.concatenate([contract_first(left_attn, attn_in_grads...]
    ppermute x0 -> x105, waiting for transfers between devices: none -> 461 us  [move(): return lax.ppermute(value, AXES, pairs)]
    all_gather x5 -> x0, waiting for transfers between devices: 382 us -> none  [the longest x1 132 us: fetch_weights(): lax.all_gather(w_gate, 'dp', axis=0, tiled=True)]
    unnamed x18 -> x0, waiting for transfers between devices: 358 us -> none
    all_gather x6 -> x0, blocking collectives: 184 us -> none  [the longest x2 57.7 us: run_batch(): lax.all_gather(values_own.reshape(seqs, rows, -1), 'dp', axis=1, tiled=True)]
    psum x4 -> x0, waiting for transfers between devices: 182 us -> none  [the longest x1 55.4 us: run_batch(): lax.psum(jnp.dot(heads, w_out, preferred_element_type=jnp.float32), 'tens...]
    ppermute x0 -> x105, starting transfers between devices: none -> 147 us  [move(): return lax.ppermute(value, AXES, pairs)]
    concatenate x4 -> x12, other arithmetic: 53.4 us -> 10.4 us  [the longest x4 5.86 us: gather_tokens(): mine = jnp.concatenate(blocks, 0)]
  transfers between devices with their start and end apart: 16 -> 105, of which waited for: 13 -> 48; matrix products, arithmetic and copies ran while one was open for 9% -> 30% of each run, Pallas kernels for 0% -> 0%
where the time goes in v1:
time: 937 us; the launch traced here: 928 us
  waiting for transfers between devices  461 us (49%)
  local copies, waits for them, and re-layouts  153 us (16%)
  starting transfers between devices  147 us (16%)
  matrix products  103 us (11%)
  other arithmetic  53.6 us (6%)
  between operations  9.65 us (1%)
    ppermute x105, waiting for transfers between devices, move(): return lax.ppermute(value, AXES, pairs)  461 us
    ppermute x105, starting transfers between devices, move(): return lax.ppermute(value, AXES, pairs)  147 us
    dynamic_update_slice x46, local copies, waits for them, and re-layouts, place(): total = lax.dynamic_update_index_in_dim(total, part, index, 0)  37.1 us
    dot_general x8, matrix products, contract_last(): lax.dot_general(left, right, (((1,), (1,)), ((), ())), preferred_element_...  30.8 us
    dot_general x8, matrix products, contract_first(): lax.dot_general(left, right, (((0,), (0,)), ((), ())), preferred_element_...  27.1 us
    dot_general x8, matrix products, dot(): return jnp.dot(left, right, preferred_element_type=F32)  21.3 us
  transfers between devices with their start and end apart: 105, of which 48 were waited for; matrix products, arithmetic and copies ran while one was open for 30% of the time, Pallas kernels for 0%

profile of v1, /device:TPU:0, one launch (start us, length us, event | category | flops | bytes accessed | tf_op | source)
XLA Modules:
  0.0 927.6 jit_solution(4779032271966010129)
XLA Ops:
  77.9 14.1 %collective-permute-done.34 = bf16[320,448]{1,0:T(8,128)(2,1)S(1)} collective-permute-done((bf16[320,448]{1,0:T(8,128)(2,1)S(1)}, bf16[320,448]{1,0:T(8,128)(2,1)S(1)}, u32[]{:S(2)}, u32[]{:S(2)}) %collective-permute-start.34) | collective-permute-done | bytes 286752 | tf_op jit(solution)/shard_map/ppermute | solution.py:62
  102.6 11.5 %collective-permute-start.4 = (bf16[64,2560]{1,0:T(8,128)(2,1)S(1)}, bf16[64,2560]{1,0:T(8,128)(2,1)S(1)}, u32[]{:S(2)}, u32[]{:S(2)}) collective-permute-start(bf16[64,2560]{1,0:T(8,128)(2,1)S(1)} %get-tuple-element.66), channel_id=1, source_target_pairs={{0,16},{1,17},{2,18},{3,19},{4,20},{5,21},{6,22},{7,23},{8,0},{9,1... | collective-permute-start | bytes 983048 | tf_op jit(solution)/shard_map/ppermute | solution.py:62
  144.4 7.5 collective-permute-done.9
  152.1 8.2 collective-permute-done.10
  165.7 7.4 collective-permute-done.5
  180.9 13.1 %collective-permute-done.12 = bf16[4,160,480]{2,1,0:T(8,128)(2,1)S(1)} collective-permute-done((bf16[4,160,480]{2,1,0:T(8,128)(2,1)S(1)}, bf16[4,160,480]{2,1,0:T(8,128)(2,1)S(1)}, u32[]{:S(2)}, u32[]{:S(2)}) %collective-permute-start.12) | collective-permute-done | bytes 614432 | tf_op jit(solution)/shard_map/ppermute | solution.py:62
  195.5 27.3 %collective-permute-done.13 = bf16[2,4,160,480]{3,2,0,1:T(8,128)(2,1)S(1)} collective-permute-done((bf16[2,4,160,480]{3,2,0,1:T(8,128)(2,1)S(1)}, bf16[2,4,160,480]{3,2,0,1:T(8,128)(2,1)S(1)}, u32[]{:S(2)}, u32[]{:S(2)}) %collective-permute-start.13) | collective-permute-done | bytes 1228832 | tf_op jit(solution)/shard_map/ppermute | solution.py:62
  230.5 7.5 fusion.116
  261.6 8.1 collective-permute-done.52
  340.8 7.5 collective-permute-done.43
  371.2 41.5 %collective-permute-done.41 = bf16[2560,448]{0,1:T(8,128)(2,1)S(1)} collective-permute-done((bf16[2560,448]{0,1:T(8,128)(2,1)}, bf16[2560,448]{0,1:T(8,128)(2,1)S(1)}, u32[]{:S(2)}, u32[]{:S(2)}) %collective-permute-start.41) | collective-permute-done | bytes 2293792 | tf_op jit(solution)/shard_map/ppermute | solution.py:62
  506.9 13.3 %collective-permute-done.100 = bf16[4,320,448]{2,1,0:T(8,128)(2,1)} collective-permute-done((bf16[4,320,448]{2,1,0:T(8,128)(2,1)}, bf16[4,320,448]{2,1,0:T(8,128)(2,1)}, u32[]{:S(2)}, u32[]{:S(2)}) %collective-permute-start.100) | collective-permute-done | bytes 1146912 | tf_op jit(solution)/shard_map/ppermute | solution.py:62
  544.6 8.8 collective-permute-done.57
  569.5 38.6 %collective-permute-done.95 = bf16[4,320,448]{2,1,0:T(8,128)(2,1)S(1)} collective-permute-done((bf16[4,320,448]{2,1,0:T(8,128)(2,1)S(1)}, bf16[4,320,448]{2,1,0:T(8,128)(2,1)S(1)}, u32[]{:S(2)}, u32[]{:S(2)}) %collective-permute-start.95) | collective-permute-done | bytes 1146912 | tf_op jit(solution)/shard_map/ppermute | solution.py:62
  614.5 18.7 %collective-permute-done.101 = bf16[4,320,448]{2,1,0:T(8,128)(2,1)S(1)} collective-permute-done((bf16[4,320,448]{2,1,0:T(8,128)(2,1)S(1)}, bf16[4,320,448]{2,1,0:T(8,128)(2,1)S(1)}, u32[]{:S(2)}, u32[]{:S(2)}) %collective-permute-start.101) | collective-permute-done | bytes 1146912 | tf_op jit(solution)/shard_map/ppermute | solution.py:62
  652.9 16.8 %collective-permute-done.103 = bf16[320,448]{1,0:T(8,128)(2,1)S(1)} collective-permute-done((bf16[320,448]{1,0:T(8,128)(2,1)S(1)}, bf16[320,448]{1,0:T(8,128)(2,1)S(1)}, u32[]{:S(2)}, u32[]{:S(2)}) %collective-permute-start.103) | collective-permute-done | bytes 286752 | tf_op jit(solution)/shard_map/ppermute | solution.py:62
  724.4 13.6 %collective-permute-done.91 = bf16[320,448]{1,0:T(8,128)(2,1)S(1)} collective-permute-done((bf16[320,448]{1,0:T(8,128)(2,1)S(1)}, bf16[320,448]{1,0:T(8,128)(2,1)S(1)}, u32[]{:S(2)}, u32[]{:S(2)}) %collective-permute-start.91) | collective-permute-done | bytes 286752 | tf_op jit(solution)/shard_map/ppermute | solution.py:62
  769.4 8.4 collective-permute-done.63
  782.5 8.1 collective-permute-done.83
  790.8 7.7 collective-permute-start.84
  822.2 25.3 %collective-permute-done.76 = bf16[2,4,160,480]{3,2,0,1:T(8,128)(2,1)S(1)} collective-permute-done((bf16[2,4,160,480]{3,2,0,1:T(8,128)(2,1)S(1)}, bf16[2,4,160,480]{3,2,0,1:T(8,128)(2,1)S(1)}, u32[]{:S(2)}, u32[]{:S(2)}) %collective-permute-start.76) | collective-permute-done | bytes 1228832 | tf_op jit(solution)/shard_map/ppermute | solution.py:62
  849.2 15.2 %collective-permute-done.77 = bf16[4,160,480]{2,1,0:T(8,128)(2,1)S(1)} collective-permute-done((bf16[4,160,480]{2,1,0:T(8,128)(2,1)S(1)}, bf16[4,160,480]{2,1,0:T(8,128)(2,1)S(1)}, u32[]{:S(2)}, u32[]{:S(2)}) %collective-permute-start.77) | collective-permute-done | bytes 614432 | tf_op jit(solution)/shard_map/ppermute | solution.py:62
  880.5 8.0 collective-permute-done.67
  909.2 16.6 %collective-permute-done.69 = f32[128,2560]{1,0:T(8,128)S(1)} collective-permute-done((f32[128,2560]{1,0:T(8,128)S(1)}, f32[128,2560]{1,0:T(8,128)S(1)}, u32[]{:S(2)}, u32[]{:S(2)}) %collective-permute-start.69) | collective-permute-done | bytes 1310752 | tf_op jit(solution)/shard_map/ppermute | solution.py:62
  (609 shorter events, 565.2 us)
Async XLA Ops:
  4.9 59.3 %collective-permute-start.37 = (bf16[320,448]{1,0:T(8,128)(2,1)}, bf16[320,448]{1,0:T(8,128)(2,1)}, u32[]{:S(2)}, u32[]{:S(2)}) collective-permute-start(bf16[320,448]{1,0:T(8,128)(2,1)} %get-tuple-element.101), channel_id=1, source_target_pairs={{0,8},{1,9},{2,10},{3,11},{4,12},{5,13},{6,14},{7,15},{8,16},{9,17... | collective-permute-start | bytes 860168 | tf_op jit(solution)/shard_map/ppermute | solution.py:62
  7.9 61.2 %collective-permute-start.38 = (bf16[320,448]{1,0:T(8,128)(2,1)}, bf16[320,448]{1,0:T(8,128)(2,1)}, u32[]{:S(2)}, u32[]{:S(2)}) collective-permute-start(bf16[320,448]{1,0:T(8,128)(2,1)} %get-tuple-element.100), channel_id=1, source_target_pairs={{0,16},{1,17},{2,18},{3,19},{4,20},{5,21},{6,22},{7,23},{8,24},{9,... | collective-permute-start | bytes 860168 | tf_op jit(solution)/shard_map/ppermute | solution.py:62
  10.5 61.9 %collective-permute-start.39 = (bf16[320,448]{1,0:T(8,128)(2,1)}, bf16[320,448]{1,0:T(8,128)(2,1)}, u32[]{:S(2)}, u32[]{:S(2)}) collective-permute-start(bf16[320,448]{1,0:T(8,128)(2,1)} %get-tuple-element.99), channel_id=1, source_target_pairs={{0,24},{1,25},{2,26},{3,27},{4,28},{5,29},{6,30},{7,31},{8,0},{9,1... | collective-permute-start | bytes 860168 | tf_op jit(solution)/shard_map/ppermute | solution.py:62
  14.7 60.0 %collective-permute-start.33 = (bf16[320,448]{1,0:T(8,128)(2,1)}, bf16[320,448]{1,0:T(8,128)(2,1)}, u32[]{:S(2)}, u32[]{:S(2)}) collective-permute-start(bf16[320,448]{1,0:T(8,128)(2,1)} %get-tuple-element.109), channel_id=1, source_target_pairs={{0,8},{1,9},{2,10},{3,11},{4,12},{5,13},{6,14},{7,15},{8,16},{9,17... | collective-permute-start | bytes 860168 | tf_op jit(solution)/shard_map/ppermute | solution.py:62
  69.1 73.1 %collective-permute-start.8 = (bf16[2,160,480]{2,1,0:T(8,128)(2,1)}, bf16[2,160,480]{2,1,0:T(8,128)(2,1)S(1)}, u32[]{:S(2)}, u32[]{:S(2)}) collective-permute-start(bf16[2,160,480]{2,1,0:T(8,128)(2,1)} %get-tuple-element.141), channel_id=1, source_target_pairs={{0,2},{1,3},{2,0},{3,1},{4,6},{5,7},{6,4},{7,5},{8,10},{9,11},{10,... | collective-permute-start | bytes 921608 | tf_op jit(solution)/shard_map/ppermute | solution.py:62
  74.7 45.3 %collective-permute-start.30 = (bf16[320,448]{1,0:T(8,128)(2,1)S(1)}, bf16[320,448]{1,0:T(8,128)(2,1)S(1)}, u32[]{:S(2)}, u32[]{:S(2)}) collective-permute-start(bf16[320,448]{1,0:T(8,128)(2,1)S(1)} %get-tuple-element.104), channel_id=1, source_target_pairs={{0,16},{1,17},{2,18},{3,19},{4,20},{5,21},{6,22},{7,23},{8,24},{9,... | collective-permute-start | bytes 860168 | tf_op jit(solution)/shard_map/ppermute | solution.py:62
  92.0 152.3 %collective-permute-start.31 = (bf16[320,448]{1,0:T(8,128)(2,1)}, bf16[320,448]{1,0:T(8,128)(2,1)S(1)}, u32[]{:S(2)}, u32[]{:S(2)}) collective-permute-start(bf16[320,448]{1,0:T(8,128)(2,1)} %get-tuple-element.103), channel_id=1, source_target_pairs={{0,24},{1,25},{2,26},{3,27},{4,28},{5,29},{6,30},{7,31},{8,0},{9,1... | collective-permute-start | bytes 860168 | tf_op jit(solution)/shard_map/ppermute | solution.py:62
  94.7 160.8 %collective-permute-start.51 = (bf16[64,2560]{1,0:T(8,128)(2,1)}, bf16[64,2560]{1,0:T(8,128)(2,1)}, u32[]{:S(2)}, u32[]{:S(2)}) collective-permute-start(bf16[64,2560]{1,0:T(8,128)(2,1)} %get-tuple-element.58), channel_id=1, source_target_pairs={{0,16},{1,17},{2,18},{3,19},{4,20},{5,21},{6,22},{7,23},{8,0},{9,1... | collective-permute-start | bytes 983048 | tf_op jit(solution)/shard_map/ppermute | solution.py:62
  140.2 166.6 %collective-permute-start.40 = (bf16[4,320,448]{2,1,0:T(8,128)(2,1)}, bf16[4,320,448]{2,1,0:T(8,128)(2,1)}, u32[]{:S(2)}, u32[]{:S(2)}) collective-permute-start(bf16[4,320,448]{2,1,0:T(8,128)(2,1)} %bitcast_dynamic-update-slice_fusion.26), channel_id=1, source_target_pairs={{0,4},{1,5},{2,6},{3,7},{4,0},{5,1},{6,2},{7,3},{8,12},{9,13},{10,... | collective-permute-start | bytes 3440648 | tf_op jit(solution)/shard_map/ppermute | solution.py:62
  222.8 88.0 %collective-permute-start.42 = (bf16[4,320,448]{2,1,0:T(8,128)(2,1)}, bf16[4,320,448]{2,1,0:T(8,128)(2,1)}, u32[]{:S(2)}, u32[]{:S(2)}) collective-permute-start(bf16[4,320,448]{2,1,0:T(8,128)(2,1)} %bitcast_dynamic-update-slice_fusion.29), channel_id=1, source_target_pairs={{0,2},{1,3},{2,0},{3,1},{4,6},{5,7},{6,4},{7,5},{8,10},{9,11},{10,... | collective-permute-start | bytes 3440648 | tf_op jit(solution)/shard_map/ppermute | solution.py:62
  245.0 72.1 %collective-permute-start.32 = (bf16[4,320,448]{2,1,0:T(8,128)(2,1)}, bf16[4,320,448]{2,1,0:T(8,128)(2,1)}, u32[]{:S(2)}, u32[]{:S(2)}) collective-permute-start(bf16[4,320,448]{2,1,0:T(8,128)(2,1)} %bitcast_dynamic-update-slice_fusion.32), channel_id=1, source_target_pairs={{0,4},{1,5},{2,6},{3,7},{4,0},{5,1},{6,2},{7,3},{8,12},{9,13},{10,... | collective-permute-start | bytes 3440648 | tf_op jit(solution)/shard_map/ppermute | solution.py:62
  255.5 71.8 %collective-permute-start.36 = (bf16[4,320,448]{2,1,0:T(8,128)(2,1)}, bf16[4,320,448]{2,1,0:T(8,128)(2,1)}, u32[]{:S(2)}, u32[]{:S(2)}) collective-permute-start(bf16[4,320,448]{2,1,0:T(8,128)(2,1)} %bitcast_dynamic-update-slice_fusion.29), channel_id=1, source_target_pairs={{0,4},{1,5},{2,6},{3,7},{4,0},{5,1},{6,2},{7,3},{8,12},{9,13},{10,... | collective-permute-start | bytes 3440648 | tf_op jit(solution)/shard_map/ppermute | solution.py:62
  310.8 106.5 %collective-permute-start.44 = (bf16[2560,448]{0,1:T(8,128)(2,1)}, bf16[2560,448]{0,1:T(8,128)(2,1)}, u32[]{:S(2)}, u32[]{:S(2)}) collective-permute-start(bf16[2560,448]{0,1:T(8,128)(2,1)} %copy.125), channel_id=1, source_target_pairs={{0,2},{1,3},{2,0},{3,1},{4,6},{5,7},{6,4},{7,5},{8,10},{9,11},{10,... | collective-permute-start | bytes 6881288 | tf_op jit(solution)/shard_map/ppermute | solution.py:62
  327.2 85.5 %collective-permute-start.41 = (bf16[2560,448]{0,1:T(8,128)(2,1)}, bf16[2560,448]{0,1:T(8,128)(2,1)S(1)}, u32[]{:S(2)}, u32[]{:S(2)}) collective-permute-start(bf16[2560,448]{0,1:T(8,128)(2,1)} %copy.123), channel_id=1, source_target_pairs={{0,2},{1,3},{2,0},{3,1},{4,6},{5,7},{6,4},{7,5},{8,10},{9,11},{10,... | collective-permute-start | bytes 6881288 | tf_op jit(solution)/shard_map/ppermute | solution.py:62
  432.1 72.9 %collective-permute-start.94 = (bf16[4,320,448]{2,1,0:T(8,128)(2,1)}, bf16[4,320,448]{2,1,0:T(8,128)(2,1)}, u32[]{:S(2)}, u32[]{:S(2)}) collective-permute-start(bf16[4,320,448]{2,1,0:T(8,128)(2,1)} %dynamic-slice_bitcast_fusion.2), channel_id=1, source_target_pairs={{0,4},{1,5},{2,6},{3,7},{4,0},{5,1},{6,2},{7,3},{8,12},{9,13},{10,... | collective-permute-start | bytes 3440648 | tf_op jit(solution)/shard_map/ppermute | solution.py:62
  440.0 127.8 %collective-permute-start.93 = (bf16[4,320,448]{2,1,0:T(8,128)(2,1)}, bf16[4,320,448]{2,1,0:T(8,128)(2,1)}, u32[]{:S(2)}, u32[]{:S(2)}) collective-permute-start(bf16[4,320,448]{2,1,0:T(8,128)(2,1)} %dynamic-slice_bitcast_fusion.3), channel_id=1, source_target_pairs={{0,4},{1,5},{2,6},{3,7},{4,0},{5,1},{6,2},{7,3},{8,12},{9,13},{10,... | collective-permute-start | bytes 3440648 | tf_op jit(solution)/shard_map/ppermute | solution.py:62
  452.2 68.0 %collective-permute-start.100 = (bf16[4,320,448]{2,1,0:T(8,128)(2,1)}, bf16[4,320,448]{2,1,0:T(8,128)(2,1)}, u32[]{:S(2)}, u32[]{:S(2)}) collective-permute-start(bf16[4,320,448]{2,1,0:T(8,128)(2,1)} %dynamic-slice_bitcast_fusion), channel_id=1, source_target_pairs={{0,4},{1,5},{2,6},{3,7},{4,0},{5,1},{6,2},{7,3},{8,12},{9,13},{10,... | collective-permute-start | bytes 3440648 | tf_op jit(solution)/shard_map/ppermute | solution.py:62
  464.9 149.0 %collective-permute-start.99 = (bf16[4,320,448]{2,1,0:T(8,128)(2,1)}, bf16[4,320,448]{2,1,0:T(8,128)(2,1)}, u32[]{:S(2)}, u32[]{:S(2)}) collective-permute-start(bf16[4,320,448]{2,1,0:T(8,128)(2,1)} %dynamic-slice_bitcast_fusion.1), channel_id=1, source_target_pairs={{0,4},{1,5},{2,6},{3,7},{4,0},{5,1},{6,2},{7,3},{8,12},{9,13},{10,... | collective-permute-start | bytes 3440648 | tf_op jit(solution)/shard_map/ppermute | solution.py:62
  520.2 122.1 %collective-permute-start.88 = (bf16[2,4,320,448]{3,2,0,1:T(8,128)(2,1)S(1)}, bf16[2,4,320,448]{3,2,0,1:T(8,128)(2,1)S(1)}, u32[]{:S(2)}, u32[]{:S(2)}) collective-permute-start(bf16[2,4,320,448]{3,2,0,1:T(8,128)(2,1)S(1)} %bitcast.555), channel_id=1, source_target_pairs={{0,2},{1,3},{2,0},{3,1},{4,6},{5,7},{6,4},{7,5},{8,10},{9,11},{10,... | collective-permute-start | bytes 6881288 | tf_op jit(solution)/shard_map/ppermute | solution.py:62
  523.7 84.4 %collective-permute-start.95 = (bf16[4,320,448]{2,1,0:T(8,128)(2,1)S(1)}, bf16[4,320,448]{2,1,0:T(8,128)(2,1)S(1)}, u32[]{:S(2)}, u32[]{:S(2)}) collective-permute-start(bf16[4,320,448]{2,1,0:T(8,128)(2,1)S(1)} %fusion.12), channel_id=1, source_target_pairs={{0,2},{1,3},{2,0},{3,1},{4,6},{5,7},{6,4},{7,5},{8,10},{9,11},{10,... | collective-permute-start | bytes 3440648 | tf_op jit(solution)/shard_map/ppermute | solution.py:62
  562.2 71.0 %collective-permute-start.101 = (bf16[4,320,448]{2,1,0:T(8,128)(2,1)S(1)}, bf16[4,320,448]{2,1,0:T(8,128)(2,1)S(1)}, u32[]{:S(2)}, u32[]{:S(2)}) collective-permute-start(bf16[4,320,448]{2,1,0:T(8,128)(2,1)S(1)} %fusion.9), channel_id=1, source_target_pairs={{0,2},{1,3},{2,0},{3,1},{4,6},{5,7},{6,4},{7,5},{8,10},{9,11},{10,... | collective-permute-start | bytes 3440648 | tf_op jit(solution)/shard_map/ppermute | solution.py:62
  567.8 44.1 %collective-permute-start.58 = (bf16[64,2560]{1,0:T(8,128)(2,1)S(1)}, bf16[64,2560]{1,0:T(8,128)(2,1)S(1)}, u32[]{:S(2)}, u32[]{:S(2)}) collective-permute-start(bf16[64,2560]{1,0:T(8,128)(2,1)S(1)} %fusion.47), channel_id=1, source_target_pairs={{0,8},{1,9},{2,10},{3,11},{4,12},{5,13},{6,14},{7,15},{8,24},{9,25... | collective-permute-start | bytes 983048 | tf_op jit(solution)/shard_map/ppermute | solution.py:62
  648.5 61.6 %collective-permute-start.89 = (bf16[4,320,448]{2,1,0:T(8,128)(2,1)}, bf16[4,320,448]{2,1,0:T(8,128)(2,1)}, u32[]{:S(2)}, u32[]{:S(2)}) collective-permute-start(bf16[4,320,448]{2,1,0:T(8,128)(2,1)} %dynamic-slice_bitcast_fusion.4), channel_id=1, source_target_pairs={{0,4},{1,5},{2,6},{3,7},{4,0},{5,1},{6,2},{7,3},{8,12},{9,13},{10,... | collective-permute-start | bytes 3440648 | tf_op jit(solution)/shard_map/ppermute | solution.py:62
  693.8 47.8 %collective-permute-start.50 = (f32[128,2560]{1,0:T(8,128)}, f32[128,2560]{1,0:T(8,128)}, u32[]{:S(2)}, u32[]{:S(2)}) collective-permute-start(f32[128,2560]{1,0:T(8,128)} %bitcast.120), channel_id=1, source_target_pairs={{0,2},{1,3},{2,0},{3,1},{4,6},{5,7},{6,4},{7,5},{8,10},{9,11},{10,... | collective-permute-start | bytes 3932168 | tf_op jit(solution)/shard_map/ppermute | solution.py:62
  (149 other events, 2323.8 us)

commit v2 on v1

v2 whole, which is shorter than its diff:
```python
import functools

import jax
import jax.numpy as jnp
from jax import lax
from jax.experimental import pallas as pl
from jax.experimental.pallas import tpu as pltpu
from jax.sharding import PartitionSpec as P

HEAD_DIM = 80
EPSILON = 1e-05
NEGATIVE = -1e30
BF16 = jnp.bfloat16
F32 = jnp.float32
AXES = ("dp", "tensor")


def dot(left, right):
    return jnp.dot(left, right, preferred_element_type=F32)


def contract_last(left, right):
    return lax.dot_general(left, right, (((1,), (1,)), ((), ())), preferred_element_type=F32)


def contract_first(left, right):
    return lax.dot_general(left, right, (((0,), (0,)), ((), ())), preferred_element_type=F32)


def after(value, *others):
    return lax.optimization_barrier((value,) + others)[0]


def pick(stack, index):
    return lax.dynamic_index_in_dim(stack, index, 0, keepdims=False)


def place(parts, indices):
    total = jnp.zeros((len(parts),) + parts[0].shape, parts[0].dtype)
    for part, index in zip(parts, indices):
        total = lax.dynamic_update_index_in_dim(total, part, index, 0)
    return total


def whole_vmem():
    return pl.BlockSpec(memory_space=pltpu.VMEM)


def anywhere():
    return pl.BlockSpec(memory_space=pl.ANY)


class Taker:
    def __init__(self, refs):
        self.refs, self.at = refs, 0

    def __call__(self, number):
        taken = self.refs[self.at : self.at + number]
        self.at += number
        return taken


def pack_kernel(Z, where, gate, up, down, *outs):
    n = gate.shape[1] // Z
    for k in range(Z):
        wanted = lax.rem(where[0] + k, Z)
        for s in range(Z):

            @pl.when(wanted == s)
            def _(k=k, s=s):
                for i, weight in enumerate((gate, up, down)):
                    outs[k][:, i * n : (i + 1) * n] = weight[:, s * n : (s + 1) * n]


def pack_hidden(grid, w_gate, w_up, w_down_t):
    rows, cols = w_gate.shape
    return pl.pallas_call(
        functools.partial(pack_kernel, grid.Z),
        out_shape=[jax.ShapeDtypeStruct((rows, 3 * cols // grid.Z), BF16)] * grid.Z,
        in_specs=[pl.BlockSpec(memory_space=pltpu.SMEM)] + [whole_vmem()] * 3,
        out_specs=[whole_vmem()] * grid.Z,
        compiler_params=pltpu.CompilerParams(vmem_limit_bytes=32 * 2**20),
    )(grid.where, w_gate, w_up, w_down_t)


def unpack_kernel(Z, where, *refs):
    parts, outs = refs[:Z], refs[Z:]
    n = parts[0].shape[1] // 3
    for k in range(Z):
        block = lax.rem(where[0] - k + Z, Z)
        for s in range(Z):

            @pl.when(block == s)
            def _(k=k, s=s):
                for i in range(3):
                    outs[i][:, s * n : (s + 1) * n] = parts[k][:, i * n : (i + 1) * n].astype(F32)


def unpack_hidden(grid, parts):
    rows, n = parts[0].shape
    return pl.pallas_call(
        functools.partial(unpack_kernel, grid.Z),
        out_shape=[jax.ShapeDtypeStruct((rows, grid.Z * n // 3), F32)] * 3,
        in_specs=[pl.BlockSpec(memory_space=pltpu.SMEM)] + [whole_vmem()] * grid.Z,
        out_specs=[whole_vmem()] * 3,
        compiler_params=pltpu.CompilerParams(vmem_limit_bytes=32 * 2**20),
    )(grid.where, *parts)


def pack_heads_kernel(U, Y, sizes, where, *refs):
    take = Taker(refs)
    sources, outs, weights, sems = take(len(sizes)), take(Y), take(len(sizes)), take(1)[0]
    copies = [
        pltpu.make_async_copy(source, weight, sems.at[i])
        for i, (source, weight) in enumerate(zip(sources, weights))
    ]
    for copy in copies:
        copy.start()
    for copy in copies:
        copy.wait()
    half = outs[0].shape[1]
    y = where[2]
    for u in range(U):
        first = 0
        for weight, size in zip(weights, sizes):
            columns = weight[:, u * size : (u + 1) * size].astype(F32)
            for k in range(Y):
                part = columns[:half]
                for h in range(1, Y):
                    chosen = lax.rem(y + k, Y) == h
                    part = jnp.where(chosen, columns[h * half : (h + 1) * half], part)
                outs[k][u, :, first : first + size] = part.astype(BF16)
            first += size
        spare = outs[0].shape[2] - first
        if spare:
            for k in range(Y):
                outs[k][u, :, first:] = jnp.zeros((half, spare), BF16)


def pack_heads(grid, weights):
    U, Y = grid.U, grid.Y
    rows = weights[0].shape[0]
    sizes = tuple(weight.shape[1] // U for weight in weights)
    n = -(-sum(sizes) // 128) * 128
    return pl.pallas_call(
        functools.partial(pack_heads_kernel, U, Y, sizes),
        out_shape=[jax.ShapeDtypeStruct((U, rows // Y, n), BF16)] * Y,
        in_specs=[pl.BlockSpec(memory_space=pltpu.SMEM)] + [anywhere()] * len(weights),
        out_specs=[whole_vmem()] * Y,
        scratch_shapes=[pltpu.VMEM(weight.shape, BF16) for weight in weights]
        + [pltpu.SemaphoreType.DMA((len(weights),))],
        compiler_params=pltpu.CompilerParams(vmem_limit_bytes=32 * 2**20),
    )(grid.where, *weights)


def route_kernel(Z, U, Y, where, *refs):
    near, outs = refs[:Y], refs[Y:]
    z, y = where[0], where[2]
    for k in range(Z):
        target = lax.rem(z + k, Z)
        u = lax.rem(target, U)
        from_y = lax.rem(y - lax.div(target, U) + Y, Y)
        for r in range(Y):

            @pl.when(from_y == r)
            def _(k=k, r=r, u=u):
                outs[k][...] = near[r][u]


def route_heads(grid, near):
    _, half, n = near[0].shape
    return pl.pallas_call(
        functools.partial(route_kernel, grid.Z, grid.U, grid.Y),
        out_shape=[jax.ShapeDtypeStruct((half, n), BF16)] * grid.Z,
        in_specs=[pl.BlockSpec(memory_space=pltpu.SMEM)] + [whole_vmem()] * grid.Y,
        out_specs=[whole_vmem()] * grid.Z,
        compiler_params=pltpu.CompilerParams(vmem_limit_bytes=32 * 2**20),
    )(grid.where, *near)


def assemble_kernel(Z, X, Y, where, *refs):
    units, out = refs[: X * Y], refs[X * Y]
    z, x, y = where[0], where[1], where[2]
    for yr in range(Y):
        for xr in range(X):
            for k in range(Z):
                spot = lax.rem(z - k + Z, Z) * X + lax.rem(x - xr + X, X)
                spot = spot * Y + lax.rem(y - yr + Y, Y)
                out[spot] = units[yr * X + xr][k]


def assemble(grid, units):
    Z, X, Y = grid.Z, grid.X, grid.Y
    _, part, n = units[0].shape
    out = pl.pallas_call(
        functools.partial(assemble_kernel, Z, X, Y),
        out_shape=jax.ShapeDtypeStruct((Z * X * Y, part, n), BF16),
        in_specs=[pl.BlockSpec(memory_space=pltpu.SMEM)] + [whole_vmem()] * (X * Y),
        out_specs=whole_vmem(),
        compiler_params=pltpu.CompilerParams(vmem_limit_bytes=32 * 2**20),
    )(grid.where, *units)
    return out.reshape(-1, n)


def hidden_kernel(Z, X, tiles, order, where, *refs):
    take = Taker(refs)
    act_refs, grad_refs, units = take(tiles), take(tiles), take(X * Z)
    in_own, in_low, out_own, out_low, both_grads, products = take(6)
    weights, acts, grads, sems = take(4)
    z, x = where[0], where[1]
    rows = units[0].shape[0]
    n = units[0].shape[1] // 3
    tokens = act_refs[0].shape[0]
    own = tokens // Z
    ring = sum(jnp.where(z == value, place, 0) for place, value in enumerate(order))

    def rows_of(s):
        ranked = lax.rem(ring - s + Z, Z)
        at = sum(jnp.where(ranked == place, value, 0) for place, value in enumerate(order))
        return at * own

    copies = []
    for xr in range(X):
        for k in range(Z):
            spot = lax.rem(z - k + Z, Z) * X + lax.rem(x - xr + X, X)
            at = pl.ds(pl.multiple_of(spot * rows, 16), rows)
            copies.append(pltpu.make_async_copy(units[xr * Z + k], weights.at[at], sems.at[0]))
    for i in range(tiles):
        copies.append(pltpu.make_async_copy(act_refs[i], acts.at[i], sems.at[0]))
        for s in range(Z):
            at = pl.ds(pl.multiple_of(rows_of(s), own), own)
            copies.append(
                pltpu.make_async_copy(
                    grad_refs[i].at[at], grads.at[i, pl.ds(s * own, own)], sems.at[0]
                )
            )
    for copy in copies:
        copy.start()
    for copy in copies:
        copy.wait()

    def one_tile(i, carry):
        both = dot(acts[i], weights[:, : 2 * n])
        gate, up = both[:, :n], both[:, n:]
        product_grad = dot(grads[i], weights[:, 2 * n :])
        sigma = 1.0 / (1.0 + jnp.exp(-gate))
        silu = gate * sigma
        product = (silu * up).astype(BF16)
        up_grad = (product_grad * silu).astype(BF16)
        gate_grad = (product_grad * up * sigma * (1.0 + gate * (1.0 - sigma))).astype(BF16)
        both_grad = jnp.concatenate([gate_grad, up_grad], 1)
        at = pl.ds(pl.multiple_of(i * tokens, tokens), tokens)
        both_grads[at, :] = both_grad
        in_part = contract_last(both_grad, weights[:, : 2 * n])
        out_part = contract_last(product, weights[:, 2 * n :])
        for s in range(Z):
            spot = pl.ds(pl.multiple_of(i * tokens + rows_of(s), own), own)
            products[spot, :] = product[s * own : (s + 1) * own]

        @pl.when(i == 0)
        def _():
            in_own[...] = in_part
            for s in range(Z):
                spot = pl.ds(pl.multiple_of(rows_of(s), own), own)
                out_own[spot, :] = out_part[s * own : (s + 1) * own]

        @pl.when(i > 0)
        def _():
            low_at = pl.ds(pl.multiple_of((i - 1) * tokens, tokens), tokens)
            in_low[low_at, :] = in_part.astype(BF16)
            for s in range(Z):
                spot = pl.ds(pl.multiple_of((i - 1) * tokens + rows_of(s), own), own)
                out_low[spot, :] = out_part[s * own : (s + 1) * own].astype(BF16)

        return carry

    lax.fori_loop(0, tiles, one_tile, 0)


def hidden_layer(grid, acts, grads, units):
    Z, X, C = grid.Z, grid.X, grid.C
    tokens, width = acts[0].shape
    n = units[0].shape[1] // 3
    shape = jax.ShapeDtypeStruct
    rows = [shape((tokens, width), F32), shape(((C - 1) * tokens, width), BF16)]
    shapes = rows + rows + [shape((C * tokens, 2 * n), BF16), shape((C * tokens, n), BF16)]
    return pl.pallas_call(
        functools.partial(hidden_kernel, Z, X, C, tuple(grid.order)),
        out_shape=shapes,
        in_specs=[pl.BlockSpec(memory_space=pltpu.SMEM)] + [anywhere()] * (2 * C + X * Z),
        out_specs=[whole_vmem()] * len(shapes),
        scratch_shapes=[
            pltpu.VMEM((width, 3 * n), BF16),
            pltpu.VMEM((C, tokens, width), BF16),
            pltpu.VMEM((C, tokens, width), BF16),
            pltpu.SemaphoreType.DMA((1,)),
        ],
        compiler_params=pltpu.CompilerParams(vmem_limit_bytes=36 * 2**20),
        cost_estimate=pl.CostEstimate(
            flops=12 * C * tokens * width * n,
            bytes_accessed=20 * 2**20,
            transcendentals=C * tokens * n,
        ),
    )(grid.where, *acts, *grads, *units)


def norm_kernel(values, more, gain, total, normed):
    hidden = values[...].astype(F32) + more[...].astype(F32)
    recip = lax.rsqrt(jnp.mean(hidden * hidden, -1, keepdims=True) + EPSILON)
    total[...] = hidden
    normed[...] = (hidden * recip * gain[...]).astype(BF16)


def add_norm(values, more, gain):
    return pl.pallas_call(
        norm_kernel,
        out_shape=[
            jax.ShapeDtypeStruct(values.shape, F32),
            jax.ShapeDtypeStruct(values.shape, BF16),
        ],
        in_specs=[whole_vmem()] * 3,
        out_specs=[whole_vmem()] * 2,
        compiler_params=pltpu.CompilerParams(vmem_limit_bytes=32 * 2**20),
    )(values, more, gain)


def norm_back_kernel(number, *refs):
    parts = refs[:number]
    values, beside, gain, grad, low, gain_term = refs[number:]
    part = parts[0][...].astype(F32)
    for ref in parts[1:]:
        part = part + ref[...].astype(F32)
    value = values[...].astype(F32)
    recip = lax.rsqrt(jnp.mean(value * value, -1, keepdims=True) + EPSILON)
    normal = value * recip
    scaled = part * gain[...]
    mean = jnp.mean(scaled * normal, -1, keepdims=True)
    total = beside[...].astype(F32) + recip * (scaled - normal * mean)
    grad[...] = total
    low[...] = total.astype(BF16)
    gain_term[...] = jnp.sum(part * normal, 0, keepdims=True)


def norm_back(parts, values, beside, gain):
    return pl.pallas_call(
        functools.partial(norm_back_kernel, len(parts)),
        out_shape=[
            jax.ShapeDtypeStruct(values.shape, F32),
            jax.ShapeDtypeStruct(values.shape, BF16),
            jax.ShapeDtypeStruct(gain.shape, F32),
        ],
        in_specs=[whole_vmem()] * (3 + len(parts)),
        out_specs=[whole_vmem()] * 3,
        compiler_params=pltpu.CompilerParams(vmem_limit_bytes=32 * 2**20),
    )(*parts, values, beside, gain)


def place_kernel(Y, C, where, *refs):
    parts, out = refs[:-1], refs[-1]
    y, c = where[2], where[3]
    own = parts[0].shape[0]
    for i, part in enumerate(parts):
        at = lax.rem(c - i // Y + C, C) * own
        at = pl.ds(pl.multiple_of(at, own), own)
        out[lax.rem(y - i % Y + Y, Y), at, :] = part[...].astype(F32)


def place_rows(grid, parts):
    own, width = parts[0].shape
    return pl.pallas_call(
        functools.partial(place_kernel, grid.Y, grid.C),
        out_shape=jax.ShapeDtypeStruct((grid.Y, grid.C * own, width), F32),
        in_specs=[pl.BlockSpec(memory_space=pltpu.SMEM)] + [whole_vmem()] * len(parts),
        out_specs=whole_vmem(),
        compiler_params=pltpu.CompilerParams(vmem_limit_bytes=32 * 2**20),
    )(grid.where, *parts)


def core_sum_kernel(number, own, *refs):
    lows, outs = refs[:number], refs[number:]
    total = own[...]
    for low in lows:
        total = total + low[...].astype(F32)
    if len(outs) == 1:
        outs[0][...] = total.astype(outs[0].dtype)
        return
    half = total.shape[0] // 2
    outs[0][...] = total[:half].astype(outs[0].dtype)
    outs[1][...] = total[half:].astype(outs[1].dtype)


def core_sum(own, lows, kind, pieces):
    rows, width = own.shape
    return pl.pallas_call(
        functools.partial(core_sum_kernel, len(lows)),
        out_shape=[jax.ShapeDtypeStruct((rows // pieces, width), kind)] * pieces,
        in_specs=[whole_vmem()] * (1 + len(lows)),
        out_specs=[whole_vmem()] * pieces,
        compiler_params=pltpu.CompilerParams(vmem_limit_bytes=32 * 2**20),
    )(own, *lows)


def hidden_weight_kernel(X, tiles, where, *refs):
    take = Taker(refs)
    acts, grads = take(tiles), take(tiles)
    Y = (len(refs) - 2 * tiles - X - 1) // 2
    both_grads, products, outs, total = take(Y), take(Y), take(X), take(1)[0]
    x = where[1]
    tokens = acts[0].shape[0]
    rows = outs[0].shape[0]
    n = products[0].shape[1]

    def summed(parts, values):
        sums = None
        for i in range(tiles):
            at = i // Y * tokens
            part = contract_first(parts[i][...], values[i % Y][at : at + tokens, :])
            sums = part if sums is None else sums + part
        return sums

    total[:, : 2 * n] = summed(acts, both_grads)
    total[:, 2 * n :] = summed(grads, products)
    for xr in range(X):
        at = pl.ds(pl.multiple_of(lax.rem(x + xr, X) * rows, 8), rows)
        outs[xr][...] = total[at, :].astype(BF16)


def hidden_weight_grad(grid, k, acts, grads, both_grads, products):
    Z, X, tiles = grid.Z, grid.X, len(acts)
    tokens, width = acts[0].shape
    n = products[0].shape[1]
    block = width // Z

    def features(i, s):
        return (0, lax.rem(s[0] + k, Z))

    return pl.pallas_call(
        functools.partial(hidden_weight_kernel, X, tiles),
        out_shape=[jax.ShapeDtypeStruct((block // X, 3 * n), BF16)] * X,
        grid_spec=pltpu.PrefetchScalarGridSpec(
            num_scalar_prefetch=1,
            grid=(1,),
            in_specs=[pl.BlockSpec((tokens, block), features)] * (2 * tiles)
            + [pl.BlockSpec(value.shape, lambda i, s: (0, 0)) for value in both_grads + products],
            out_specs=[pl.BlockSpec((block // X, 3 * n), lambda i, s: (0, 0))] * X,
            scratch_shapes=[pltpu.VMEM((block, 3 * n), F32)],
        ),
        compiler_params=pltpu.CompilerParams(vmem_limit_bytes=26 * 2**20),
        cost_estimate=pl.CostEstimate(
            flops=6 * tiles * tokens * block * n, bytes_accessed=10 * 2**20, transcendentals=0
        ),
    )(grid.where, *acts, *grads, *both_grads, *products)


def weight_kernel(X, Y, where, act, grad, *refs):
    outs, total = refs[: Y * X], refs[Y * X]
    x, y = where[1], where[2]
    part = outs[0].shape[1]
    total[...] = contract_first(act[...], grad[...])
    for xr in range(X):
        for yr in range(Y):
            at = (lax.rem(x + xr, X) * Y + lax.rem(y + yr, Y)) * part
            at = pl.ds(pl.multiple_of(at, 8), part)
            outs[yr * X + xr][0] = total[at, :].astype(BF16)


def weight_grad(grid, act, grad):
    Z, X, Y = grid.Z, grid.X, grid.Y
    tokens, width = act.shape
    n = grad.shape[1]
    part = width // (Z * X * Y)
    return pl.pallas_call(
        functools.partial(weight_kernel, X, Y),
        out_shape=[jax.ShapeDtypeStruct((Z, part, n), BF16)] * (Y * X),
        grid_spec=pltpu.PrefetchScalarGridSpec(
            num_scalar_prefetch=1,
            grid=(Z,),
            in_specs=[
                pl.BlockSpec((tokens, width // Z), lambda k, s: (0, lax.rem(s[0] + k, Z))),
                pl.BlockSpec((tokens, n), lambda k, s: (0, 0)),
            ],
            out_specs=[pl.BlockSpec((1, part, n), lambda k, s: (k, 0, 0))] * (Y * X),
            scratch_shapes=[pltpu.VMEM((width // Z, n), F32)],
        ),
        compiler_params=pltpu.CompilerParams(vmem_limit_bytes=26 * 2**20),
        cost_estimate=pl.CostEstimate(
            flops=2 * tokens * width * n, bytes_accessed=2 * width * n, transcendentals=0
        ),
    )(grid.where, act, grad)


def identity(number):
    row = lax.broadcasted_iota(jnp.int32, (number, number), 0)
    column = lax.broadcasted_iota(jnp.int32, (number, number), 1)
    return jnp.where(row == column, 1.0, 0.0).astype(BF16)


def visible(X, rows, where, limit, first, tile, keys):
    x = where[1]
    key = lax.broadcasted_iota(jnp.int32, (keys, 1), 0)
    tokens = keys // X
    inside = lax.rem(key, tokens)
    key_x = lax.rem(x - lax.div(key, tokens) + X, X)
    key_pos = (lax.div(inside, rows) * X + key_x) * rows + lax.rem(inside, rows)
    query = first + lax.broadcasted_iota(jnp.int32, (1, tile), 1)
    query_pos = (lax.div(query, rows) * X + x) * rows + lax.rem(query, rows)
    return (key_pos <= query_pos) | (key_pos < limit)


def split_heads(qkv, others, queries, keys_values, turned, group):
    tokens = qkv.shape[0]
    for g in range(group):
        queries[g] = qkv[:, g * HEAD_DIM : (g + 1) * HEAD_DIM]
    eye = identity(2 * HEAD_DIM)
    for i in range(1 + len(others)):
        at = slice(i * tokens, (i + 1) * tokens)
        both = qkv[:, group * HEAD_DIM : (group + 2) * HEAD_DIM] if i == 0 else others[i - 1][...]
        keys_values[0, at, :] = both[:, :HEAD_DIM]
        keys_values[1, at, :] = both[:, HEAD_DIM:]
        turned[:, at] = contract_last(eye, both).astype(BF16)


def attend_kernel(X, rows, group, tile, where, prefix, qkv, *refs):
    take = Taker(refs)
    others, heads, stats = take(X - 1), take(1)[0], take(1)[0]
    queries, keys_values, turned = take(3)
    tokens = qkv.shape[0]
    scale = HEAD_DIM ** (-0.5)
    split_heads(qkv, others, queries, keys_values, turned, group)
    limit = prefix[where[2]]
    for t in range(tokens // tile):
        at = slice(t * tile, (t + 1) * tile)
        allowed = visible(X, rows, where, limit, t * tile, tile, X * tokens)
        outs = []
        for g in range(group):
            scores = contract_last(keys_values[0], queries[g, at, :]) * scale
            scores = jnp.where(allowed, scores, NEGATIVE)
            top = jnp.max(scores, 0, keepdims=True)
            expo = jnp.exp(scores - top)
            total = jnp.sum(expo, 0, keepdims=True)
            probs = (expo / total).astype(BF16)
            outs.append(jnp.transpose(dot(turned[HEAD_DIM:, :], probs)).astype(BF16))
            stats[g : g + 1, at] = top
            stats[group + g : group + g + 1, at] = total
        heads[at, :] = jnp.concatenate(outs, 1)


def attend_back_kernel(X, rows, group, tile, where, prefix, qkv, *refs):
    take = Taker(refs)
    others, heads_grad, stats = take(X - 1), take(1)[0], take(1)[0]
    query_grad, kv_grads = take(1)[0], take(X)
    queries, keys_values, turned, grads, key_sum, value_sum = take(6)
    tokens = qkv.shape[0]
    scale = HEAD_DIM ** (-0.5)
    split_heads(qkv, others, queries, keys_values, turned, group)
    for g in range(group):
        grads[g] = heads_grad[:, g * HEAD_DIM : (g + 1) * HEAD_DIM]
    limit = prefix[where[2]]
    for t in range(tokens // tile):
        at = slice(t * tile, (t + 1) * tile)
        allowed = visible(X, rows, where, limit, t * tile, tile, X * tokens)
        outs = []
        for g in range(group):
            query, grad = queries[g, at, :], grads[g, at, :]
            scores = contract_last(keys_values[0], query) * scale
            scores = jnp.where(allowed, scores, NEGATIVE)
            probs = jnp.exp(scores - stats[g : g + 1, at]) / stats[group + g : group + g + 1, at]
            prob_grad = contract_last(keys_values[1], grad)
            mean = jnp.sum(probs * prob_grad, 0, keepdims=True)
            score_grad = (probs * (prob_grad - mean)).astype(BF16)
            out = jnp.transpose(dot(turned[:HEAD_DIM, :], score_grad)) * scale
            outs.append(out.astype(BF16))
            key_part = dot(score_grad, query)
            value_part = dot(probs.astype(BF16), grad)
            if t == 0 and g == 0:
                key_sum[...] = key_part
                value_sum[...] = value_part
            else:
                key_sum[...] += key_part
                value_sum[...] += value_part
        query_grad[at, :] = jnp.concatenate(outs, 1)
    for i, out in enumerate(kv_grads):
        at = slice(i * tokens, (i + 1) * tokens)
        out[:, :HEAD_DIM] = key_sum[at, :] * scale
        out[:, HEAD_DIM:] = value_sum[at, :]


def query_tile(tokens, keys):
    tile = tokens
    while tile > 128 and tile * keys > 2**19:
        tile = tile // 2
    return tile


def attend(grid, rows, group, prefix, qkv, others):
    tokens, keys = qkv.shape[0], grid.X * qkv.shape[0]
    smem = pl.BlockSpec(memory_space=pltpu.SMEM)
    return pl.pallas_call(
        functools.partial(attend_kernel, grid.X, rows, group, query_tile(tokens, keys)),
        out_shape=[
            jax.ShapeDtypeStruct((tokens, group * HEAD_DIM), BF16),
            jax.ShapeDtypeStruct((2 * group, tokens), F32),
        ],
        in_specs=[smem, smem] + [whole_vmem()] * grid.X,
        out_specs=[whole_vmem()] * 2,
        scratch_shapes=[
            pltpu.VMEM((group, tokens, HEAD_DIM), BF16),
            pltpu.VMEM((2, keys, HEAD_DIM), BF16),
            pltpu.VMEM((2 * HEAD_DIM, keys), BF16),
        ],
        compiler_params=pltpu.CompilerParams(vmem_limit_bytes=36 * 2**20),
        cost_estimate=pl.CostEstimate(
            flops=8 * group * tokens * keys * 128,
            bytes_accessed=4 * 2**20,
            transcendentals=group * tokens * keys,
        ),
    )(grid.where, prefix, qkv, *others)


def attend_back(grid, rows, group, prefix, qkv, others, heads_grad, stats):
    tokens, keys = qkv.shape[0], grid.X * qkv.shape[0]
    smem = pl.BlockSpec(memory_space=pltpu.SMEM)
    return pl.pallas_call(
        functools.partial(attend_back_kernel, grid.X, rows, group, query_tile(tokens, keys)),
        out_shape=[jax.ShapeDtypeStruct((tokens, group * HEAD_DIM), BF16)]
        + [jax.ShapeDtypeStruct((tokens, 2 * HEAD_DIM), F32)] * grid.X,
        in_specs=[smem, smem] + [whole_vmem()] * (grid.X + 2),
        out_specs=[whole_vmem()] * (1 + grid.X),
        scratch_shapes=[
            pltpu.VMEM((group, tokens, HEAD_DIM), BF16),
            pltpu.VMEM((2, keys, HEAD_DIM), BF16),
            pltpu.VMEM((2 * HEAD_DIM, keys), BF16),
            pltpu.VMEM((group, tokens, HEAD_DIM), BF16),
            pltpu.VMEM((keys, HEAD_DIM), F32),
            pltpu.VMEM((keys, HEAD_DIM), F32),
        ],
        compiler_params=pltpu.CompilerParams(vmem_limit_bytes=36 * 2**20),
        cost_estimate=pl.CostEstimate(
            flops=16 * group * tokens * keys * 128,
            bytes_accessed=4 * 2**20,
            transcendentals=group * tokens * keys,
        ),
    )(grid.where, prefix, qkv, *others, heads_grad, stats)


class Grid:
    def __init__(self, dp, tensor, seqs, kv_local):
        self.Y = seqs
        self.C = tensor // seqs
        self.U = kv_local
        self.Z = seqs * kv_local
        self.X = dp // self.Z
        assert self.C * self.Y == tensor and self.X * self.Z == dp
        i, j = lax.axis_index("dp"), lax.axis_index("tensor")
        self.z, self.x = i // self.X, i % self.X
        self.y, self.c = j // self.C, j % self.C
        self.where = jnp.stack([self.z, self.x, self.y, self.c]).astype(jnp.int32)
        order = list(range(0, self.Z, 2)) + list(range(1, self.Z, 2))[::-1]
        self.order = order
        self.ring = [order.index(z) for z in range(self.Z)]

    def move(self, value, target):
        pairs = []
        for z in range(self.Z):
            for x in range(self.X):
                for y in range(self.Y):
                    for c in range(self.C):
                        tz, tx, ty, tc = target(z, x, y, c)
                        here = ((z * self.X + x) * self.Y + y) * self.C + c
                        there = ((tz * self.X + tx) * self.Y + ty) * self.C + tc
                        pairs.append((here, there))
        return lax.ppermute(value, AXES, pairs)

    def to_z(self, value, k):
        return self.move(value, lambda z, x, y, c: ((z + k) % self.Z, x, y, c))

    def hop_z(self, value, k):
        if 1 < k < self.Z - 1:
            return self.to_z(self.to_z(value, 1), k - 1)
        return self.to_z(value, k)

    def to_x(self, value, k):
        return self.move(value, lambda z, x, y, c: (z, (x + k) % self.X, y, c))

    def to_y(self, value, k):
        return self.move(value, lambda z, x, y, c: (z, x, (y + k) % self.Y, c))

    def to_c(self, value, k):
        return self.move(value, lambda z, x, y, c: (z, x, y, (c + k) % self.C))

    def along_ring(self, value, k):
        return self.move(
            value, lambda z, x, y, c: (self.order[(self.ring[z] + k) % self.Z], x, y, c)
        )

    def slot_z(self, s):
        place_of = sum(jnp.where(self.z == z, ring, 0) for z, ring in enumerate(self.ring))
        place_of = (place_of - s) % self.Z
        return sum(jnp.where(place_of == at, z, 0) for at, z in enumerate(self.order))

    def to_xy(self, value, kx, ky):
        return self.move(
            value, lambda z, x, y, c: (z, (x + kx) % self.X, (y + ky) % self.Y, c)
        )

    def groups(self, names):
        sizes = {"z": self.Z, "x": self.X, "y": self.Y, "c": self.C}
        members = {}
        for z in range(self.Z):
            for x in range(self.X):
                for y in range(self.Y):
                    for c in range(self.C):
                        at = {"z": z, "x": x, "y": y, "c": c}
                        key = tuple(at[name] for name in sizes if name not in names)
                        rank = 0
                        for name in names:
                            rank = rank * sizes[name] + at[name]
                        index = ((z * self.X + x) * self.Y + y) * self.C + c
                        members.setdefault(key, {})[rank] = index
        return [[group[rank] for rank in range(len(group))] for group in members.values()]

    def gather(self, own, names):
        return lax.all_gather(own, AXES, axis=0, tiled=True, axis_index_groups=self.groups(names))

    def scatter(self, partial, names):
        return lax.psum_scatter(
            partial,
            AXES,
            scatter_dimension=0,
            tiled=True,
            axis_index_groups=self.groups(names),
        )

    def ring_steps(self, own, steps):
        blocks = [own]
        for _ in range(steps):
            blocks.append(self.along_ring(blocks[-1], 1))
        return blocks

    def spread_yc(self, mine):
        pieces = [mine] + [self.to_y(mine, k) for k in range(1, self.Y)]
        return pieces + [self.to_c(piece, k) for k in range(1, self.C) for piece in pieces]

    def gather_wide(self, blocks, hold=()):
        half = self.Z // 2
        first = jnp.concatenate(blocks[:half], 0)
        second = jnp.concatenate(blocks[half:], 0)
        pieces = [jnp.concatenate([first, second], 0)]
        for k in range(1, self.Y):
            pieces.append(
                jnp.concatenate([after(self.to_y(first, k), *hold), self.to_y(second, k)], 0)
            )
        return pieces + [self.to_c(piece, k) for k in range(1, self.C) for piece in pieces]

    def ring_sum(self, slots, holds=()):
        total = slots[-1].astype(BF16)
        for i, s in enumerate(range(self.Z - 2, -1, -1)):
            if i < len(holds):
                total = after(total, *holds[i])
            arrived = self.along_ring(total, -1)
            total = arrived.astype(F32) + slots[s]
            if s > 0:
                total = total.astype(BF16)
        return arrived, slots[0]

    def exchange_z(self, parts):
        return [parts[0]] + [self.to_z(parts[k], k) for k in range(1, self.Z)]

    def spread_xy(self, unit):
        return [
            unit if xr == yr == 0 else self.to_xy(unit, xr, yr)
            for yr in range(self.Y)
            for xr in range(self.X)
        ]

    def send_xy(self, units):
        return [
            unit if i == 0 else self.to_xy(unit, i % self.X, i // self.X)
            for i, unit in enumerate(units)
        ]

    def sum_xy(self, arrived):
        sums = []
        for k in range(self.Z):
            total = arrived[0][k].astype(F32)
            for unit in arrived[1:]:
                total = total + unit[k].astype(F32)
            sums.append(total.astype(BF16))
        return sums

    def return_heads(self, units):
        parts = jnp.stack(self.exchange_z(self.sum_xy(units)), 0)
        parts = jnp.stack([pick(parts, (self.z - s) % self.Z) for s in range(self.Z)], 0)
        parts = parts.reshape((self.Y, self.U) + parts.shape[1:])
        halves = [pick(parts, self.y)]
        for k in range(1, self.Y):
            halves.append(self.to_y(pick(parts, (self.y + k) % self.Y), k))
        rows = place(halves, [(self.y - k) % self.Y for k in range(self.Y)])
        return [rows[:, u].reshape(-1, rows.shape[3]) for u in range(self.U)]

    def from_z(self, k):
        return (self.z - k) % self.Z

    def spread_x(self, unit):
        parts = [unit] + [self.to_x(unit, k) for k in range(1, self.X)]
        return place(parts, [(self.x - k) % self.X for k in range(self.X)])

    def gather_gains(self, gains):
        xs = self.spread_x(gains)
        parts = [xs] + [self.to_z(xs, k) for k in range(1, self.Z)]
        whole = place(parts, [self.from_z(k) for k in range(self.Z)])
        return whole.transpose(2, 0, 1, 3).reshape(gains.shape[0], -1)

    def sum_gains(self, terms):
        number = terms.shape[0]
        part = terms
        for k in range(1, self.C):
            part = part + self.to_c(terms, k)
        terms = part
        for k in range(1, self.Y):
            part = part + self.to_y(terms, k)
        part = part.reshape(number, self.Z, self.X, -1).transpose(2, 1, 0, 3)
        out = pick(part, self.x)
        for k in range(1, self.X):
            out = out + self.to_x(pick(part, (self.x + k) % self.X), k)
        return sum(self.exchange_z([pick(out, (self.z + k) % self.Z) for k in range(self.Z)]))


def per_device(
    dp,
    tensor,
    inputs,
    cotangent,
    prefix,
    gain_attn,
    w_query,
    w_key,
    w_value,
    w_out,
    gain_mlp,
    w_gate,
    w_up,
    w_down,
):
    seqs, rows, width = inputs.shape
    kv_local = w_key.shape[1] // HEAD_DIM
    group = w_query.shape[1] // w_key.shape[1]
    grid = Grid(dp, tensor, seqs, kv_local)
    own = rows // grid.C
    q_cols = group * HEAD_DIM

    def own_rows(value):
        return lax.dynamic_slice(value, (grid.y, grid.c * own, 0), (1, own, width))[0]

    others = range(1, grid.X)
    middle = grid.Z // 2
    ends = [k for k in range(1, grid.Z) if k != middle]
    near = pack_heads(grid, [w_query, w_key, w_value])
    near_own = near[0]
    near = [near_own] + [grid.to_y(near[k], k) for k in range(1, grid.Y)]
    gains = grid.gather_gains(jnp.stack([gain_attn, gain_mlp], 0))
    cot_own = own_rows(cotangent)
    cot_all = grid.gather(cot_own, "z")
    flat = own_rows(inputs)
    gain_one, gain_two = gains[0:1].astype(F32), gains[1:2].astype(F32)
    values = flat.astype(F32)
    recip = lax.rsqrt(jnp.mean(values * values, -1, keepdims=True) + EPSILON)
    attn_own = after((values * recip * gain_one).astype(BF16), *near)
    attn_in = grid.gather(attn_own, "zc")
    qkv_parts = grid.exchange_z(route_heads(grid, near))

    packed = pack_hidden(grid, after(w_gate, attn_own), w_up, w_down.T)
    out_near = pack_heads(grid, [after(w_out.T, packed[0])])
    out_near = [out_near[0]] + [grid.to_y(out_near[k], k) for k in range(1, grid.Y)]

    def ring_on(blocks, *hold):
        return blocks + [grid.along_ring(after(blocks[-1], *hold), 1)]

    qkv_units = grid.spread_xy(after(jnp.stack(qkv_parts, 0), cot_all, *out_near))
    out_parts = route_heads(grid, [after(part, *qkv_parts) for part in out_near])
    out_parts = grid.exchange_z(out_parts)
    arrived, first = {0: packed[0]}, out_parts[1:]
    for k in [middle] + ends:
        arrived[k] = grid.hop_z(after(packed[k], *first), k)
        first = [arrived[k]]
    w_qkv = assemble(grid, [after(u, *out_parts[1:]) for u in qkv_units])[:, : q_cols + 2 * HEAD_DIM]
    qkv = dot(attn_in, w_qkv).astype(BF16)
    tokens = qkv.shape[0]
    kv_own = qkv[:, q_cols:]
    kv_others = [grid.to_x(kv_own, k) for k in others]
    heads, stats = attend(grid, rows, group, prefix, qkv, kv_others)
    moved_x, first = {}, qkv_units[1:]
    for k in [0, middle] + ends:
        moved_x[k] = [grid.to_x(after(arrived[k], *first), x) for x in others]
        first = moved_x[k]
        if k == 0:
            out_unit = after(jnp.stack(out_parts, 0), *kv_others, *first)
            out_units = grid.spread_xy(out_unit)
            w_o = assemble(grid, out_units)[:, :q_cols]
            first = out_units[1:]
    mlp_grad = grid.spread_yc(after(cot_all, *out_units[1:]))
    attn_partial = contract_last(after(heads, arrived[middle]), w_o).astype(BF16)
    attn_out = grid.scatter(attn_partial, "zc")
    held = mlp_grad[: grid.Y] + [arrived[ends[0]]] + moved_x[middle]
    hidden, mlp_own = add_norm(flat, after(attn_out, *held), gain_two)
    mlp_blocks = ring_on([mlp_own])
    mlp_blocks = ring_on(mlp_blocks, *mlp_grad, *moved_x[ends[0]])
    for _ in range(grid.Z - 3):
        mlp_blocks = ring_on(mlp_blocks, arrived[ends[-1]])
    mlp_in = grid.gather_wide(mlp_blocks, moved_x[ends[-1]])
    units = [arrived[k] for k in range(grid.Z)]
    units = units + [moved_x[k][x - 1] for x in others for k in range(grid.Z)]

    layers, in_moved, hold = [None] * grid.Y, [], ()
    for yr in range(grid.Y - 1, -1, -1):
        acts = [mlp_in[c * grid.Y + yr] for c in range(grid.C)]
        acts[0] = after(acts[0], *hold)
        grads = [mlp_grad[c * grid.Y + yr] for c in range(grid.C)]
        layers[yr] = hidden_layer(grid, acts, grads, units)
        each = acts[0].shape[0]
        half = each // 2
        low = after(layers[yr][1], *[sent[0] for sent in in_moved])
        moved = [grid.to_c(low[(h - 1) * each : h * each], -h) for h in range(1, grid.C)]
        if yr > 0:
            hold = core_sum(layers[yr][0], moved, BF16, 2)
            in_moved.append([grid.to_y(hold[1], -yr), grid.to_y(hold[0], -yr)])
    both_grads = [layer[4] for layer in layers]
    products = [layer[5] for layer in layers]

    order = [middle] + ends + [0]
    swapped, hidden_parts, holds = [], [None] * grid.Z, []
    for at, k in enumerate(order):
        hold = [in_late] if at else []
        given = both_grads[:-1] + [after(both_grads[-1], *hold)]
        parts = list(hidden_weight_grad(grid, k, mlp_in, mlp_grad, given, products))
        if at == 0:
            in_late, in_first = core_sum(after(layers[0][0], *parts), moved, F32, 2)
        first = swapped[-1] if swapped else []
        swapped.append([grid.to_x(after(parts[xr], *first), xr) for xr in others])
        holds.append(parts)
        hidden_parts[k] = core_sum(parts[0], swapped[-1], BF16, 1)[0]
    for sent in in_moved:
        in_first = in_first + sent[0].astype(F32)
    in_late = after(in_late, in_first)
    for sent in in_moved:
        in_late = in_late + sent[1].astype(F32)
    slots = [
        (in_late, in_first)[2 * s // grid.Z][s % (grid.Z // 2) * own :][:own]
        for s in range(grid.Z)
    ]
    holds, last = [[], holds[1], holds[2] + [hidden_parts[middle]]], holds[3]
    in_parts = grid.ring_sum(slots, holds)
    hidden_grad, hidden_low, gain_two_term = norm_back(in_parts, hidden, cot_own, gain_two)
    attn_grad = grid.gather(hidden_low, "zc")
    out_y = []
    for yr in range(grid.Y - 1, -1, -1):
        low = after(layers[yr][3], in_parts[0])
        moved = [grid.to_c(low[(h - 1) * each : h * each], -h) for h in range(1, grid.C)]
        if yr > 0:
            out_sum = core_sum(layers[yr][2], moved, BF16, 1)[0]
            out_y.append(grid.to_y(out_sum, -yr))
    arrived, first = list(hidden_parts), []
    for k in order[:-1]:
        arrived[k] = grid.hop_z(after(hidden_parts[k], *first), k)
        first = [arrived[k]]
    attn_grad = after(attn_grad, arrived[middle], *last, *swapped[2], *out_y)
    out_sum = core_sum(layers[0][2], moved + out_y, BF16, 1)[0]
    mlp_out = grid.scatter(after(out_sum, attn_grad), "z")
    heads_grad = dot(attn_grad, w_o).astype(BF16)
    out_units = weight_grad(grid, attn_grad, heads)

    heads_grad = after(heads_grad, *out_units)
    query_grad, *kv_parts = attend_back(
        grid, rows, group, prefix, qkv, kv_others, heads_grad, stats
    )
    kv_moved = [grid.to_x(kv_parts[k], -k) for k in others]
    kv_grad = kv_parts[0]
    for part in kv_moved:
        kv_grad = kv_grad + part
    qkv_grad = jnp.concatenate(
        [query_grad, kv_grad.astype(BF16)], 1
    )
    qkv_grad = after(qkv_grad, arrived[order[1]], *swapped[3])
    attn_in_grad = grid.scatter(contract_last(qkv_grad, w_qkv).astype(BF16), "zc")
    qkv_moved = grid.send_xy(weight_grad(grid, attn_in, qkv_grad))
    out_moved = grid.send_xy([after(unit, *qkv_moved[1:]) for unit in out_units])
    ready = after(attn_in_grad, arrived[order[2]], *qkv_moved[1:])
    _, input_low, gain_one_term = norm_back([ready], flat, hidden_grad, gain_one)
    rows_y = [input_low] + [grid.to_y(input_low, k) for k in range(1, grid.Y)]
    rows_c = [grid.to_c(part, k) for k in range(1, grid.C) for part in rows_y]
    input_grad = place_rows(grid, rows_y + rows_c)
    gain_sum = grid.sum_gains(jnp.concatenate([gain_one_term, gain_two_term], 0))

    out_wgrad = grid.return_heads([after(unit, *rows_y[1:]) for unit in out_moved])
    qkv_wgrad = grid.return_heads([after(unit, input_low) for unit in qkv_moved])
    gate_wgrad, up_wgrad, down_wgrad = unpack_hidden(
        grid, [after(a, *qkv_moved[1:]) for a in arrived]
    )
    down_wgrad = down_wgrad.T
    result = hidden + mlp_out.astype(F32)
    result = grid.gather(after(result, attn_in_grad), "yc").reshape(seqs, rows, width)

    return (
        result,
        input_grad,
        gain_sum[0],
        jnp.concatenate([w[:, :q_cols] for w in qkv_wgrad], 1).astype(F32),
        jnp.concatenate([w[:, q_cols : q_cols + HEAD_DIM] for w in qkv_wgrad], 1).astype(F32),
        jnp.concatenate([w[:, q_cols + HEAD_DIM :] for w in qkv_wgrad], 1).astype(F32),
        jnp.concatenate(out_wgrad, 1).T.astype(F32),
        gain_sum[1],
        gate_wgrad,
        up_wgrad,
        down_wgrad,
    )


def solution(mesh):
    dp, tensor = mesh.shape["dp"], mesh.shape["tensor"]

    def step(*args):
        return per_device(dp, tensor, *args)

    return jax.shard_map(
        step,
        mesh=mesh,
        in_specs=(
            P(None, "dp", None),
            P(None, "dp", None),
            P(),
            P("dp"),
            P("dp", "tensor"),
            P("dp", "tensor"),
            P("dp", "tensor"),
            P("tensor", "dp"),
            P("dp"),
            P("dp", "tensor"),
            P("dp", "tensor"),
            P("tensor", "dp"),
        ),
        out_specs=(
            P(None, "dp", None),
            P(None, "dp", None),
            P("dp"),
            P("dp", "tensor"),
            P("dp", "tensor"),
            P("dp", "tensor"),
            P("tensor", "dp"),
            P("dp"),
            P("dp", "tensor"),
            P("dp", "tensor"),
            P("tensor", "dp"),
        ),
        check_vma=False,
    )
```

time: 937 us -> 649 us (0.69)
  waiting for transfers between devices: 461 us -> 325 us
  local copies, waits for them, and re-layouts: 153 us -> 47.6 us
  Pallas kernels: 0 us -> 97.8 us
  matrix products: 103 us -> 13.5 us
  other arithmetic: 53.6 us -> 12.2 us
  starting transfers between devices: 147 us -> 131 us
    ppermute x105 -> x79, waiting for transfers between devices: 461 us -> 294 us  [move(): return lax.ppermute(value, AXES, pairs)]
    pallas_call x0 -> x30, Pallas kernels: none -> 97.8 us  [the longest x2 31.7 us: hidden_layer(): pl.pallas_call(functools.partial(hidden_kernel, Z, X, C, tuple(grid.order...]
    dot_general x13 -> x0, matrix products: 43.3 us -> none  [the longest x8 27.1 us: contract_first(): lax.dot_general(left, right, (((0,), (0,)), ((), ())), preferred_element_...]
    dynamic_update_slice x46 -> x10, local copies, waits for them, and re-layouts: 37.1 us -> 1.24 us  [place(): total = lax.dynamic_update_index_in_dim(total, part, index, 0)]
    convert_element_type x8 -> x3, local copies, waits for them, and re-layouts: 36 us -> 0.27 us  [per_device(): gain_one, gain_two = (gains[0:1].astype(F32), gains[1:2].astype(F32))]
    reduce_scatter x0 -> x3, waiting for transfers between devices: none -> 30.8 us  [scatter(): lax.psum_scatter(partial, AXES, scatter_dimension=0, tiled=True, axis_ind...]
    unnamed x155 -> x189, local copies, waits for them, and re-layouts: 15.5 us -> 41.6 us
    dot_general x8 -> x2, matrix products: 30.8 us -> 6.1 us  [contract_last(): lax.dot_general(left, right, (((1,), (1,)), ((), ())), preferred_element_...]
  transfers between devices with their start and end apart: 105 -> 86, of which waited for: 48 -> 39; matrix products, arithmetic and copies ran while one was open for 30% -> 4% of each run, Pallas kernels for 0% -> 12%
where the time goes in v2:
time: 649 us; the launch traced here: 643 us
  waiting for transfers between devices  325 us (50%)
  starting transfers between devices  131 us (20%)
  Pallas kernels  97.8 us (15%)
  local copies, waits for them, and re-layouts  47.6 us (7%)
  between operations  16.1 us (2%)
  matrix products  13.5 us (2%)
  other arithmetic  12.2 us (2%)
    ppermute x79, waiting for transfers between devices, move(): return lax.ppermute(value, AXES, pairs)  294 us
    ppermute x79, starting transfers between devices, move(): return lax.ppermute(value, AXES, pairs)  131 us
    unnamed x189, local copies, waits for them, and re-layouts  41.6 us
    pallas_call x2, Pallas kernels, hidden_layer(): pl.pallas_call(functools.partial(hidden_kernel, Z, X, C, tuple(grid.order...  31.7 us
    reduce_scatter x3, waiting for transfers between devices, scatter(): lax.psum_scatter(partial, AXES, scatter_dimension=0, tiled=True, axis_ind...  30.8 us
    pallas_call x4, Pallas kernels, hidden_weight_grad(): pl.pallas_call(functools.partial(hidden_weight_kernel, X, tiles), out_sha...  19.5 us
  transfers between devices with their start and end apart: 86, of which 39 were waited for; matrix products, arithmetic and copies ran while one was open for 4% of the time, Pallas kernels for 12%

profile of v2, /device:TPU:0, one launch (start us, length us, event | category | flops | bytes accessed | tf_op | source)
XLA Modules:
  0.0 643.5 jit_solution(10392949242393897807)
XLA Ops:
  42.8 9.0 %collective-permute-done.7 = bf16[160,512]{1,0:T(8,128)(2,1)S(1)} collective-permute-done((bf16[160,512]{1,0:T(8,128)(2,1)S(1)}, bf16[160,512]{1,0:T(8,128)(2,1)S(1)}, u32[]{:S(2)}, u32[]{:S(2)}) %collective-permute-start.7) | collective-permute-done | bytes 163872 | tf_op jit(solution)/shard_map/ppermute | solution.py:672
  51.7 13.7 %collective-permute-done.6 = bf16[160,512]{1,0:T(8,128)(2,1)S(1)} collective-permute-done((bf16[160,512]{1,0:T(8,128)(2,1)S(1)}, bf16[160,512]{1,0:T(8,128)(2,1)S(1)}, u32[]{:S(2)}, u32[]{:S(2)}) %collective-permute-start.6) | collective-permute-done | bytes 163872 | tf_op jit(solution)/shard_map/ppermute | solution.py:672
  82.4 14.3 %collective-permute-start.16 = (bf16[320,1344]{1,0:T(8,128)(2,1)}, bf16[320,1344]{1,0:T(8,128)(2,1)}, u32[]{:S(2)}, u32[]{:S(2)}) collective-permute-start(bf16[320,1344]{1,0:T(8,128)(2,1)} %copy-done.73), channel_id=1, source_target_pairs={{0,8},{1,9},{2,10},{3,11},{4,12},{5,13},{6,14},{7,15},{8,16},{9,17... | collective-permute-start | bytes 2580488 | tf_op jit(solution)/shard_map/ppermute | solution.py:672
  102.9 16.4 %collective-permute-done.16 = bf16[320,1344]{1,0:T(8,128)(2,1)} collective-permute-done((bf16[320,1344]{1,0:T(8,128)(2,1)}, bf16[320,1344]{1,0:T(8,128)(2,1)}, u32[]{:S(2)}, u32[]{:S(2)}) %collective-permute-start.16) | collective-permute-done | bytes 860192 | tf_op jit(solution)/shard_map/ppermute | solution.py:672
  149.3 10.4 %collective-permute-done.20.refs_2_ = bf16[4,160,384]{2,1,0:T(8,128)(2,1)S(1)} collective-permute-done((bf16[4,160,384]{2,1,0:T(8,128)(2,1)S(1)}, bf16[4,160,384]{2,1,0:T(8,128)(2,1)S(1)}, u32[]{:S(2)}, u32[]{:S(2)}) %collective-permute-start.20) | collective-permute-done | bytes 491552 | tf_op jit(solution)/shard_map/ppermute | solution.py:672
  167.9 27.1 %collective-permute-done.22.refs_2_.refs_5_ = bf16[256,2560]{1,0:T(8,128)(2,1)} collective-permute-done((bf16[256,2560]{1,0:T(8,128)(2,1)S(1)}, bf16[256,2560]{1,0:T(8,128)(2,1)}, u32[]{:S(2)}, u32[]{:S(2)}) %collective-permute-start.22) | collective-permute-done | bytes 1310752 | tf_op jit(solution)/shard_map/ppermute | solution.py:672
  195.0 15.0 %collective-permute-done.23.refs_5_ = bf16[320,1344]{1,0:T(8,128)(2,1)} collective-permute-done((bf16[320,1344]{1,0:T(8,128)(2,1)}, bf16[320,1344]{1,0:T(8,128)(2,1)}, u32[]{:S(2)}, u32[]{:S(2)}) %collective-permute-start.23) | collective-permute-done | bytes 860192 | tf_op jit(solution)/shard_map/ppermute | solution.py:672
  212.6 6.7 %reduce-scatter.4.cloned.1.call-done.more = bf16[64,2560]{1,0:T(8,128)(2,1)} async-done(((bf16[512,2560]{1,0:T(8,128)(2,1)}), bf16[64,2560]{1,0:T(8,128)(2,1)}) %reduce-scatter.4.cloned.1.call-update) | async-done | bytes 327696 | tf_op jit(solution)/shard_map/reduce_scatter | solution.py:726
  220.5 17.3 %collective-permute-start.25 = (bf16[64,2560]{1,0:T(8,128)(2,1)S(1)}, bf16[64,2560]{1,0:T(8,128)(2,1)S(1)}, u32[]{:S(2)}, u32[]{:S(2)}) collective-permute-start(bf16[64,2560]{1,0:T(8,128)(2,1)S(1)} %get-tuple-element.169), channel_id=1, source_target_pairs={{0,16},{1,17},{2,18},{3,19},{4,20},{5,21},{6,22},{7,23},{8,0},{9,1... | collective-permute-start | bytes 983048 | tf_op jit(solution)/shard_map/ppermute | solution.py:672
  264.4 10.4 %collective-permute-done.32 = bf16[128,2560]{1,0:T(8,128)(2,1)S(1)} collective-permute-done((bf16[128,2560]{1,0:T(8,128)(2,1)S(1)}, bf16[128,2560]{1,0:T(8,128)(2,1)S(1)}, u32[]{:S(2)}, u32[]{:S(2)}) %collective-permute-start.32) | collective-permute-done | bytes 655392 | tf_op jit(solution)/shard_map/ppermute | solution.py:672
  274.8 7.0 %collective-permute-done.34 = bf16[128,2560]{1,0:T(8,128)(2,1)S(1)} collective-permute-done((bf16[128,2560]{1,0:T(8,128)(2,1)S(1)}, bf16[128,2560]{1,0:T(8,128)(2,1)S(1)}, u32[]{:S(2)}, u32[]{:S(2)}) %collective-permute-start.34) | collective-permute-done | bytes 655392 | tf_op jit(solution)/shard_map/ppermute | solution.py:672
  285.0 16.3 %shard_map.212 = (f32[256,2560]{1,0:T(8,128)}, bf16[256,2560]{1,0:T(8,128)(2,1)S(1)}, f32[256,2560]{1,0:T(8,128)}, bf16[256,2560]{1,0:T(8,128)(2,1)S(1)}, bf16[5...) custom-call(s32[4]{0:T(128)S(1)} %pad_add_fusion.where, ...), custom_call_target="tpu_custom_call" | custom-call | flops 7046430720 | bytes 20971520 | tf_op jit(solution)/shard_map/pallas_call | solution.py:287
  308.8 15.4 %shard_map.214 = (f32[256,2560]{1,0:T(8,128)}, bf16[256,2560]{1,0:T(8,128)(2,1)S(1)}, f32[256,2560]{1,0:T(8,128)}, bf16[256,2560]{1,0:T(8,128)(2,1)S(1)}, bf16[5...) custom-call(s32[4]{0:T(128)S(1)} %pad_add_fusion.where, ...), custom_call_target="tpu_custom_call" | custom-call | flops 7046430720 | bytes 20971520 | tf_op jit(solution)/shard_map/pallas_call | solution.py:287
  336.4 16.0 %collective-permute-done.43.refs_0_ = bf16[320,1344]{1,0:T(8,128)(2,1)S(1)} collective-permute-done((bf16[320,1344]{1,0:T(8,128)(2,1)S(1)}, bf16[320,1344]{1,0:T(8,128)(2,1)S(1)}, u32[]{:S(2)}, u32[]{:S(2)}) %collective-permute-start.43) | collective-permute-done | bytes 860192 | tf_op jit(solution)/shard_map/ppermute | solution.py:672
  369.9 7.1 %collective-permute-done.44.refs_0_ = bf16[64,2560]{1,0:T(8,128)(2,1)S(1)} collective-permute-done((bf16[64,2560]{1,0:T(8,128)(2,1)S(1)}, bf16[64,2560]{1,0:T(8,128)(2,1)S(1)}, u32[]{:S(2)}, u32[]{:S(2)}) %collective-permute-start.44) | collective-permute-done | bytes 327712 | tf_op jit(solution)/shard_map/ppermute | solution.py:672
  386.1 29.7 %collective-permute-done.48 = bf16[320,1344]{1,0:T(8,128)(2,1)S(1)} collective-permute-done((bf16[320,1344]{1,0:T(8,128)(2,1)}, bf16[320,1344]{1,0:T(8,128)(2,1)S(1)}, u32[]{:S(2)}, u32[]{:S(2)}) %collective-permute-start.48) | collective-permute-done | bytes 860192 | tf_op jit(solution)/shard_map/ppermute | solution.py:672
  433.7 13.5 %collective-permute-done.49.refs_2_ = bf16[320,1344]{1,0:T(8,128)(2,1)S(1)} collective-permute-done((bf16[320,1344]{1,0:T(8,128)(2,1)S(1)}, bf16[320,1344]{1,0:T(8,128)(2,1)S(1)}, u32[]{:S(2)}, u32[]{:S(2)}) %collective-permute-start.49) | collective-permute-done | bytes 860192 | tf_op jit(solution)/shard_map/ppermute | solution.py:672
  461.2 9.1 %shard_map.225 = (bf16[512,320]{1,0:T(8,128)(2,1)S(1)}, f32[512,160]{1,0:T(8,128)S(1)}, f32[512,160]{1,0:T(8,128)S(1)}) custom-call(s32[4]{0:T(128)S(1)} %pad_add_fusion.where, s32[2]{0:T(128)S(1)} %copy-done.81, bf16[512,480]{1,0:T(8,128)(2,1)S(1)} %copy-done.59, bf16[512,160]{1,0:T(8,128)(2,1)S(1)} %copy-done.79, bf16[512,320]{1,0:T(8,128)(2,1)S(1)} %fusion.9.refs_1_, ...), custom_call_target="tpu_custom_call" | custom-call | flops 4294967296 | bytes 4194304 | tf_op jit(solution)/shard_map/pallas_call | solution.py:623
  470.7 12.3 %collective-permute-done.52 = f32[512,160]{1,0:T(8,128)S(1)} collective-permute-done((f32[512,160]{1,0:T(8,128)S(1)}, f32[512,160]{1,0:T(8,128)S(1)}, u32[]{:S(2)}, u32[]{:S(2)}) %collective-permute-start.52) | collective-permute-done | bytes 327712 | tf_op jit(solution)/shard_map/ppermute | solution.py:672
  505.3 26.8 %collective-permute-done.55.refs_3_ = bf16[320,1344]{1,0:T(8,128)(2,1)S(1)} collective-permute-done((bf16[320,1344]{1,0:T(8,128)(2,1)}, bf16[320,1344]{1,0:T(8,128)(2,1)S(1)}, u32[]{:S(2)}, u32[]{:S(2)}) %collective-permute-start.55) | collective-permute-done | bytes 860192 | tf_op jit(solution)/shard_map/ppermute | solution.py:672
  532.8 7.7 %reduce-scatter.8.cloned.1.call-done.refs_0_ = bf16[64,2560]{1,0:T(8,128)(2,1)} async-done(((bf16[512,2560]{1,0:T(8,128)(2,1)}), bf16[64,2560]{1,0:T(8,128)(2,1)}) %reduce-scatter.8.cloned.1.call-update) | async-done | bytes 327696 | tf_op jit(solution)/shard_map/reduce_scatter | solution.py:726
  556.5 16.4 %reduce-scatter.6.cloned.1.call-done = bf16[64,2560]{1,0:T(8,128)(2,1)} async-done(((bf16[256,2560]{1,0:T(8,128)(2,1)}), bf16[64,2560]{1,0:T(8,128)(2,1)}) %reduce-scatter.6.cloned.1.call-update) | async-done | bytes 327696 | tf_op jit(solution)/shard_map/reduce_scatter | solution.py:726
  588.2 8.6 %collective-permute-done.69 = bf16[160,480]{1,0:T(8,128)(2,1)S(1)} collective-permute-done((bf16[160,480]{1,0:T(8,128)(2,1)S(1)}, bf16[160,480]{1,0:T(8,128)(2,1)S(1)}, u32[]{:S(2)}, u32[]{:S(2)}) %collective-permute-start.69) | collective-permute-done | bytes 153632 | tf_op jit(solution)/shard_map/ppermute | solution.py:672
  599.2 8.2 %collective-permute-done.59.refs_1_ = bf16[64,2560]{1,0:T(8,128)(2,1)S(1)} collective-permute-done((bf16[64,2560]{1,0:T(8,128)(2,1)S(1)}, bf16[64,2560]{1,0:T(8,128)(2,1)S(1)}, u32[]{:S(2)}, u32[]{:S(2)}) %collective-permute-start.59) | collective-permute-done | bytes 327712 | tf_op jit(solution)/shard_map/ppermute | solution.py:672
  (451 shorter events, 293.1 us)
Async XLA Ops:
  7.2 63.6 %all-gather.12.cloned.1.call-start = ((), (), s32[]{:S(2)}) async-start(), calls=%async_computation.9 | async-start | bytes 1638400 | tf_op jit(solution)/shard_map/all_gather | solution.py:723
  19.5 102.9 %all-gather.6.cloned.1.call-start = ((), (), s32[]{:S(2)}) async-start(), calls=%async_computation.3 | async-start | bytes 2949120 | tf_op jit(solution)/shard_map/all_gather | solution.py:723
  29.9 189.3 %reduce-scatter.4.cloned.1.call-start = ((), (), s32[]{:S(2)}) async-start(), calls=%async_computation.4 | async-start | bytes 2949120 | tf_op jit(solution)/shard_map/reduce_scatter | solution.py:726
  82.4 36.9 %collective-permute-start.16 = (bf16[320,1344]{1,0:T(8,128)(2,1)}, bf16[320,1344]{1,0:T(8,128)(2,1)}, u32[]{:S(2)}, u32[]{:S(2)}) collective-permute-start(bf16[320,1344]{1,0:T(8,128)(2,1)} %copy-done.73), channel_id=1, source_target_pairs={{0,8},{1,9},{2,10},{3,11},{4,12},{5,13},{6,14},{7,15},{8,16},{9,17... | collective-permute-start | bytes 2580488 | tf_op jit(solution)/shard_map/ppermute | solution.py:672
  164.7 287.3 %all-gather.8.cloned.1.call-start = ((), (), s32[]{:S(2)}) async-start(), calls=%async_computation.5 | async-start | bytes 2949120 | tf_op jit(solution)/shard_map/all_gather | solution.py:723
  167.5 42.6 %collective-permute-start.23 = (bf16[320,1344]{1,0:T(8,128)(2,1)}, bf16[320,1344]{1,0:T(8,128)(2,1)}, u32[]{:S(2)}, u32[]{:S(2)}) collective-permute-start(bf16[320,1344]{1,0:T(8,128)(2,1)} %copy-done.70), channel_id=1, source_target_pairs={{0,8},{1,9},{2,10},{3,11},{4,12},{5,13},{6,14},{7,15},{8,16},{9,17... | collective-permute-start | bytes 2580488 | tf_op jit(solution)/shard_map/ppermute | solution.py:672
  167.5 42.6 %collective-permute-start.24 = (bf16[320,1344]{1,0:T(8,128)(2,1)}, bf16[320,1344]{1,0:T(8,128)(2,1)S(1)}, u32[]{:S(2)}, u32[]{:S(2)}) collective-permute-start(bf16[320,1344]{1,0:T(8,128)(2,1)} %collective-permute-done.17.refs_6_), channel_id=1, source_target_pairs={{0,4},{1,5},{2,6},{3,7},{4,0},{5,1},{6,2},{7,3},{8,12},{9,13},{10,... | collective-permute-start | bytes 2580488 | tf_op jit(solution)/shard_map/ppermute | solution.py:672
  167.9 69.9 %collective-permute-start.26 = (bf16[256,2560]{1,0:T(8,128)(2,1)S(1)}, bf16[256,2560]{1,0:T(8,128)(2,1)}, u32[]{:S(2)}, u32[]{:S(2)}) collective-permute-start(bf16[256,2560]{1,0:T(8,128)(2,1)S(1)} %bitcast.113), channel_id=1, source_target_pairs={{0,1},{1,0},{2,3},{3,2},{4,5},{5,4},{6,7},{7,6},{8,9},{9,8},{10,11... | collective-permute-start | bytes 3932168 | tf_op jit(solution)/shard_map/ppermute | solution.py:672
  195.0 42.8 %collective-permute-start.27 = (bf16[256,2560]{1,0:T(8,128)(2,1)}, bf16[256,2560]{1,0:T(8,128)(2,1)}, u32[]{:S(2)}, u32[]{:S(2)}) collective-permute-start(bf16[256,2560]{1,0:T(8,128)(2,1)} %collective-permute-done.22.refs_2_.refs_5_), channel_id=1, source_target_pairs={{0,1},{1,0},{2,3},{3,2},{4,5},{5,4},{6,7},{7,6},{8,9},{9,8},{10,11... | collective-permute-start | bytes 3932168 | tf_op jit(solution)/shard_map/ppermute | solution.py:672
  212.5 34.9 %collective-permute-start.30 = (bf16[320,1344]{1,0:T(8,128)(2,1)}, bf16[320,1344]{1,0:T(8,128)(2,1)}, u32[]{:S(2)}, u32[]{:S(2)}) collective-permute-start(bf16[320,1344]{1,0:T(8,128)(2,1)} %copy-done.69), channel_id=1, source_target_pairs={{0,24},{1,25},{2,26},{3,27},{4,28},{5,29},{6,30},{7,31},{8,0},{9,1... | collective-permute-start | bytes 2580488 | tf_op jit(solution)/shard_map/ppermute | solution.py:672
  379.1 161.4 %reduce-scatter.8.cloned.1.call-start = ((), (), s32[]{:S(2)}) async-start(), calls=%async_computation.7 | async-start | bytes 2949120 | tf_op jit(solution)/shard_map/reduce_scatter | solution.py:726
  379.3 36.5 %collective-permute-start.48 = (bf16[320,1344]{1,0:T(8,128)(2,1)}, bf16[320,1344]{1,0:T(8,128)(2,1)S(1)}, u32[]{:S(2)}, u32[]{:S(2)}) collective-permute-start(bf16[320,1344]{1,0:T(8,128)(2,1)} %copy-done.44), channel_id=1, source_target_pairs={{0,8},{1,9},{2,10},{3,11},{4,12},{5,13},{6,14},{7,15},{8,16},{9,17... | collective-permute-start | bytes 2580488 | tf_op jit(solution)/shard_map/ppermute | solution.py:672
  380.9 40.9 %collective-permute-start.50 = (bf16[320,1344]{1,0:T(8,128)(2,1)}, bf16[320,1344]{1,0:T(8,128)(2,1)S(1)}, u32[]{:S(2)}, u32[]{:S(2)}) collective-permute-start(bf16[320,1344]{1,0:T(8,128)(2,1)} %copy-done.75), channel_id=1, source_target_pairs={{0,4},{1,5},{2,6},{3,7},{4,0},{5,1},{6,2},{7,3},{8,12},{9,13},{10,... | collective-permute-start | bytes 2580488 | tf_op jit(solution)/shard_map/ppermute | solution.py:672
  384.6 66.4 %collective-permute-start.47 = (bf16[256,2560]{1,0:T(8,128)(2,1)S(1)}, bf16[256,2560]{1,0:T(8,128)(2,1)S(1)}, u32[]{:S(2)}, u32[]{:S(2)}) collective-permute-start(bf16[256,2560]{1,0:T(8,128)(2,1)S(1)} %shard_map.220), channel_id=1, source_target_pairs={{0,2},{1,3},{2,0},{3,1},{4,6},{5,7},{6,4},{7,5},{8,10},{9,11},{10,... | collective-permute-start | bytes 3932168 | tf_op jit(solution)/shard_map/ppermute | solution.py:672
  415.8 31.4 %collective-permute-start.49 = (bf16[320,1344]{1,0:T(8,128)(2,1)S(1)}, bf16[320,1344]{1,0:T(8,128)(2,1)S(1)}, u32[]{:S(2)}, u32[]{:S(2)}) collective-permute-start(bf16[320,1344]{1,0:T(8,128)(2,1)S(1)} %collective-permute-done.48), channel_id=1, source_target_pairs={{0,8},{1,9},{2,10},{3,11},{4,12},{5,13},{6,14},{7,15},{8,16},{9,17... | collective-permute-start | bytes 2580488 | tf_op jit(solution)/shard_map/ppermute | solution.py:672
  448.1 35.1 %collective-permute-start.53 = (bf16[320,1344]{1,0:T(8,128)(2,1)}, bf16[320,1344]{1,0:T(8,128)(2,1)}, u32[]{:S(2)}, u32[]{:S(2)}) collective-permute-start(bf16[320,1344]{1,0:T(8,128)(2,1)} %shard_map.226), channel_id=1, source_target_pairs={{0,8},{1,9},{2,10},{3,11},{4,12},{5,13},{6,14},{7,15},{8,16},{9,17... | collective-permute-start | bytes 2580488 | tf_op jit(solution)/shard_map/ppermute | solution.py:672
  449.3 34.0 %collective-permute-start.54 = (bf16[320,1344]{1,0:T(8,128)(2,1)}, bf16[320,1344]{1,0:T(8,128)(2,1)}, u32[]{:S(2)}, u32[]{:S(2)}) collective-permute-start(bf16[320,1344]{1,0:T(8,128)(2,1)} %get-tuple-element.225), channel_id=1, source_target_pairs={{0,4},{1,5},{2,6},{3,7},{4,0},{5,1},{6,2},{7,3},{8,12},{9,13},{10,... | collective-permute-start | bytes 2580488 | tf_op jit(solution)/shard_map/ppermute | solution.py:672
  487.2 85.7 %reduce-scatter.6.cloned.1.call-start = ((), (), s32[]{:S(2)}) async-start(), calls=%async_computation.6 | async-start | bytes 1638400 | tf_op jit(solution)/shard_map/reduce_scatter | solution.py:726
  489.4 42.7 %collective-permute-start.55 = (bf16[320,1344]{1,0:T(8,128)(2,1)}, bf16[320,1344]{1,0:T(8,128)(2,1)S(1)}, u32[]{:S(2)}, u32[]{:S(2)}) collective-permute-start(bf16[320,1344]{1,0:T(8,128)(2,1)} %shard_map.227), channel_id=1, source_target_pairs={{0,24},{1,25},{2,26},{3,27},{4,28},{5,29},{6,30},{7,31},{8,0},{9,1... | collective-permute-start | bytes 2580488 | tf_op jit(solution)/shard_map/ppermute | solution.py:672
  494.7 138.0 %all-gather.10.cloned.1.call-start = ((), (), s32[]{:S(2)}) async-start(), calls=%async_computation.8 | async-start | bytes 3276800 | tf_op jit(solution)/shard_map/all_gather | solution.py:723
  501.7 30.4 %collective-permute-start.56 = (bf16[4,160,480]{2,1,0:T(8,128)(2,1)}, bf16[4,160,480]{2,1,0:T(8,128)(2,1)}, u32[]{:S(2)}, u32[]{:S(2)}) collective-permute-start(bf16[4,160,480]{2,1,0:T(8,128)(2,1)} %get-tuple-element.229), channel_id=1, source_target_pairs={{0,4},{1,5},{2,6},{3,7},{4,0},{5,1},{6,2},{7,3},{8,12},{9,13},{10,... | collective-permute-start | bytes 1843208 | tf_op jit(solution)/shard_map/ppermute | solution.py:672
  547.6 50.9 %collective-permute-start.74 = (bf16[4,160,320]{2,1,0:T(8,128)(2,1)}, bf16[4,160,320]{2,1,0:T(8,128)(2,1)}, u32[]{:S(2)}, u32[]{:S(2)}) collective-permute-start(bf16[4,160,320]{2,1,0:T(8,128)(2,1)} %get-tuple-element.248), channel_id=1, source_target_pairs={{0,6},{1,7},{2,4},{3,5},{4,2},{5,3},{6,0},{7,1},{8,14},{9,15},{10,... | collective-permute-start | bytes 1228808 | tf_op jit(solution)/shard_map/ppermute | solution.py:672
  548.1 59.3 %collective-permute-start.73 = (bf16[4,160,320]{2,1,0:T(8,128)(2,1)}, bf16[4,160,320]{2,1,0:T(8,128)(2,1)}, u32[]{:S(2)}, u32[]{:S(2)}) collective-permute-start(bf16[4,160,320]{2,1,0:T(8,128)(2,1)} %get-tuple-element.246), channel_id=1, source_target_pairs={{0,2},{1,3},{2,0},{3,1},{4,6},{5,7},{6,4},{7,5},{8,10},{9,11},{10,... | collective-permute-start | bytes 1228808 | tf_op jit(solution)/shard_map/ppermute | solution.py:672
  598.2 32.3 %collective-permute-start.60 = (bf16[64,2560]{1,0:T(8,128)(2,1)S(1)}, bf16[64,2560]{1,0:T(8,128)(2,1)S(1)}, u32[]{:S(2)}, u32[]{:S(2)}) collective-permute-start(bf16[64,2560]{1,0:T(8,128)(2,1)S(1)} %copy-done.54), channel_id=1, source_target_pairs={{0,1},{1,0},{2,3},{3,2},{4,5},{5,4},{6,7},{7,6},{8,9},{9,8},{10,11... | collective-permute-start | bytes 983048 | tf_op jit(solution)/shard_map/ppermute | solution.py:672
  (150 other events, 2419.7 us)
Sparse Core Ops, SparseCore 0:
  19.6 44.8 all-gather.11
  66.7 55.6 all-gather.5
  164.9 54.3 reduce-scatter.3
  379.3 47.9 all-gather.7
  487.3 53.1 reduce-scatter.7
  543.2 29.5 reduce-scatter.5
  575.0 24.7 all-gather.9

commit v3 on v2

--- a/solution.py
+++ b/solution.py
@@ -353,6 +353,98 @@
         out_specs=[whole_vmem()] * 3,
         compiler_params=pltpu.CompilerParams(vmem_limit_bytes=32 * 2**20),
     )(*parts, values, beside, gain)
+
+
+def order_kernel(Z, C, order, where, *refs):
+    pieces, out = refs[:-1], refs[-1]
+    own = out.shape[0] // (Z * C)
+    z, c = where[0], where[3]
+    ring = sum(jnp.where(z == value, place, 0) for place, value in enumerate(order))
+    for s in range(Z):
+        ranked = lax.rem(ring - s + Z, Z)
+        at = sum(jnp.where(ranked == place, value, 0) for place, value in enumerate(order))
+        for h in range(C):
+            spot = pl.multiple_of((at * C + lax.rem(c - h + C, C)) * own, own)
+            out[pl.ds(spot, own), :] = pieces[h][s * own : (s + 1) * own, :]
+
+
+def order_tokens(grid, pieces):
+    tokens, width = pieces[0].shape
+    return pl.pallas_call(
+        functools.partial(order_kernel, grid.Z, grid.C, tuple(grid.order)),
+        out_shape=jax.ShapeDtypeStruct((grid.C * tokens, width), BF16),
+        in_specs=[pl.BlockSpec(memory_space=pltpu.SMEM)] + [whole_vmem()] * grid.C,
+        out_specs=whole_vmem(),
+        compiler_params=pltpu.CompilerParams(vmem_limit_bytes=24 * 2**20),
+    )(grid.where, *pieces)
+
+
+def unit_sum_kernel(number, *refs):
+    units, outs = refs[:number], refs[number:]
+    for k, out in enumerate(outs):
+        total = units[0][k].astype(F32)
+        for unit in units[1:]:
+            total = total + unit[k].astype(F32)
+        out[...] = total.astype(BF16)
+
+
+def unit_sum(units):
+    Z, part, n = units[0].shape
+    return pl.pallas_call(
+        functools.partial(unit_sum_kernel, len(units)),
+        out_shape=[jax.ShapeDtypeStruct((part, n), BF16)] * Z,
+        in_specs=[whole_vmem()] * len(units),
+        out_specs=[whole_vmem()] * Z,
+        compiler_params=pltpu.CompilerParams(vmem_limit_bytes=24 * 2**20),
+    )(*units)
+
+
+def sort_kernel(Z, U, Y, where, *refs):
+    parts, outs = refs[:Z], refs[Z:]
+    z, y = where[0], where[2]
+    for k in range(Z):
+        source = lax.rem(z - k + Z, Z)
+        ahead = lax.rem(lax.div(source, U) - y + Y, Y)
+        for r in range(Y):
+
+            @pl.when(ahead == r)
+            def _(k=k, r=r, source=source):
+                outs[r][lax.rem(source, U)] = parts[k][...]
+
+
+def sort_heads(grid, parts):
+    half, n = parts[0].shape
+    return pl.pallas_call(
+        functools.partial(sort_kernel, grid.Z, grid.U, grid.Y),
+        out_shape=[jax.ShapeDtypeStruct((grid.U, half, n), BF16)] * grid.Y,
+        in_specs=[pl.BlockSpec(memory_space=pltpu.SMEM)] + [whole_vmem()] * grid.Z,
+        out_specs=[whole_vmem()] * grid.Y,
+        compiler_params=pltpu.CompilerParams(vmem_limit_bytes=24 * 2**20),
+    )(grid.where, *parts)
+
+
+def join_kernel(U, Y, sizes, where, *refs):
+    parts, outs = refs[:Y], refs[Y:]
+    half = parts[0].shape[1]
+    for r in range(Y):
+        at = pl.multiple_of(lax.rem(where[2] - r + Y, Y) * half, 8)
+        for u in range(U):
+            first = 0
+            for out, size in zip(outs, sizes):
+                columns = parts[r][u, :, first : first + size].astype(F32)
+                out[pl.ds(at, half), u * size : (u + 1) * size] = columns
+                first += size
+
+
+def join_heads(grid, parts, sizes):
+    U, half, _ = parts[0].shape
+    return pl.pallas_call(
+        functools.partial(join_kernel, U, grid.Y, sizes),
+        out_shape=[jax.ShapeDtypeStruct((grid.Y * half, U * size), F32) for size in sizes],
+        in_specs=[pl.BlockSpec(memory_space=pltpu.SMEM)] + [whole_vmem()] * grid.Y,
+        out_specs=[whole_vmem()] * len(sizes),
+        compiler_params=pltpu.CompilerParams(vmem_limit_bytes=24 * 2**20),
+    )(grid.where, *parts)
 
 
 def place_kernel(Y, C, where, *refs):
@@ -581,8 +673,8 @@
         query_grad[at, :] = jnp.concatenate(outs, 1)
     for i, out in enumerate(kv_grads):
         at = slice(i * tokens, (i + 1) * tokens)
-        out[:, :HEAD_DIM] = key_sum[at, :] * scale
-        out[:, HEAD_DIM:] = value_sum[at, :]
+        out[:, :HEAD_DIM] = (key_sum[at, :] * scale).astype(out.dtype)
+        out[:, HEAD_DIM:] = value_sum[at, :].astype(out.dtype)
 
 
 def query_tile(tokens, keys):
@@ -623,7 +715,8 @@
     return pl.pallas_call(
         functools.partial(attend_back_kernel, grid.X, rows, group, query_tile(tokens, keys)),
         out_shape=[jax.ShapeDtypeStruct((tokens, group * HEAD_DIM), BF16)]
-        + [jax.ShapeDtypeStruct((tokens, 2 * HEAD_DIM), F32)] * grid.X,
+        + [jax.ShapeDtypeStruct((tokens, 2 * HEAD_DIM), F32)]
+        + [jax.ShapeDtypeStruct((tokens, 2 * HEAD_DIM), BF16)] * (grid.X - 1),
         in_specs=[smem, smem] + [whole_vmem()] * (grid.X + 2),
         out_specs=[whole_vmem()] * (1 + grid.X),
         scratch_shapes=[
@@ -779,24 +872,10 @@
             for i, unit in enumerate(units)
         ]
 
-    def sum_xy(self, arrived):
-        sums = []
-        for k in range(self.Z):
-            total = arrived[0][k].astype(F32)
-            for unit in arrived[1:]:
-                total = total + unit[k].astype(F32)
-            sums.append(total.astype(BF16))
-        return sums
-
-    def return_heads(self, units):
-        parts = jnp.stack(self.exchange_z(self.sum_xy(units)), 0)
-        parts = jnp.stack([pick(parts, (self.z - s) % self.Z) for s in range(self.Z)], 0)
-        parts = parts.reshape((self.Y, self.U) + parts.shape[1:])
-        halves = [pick(parts, self.y)]
-        for k in range(1, self.Y):
-            halves.append(self.to_y(pick(parts, (self.y + k) % self.Y), k))
-        rows = place(halves, [(self.y - k) % self.Y for k in range(self.Y)])
-        return [rows[:, u].reshape(-1, rows.shape[3]) for u in range(self.U)]
+    def return_heads(self, parts, sizes):
+        sorted_parts = sort_heads(self, parts)
+        arrived = [sorted_parts[0]] + [self.to_y(sorted_parts[r], r) for r in range(1, self.Y)]
+        return join_heads(self, arrived, sizes)
 
     def from_z(self, k):
         return (self.z - k) % self.Z
@@ -811,7 +890,7 @@
         whole = place(parts, [self.from_z(k) for k in range(self.Z)])
         return whole.transpose(2, 0, 1, 3).reshape(gains.shape[0], -1)
 
-    def sum_gains(self, terms):
+    def sum_gains(self, terms, hold):
         number = terms.shape[0]
         part = terms
         for k in range(1, self.C):
@@ -819,6 +898,7 @@
         terms = part
         for k in range(1, self.Y):
             part = part + self.to_y(terms, k)
+        part = after(part, *hold)
         part = part.reshape(number, self.Z, self.X, -1).transpose(2, 1, 0, 3)
         out = pick(part, self.x)
         for k in range(1, self.X):
@@ -855,18 +935,17 @@
     others = range(1, grid.X)
     middle = grid.Z // 2
     ends = [k for k in range(1, grid.Z) if k != middle]
-    near = pack_heads(grid, [w_query, w_key, w_value])
+    cot_own = own_rows(cotangent)
+    cot_all = grid.gather(cot_own, "z")
+    near = pack_heads(grid, [after(w_query, cot_own), w_key, w_value])
     near_own = near[0]
     near = [near_own] + [grid.to_y(near[k], k) for k in range(1, grid.Y)]
-    gains = grid.gather_gains(jnp.stack([gain_attn, gain_mlp], 0))
-    cot_own = own_rows(cotangent)
-    cot_all = grid.gather(cot_own, "z")
+    gains = grid.gather_gains(jnp.stack([after(gain_attn, cot_own), gain_mlp], 0))
     flat = own_rows(inputs)
     gain_one, gain_two = gains[0:1].astype(F32), gains[1:2].astype(F32)
     values = flat.astype(F32)
     recip = lax.rsqrt(jnp.mean(values * values, -1, keepdims=True) + EPSILON)
     attn_own = after((values * recip * gain_one).astype(BF16), *near)
-    attn_in = grid.gather(attn_own, "zc")
     qkv_parts = grid.exchange_z(route_heads(grid, near))
 
     packed = pack_hidden(grid, after(w_gate, attn_own), w_up, w_down.T)
@@ -876,38 +955,50 @@
     def ring_on(blocks, *hold):
         return blocks + [grid.along_ring(after(blocks[-1], *hold), 1)]
 
-    qkv_units = grid.spread_xy(after(jnp.stack(qkv_parts, 0), cot_all, *out_near))
+    blocks = ring_on([attn_own])
+    blocks = ring_on(blocks, *packed[:1])
+    blocks = ring_on(blocks, *qkv_parts, *[cot_all])
+    for _ in range(grid.Z - 4):
+        blocks = ring_on(blocks)
+    qkv_units = grid.spread_xy(jnp.stack(qkv_parts, 0))
     out_parts = route_heads(grid, [after(part, *qkv_parts) for part in out_near])
     out_parts = grid.exchange_z(out_parts)
-    arrived, first = {0: packed[0]}, out_parts[1:]
-    for k in [middle] + ends:
-        arrived[k] = grid.hop_z(after(packed[k], *first), k)
-        first = [arrived[k]]
-    w_qkv = assemble(grid, [after(u, *out_parts[1:]) for u in qkv_units])[:, : q_cols + 2 * HEAD_DIM]
+    mine = after(jnp.concatenate(blocks, 0), *qkv_units[1:], *out_parts[1:])
+    attn_in = order_tokens(grid, [mine] + [grid.to_c(mine, k) for k in range(1, grid.C)])
+
+    w_qkv = assemble(grid, qkv_units)
+    w_qkv = w_qkv[:, : q_cols + 2 * HEAD_DIM]
     qkv = dot(attn_in, w_qkv).astype(BF16)
     tokens = qkv.shape[0]
     kv_own = qkv[:, q_cols:]
     kv_others = [grid.to_x(kv_own, k) for k in others]
-    heads, stats = attend(grid, rows, group, prefix, qkv, kv_others)
-    moved_x, first = {}, qkv_units[1:]
+    out_units = grid.spread_xy(after(jnp.stack(out_parts, 0), *qkv_units[1:]))
+    w_o = assemble(grid, out_units)[:, :q_cols]
+    arrived, first, hop = {0: packed[0]}, out_parts[1:], []
+    for k in [middle] + ends:
+        part = after(packed[k], *first)
+        if k == middle and middle > 1:
+            hop = [grid.to_z(part, 1)]
+            arrived[k] = grid.to_z(after(hop[0], *out_units[1:]), middle - 1)
+        else:
+            arrived[k] = grid.to_z(part, k)
+        first = [arrived[k]]
+    ready = after(qkv, *out_units[1:], *hop)
+    heads, stats = attend(grid, rows, group, prefix, ready, kv_others)
+    moved_x, first = {}, out_units[1:]
     for k in [0, middle] + ends:
         moved_x[k] = [grid.to_x(after(arrived[k], *first), x) for x in others]
         first = moved_x[k]
-        if k == 0:
-            out_unit = after(jnp.stack(out_parts, 0), *kv_others, *first)
-            out_units = grid.spread_xy(out_unit)
-            w_o = assemble(grid, out_units)[:, :q_cols]
-            first = out_units[1:]
     mlp_grad = grid.spread_yc(after(cot_all, *out_units[1:]))
-    attn_partial = contract_last(after(heads, arrived[middle]), w_o).astype(BF16)
+    attn_partial = contract_last(after(heads, *[arrived[middle]]), w_o).astype(BF16)
     attn_out = grid.scatter(attn_partial, "zc")
-    held = mlp_grad[: grid.Y] + [arrived[ends[0]]] + moved_x[middle]
+    held = list(mlp_grad[: grid.Y]) + list([arrived[ends[0]]]) + list(moved_x[middle])
     hidden, mlp_own = add_norm(flat, after(attn_out, *held), gain_two)
     mlp_blocks = ring_on([mlp_own])
-    mlp_blocks = ring_on(mlp_blocks, *mlp_grad, *moved_x[ends[0]])
+    mlp_blocks = ring_on(mlp_blocks)
     for _ in range(grid.Z - 3):
-        mlp_blocks = ring_on(mlp_blocks, arrived[ends[-1]])
-    mlp_in = grid.gather_wide(mlp_blocks, moved_x[ends[-1]])
+        mlp_blocks = ring_on(mlp_blocks, *[arrived[ends[-1]]])
+    mlp_in = grid.gather_wide(mlp_blocks, list(moved_x[ends[-1]]))
     units = [arrived[k] for k in range(grid.Z)]
     units = units + [moved_x[k][x - 1] for x in others for k in range(grid.Z)]
 
@@ -938,7 +1029,9 @@
         first = swapped[-1] if swapped else []
         swapped.append([grid.to_x(after(parts[xr], *first), xr) for xr in others])
         holds.append(parts)
-        hidden_parts[k] = core_sum(parts[0], swapped[-1], BF16, 1)[0]
+    for at, k in enumerate(order):
+        late = list(holds[1]) + list(holds[2]) if at == 0 else []
+        hidden_parts[k] = core_sum(after(holds[at][0], *late), swapped[at], BF16, 1)[0]
     for sent in in_moved:
         in_first = in_first + sent[0].astype(F32)
     in_late = after(in_late, in_first)
@@ -948,66 +1041,111 @@
         (in_late, in_first)[2 * s // grid.Z][s % (grid.Z // 2) * own :][:own]
         for s in range(grid.Z)
     ]
-    holds, last = [[], holds[1], holds[2] + [hidden_parts[middle]]], holds[3]
+    last = holds[3]
+    holds = [
+        [],
+        list(holds[1]),
+        list(holds[2]) + list([hidden_parts[middle]]),
+    ]
     in_parts = grid.ring_sum(slots, holds)
+    arrived, first, hop = list(hidden_parts), [], None
+    for k in order[:-1]:
+        part = after(hidden_parts[k], *first)
+        if k == middle and middle > 1:
+            hop = grid.to_z(part, 1)
+            arrived[k] = grid.to_z(hop, middle - 1)
+        else:
+            arrived[k] = grid.to_z(part, k)
+        first = [arrived[k]]
+    held = list(swapped[1]) + list(swapped[2]) + list([arrived[middle]])
+    held = held
+    in_parts = (after(in_parts[0], *held), in_parts[1])
     hidden_grad, hidden_low, gain_two_term = norm_back(in_parts, hidden, cot_own, gain_two)
-    attn_grad = grid.gather(hidden_low, "zc")
-    out_y = []
+    out_y, out_sent, moved_out = [], [], [None] * grid.Y
     for yr in range(grid.Y - 1, -1, -1):
         low = after(layers[yr][3], in_parts[0])
-        moved = [grid.to_c(low[(h - 1) * each : h * each], -h) for h in range(1, grid.C)]
+        moved_out[yr] = [grid.to_c(low[(h - 1) * each : h * each], -h) for h in range(1, grid.C)]
         if yr > 0:
-            out_sum = core_sum(layers[yr][2], moved, BF16, 1)[0]
-            out_y.append(grid.to_y(out_sum, -yr))
-    arrived, first = list(hidden_parts), []
-    for k in order[:-1]:
-        arrived[k] = grid.hop_z(after(hidden_parts[k], *first), k)
-        first = [arrived[k]]
-    attn_grad = after(attn_grad, arrived[middle], *last, *swapped[2], *out_y)
-    out_sum = core_sum(layers[0][2], moved + out_y, BF16, 1)[0]
-    mlp_out = grid.scatter(after(out_sum, attn_grad), "z")
+            out_sent.append(core_sum(layers[yr][2], moved_out[yr], BF16, 1)[0])
+            out_y.append(grid.to_y(out_sent[-1], -yr))
+    blocks = ring_on([hidden_low])
+    blocks = ring_on(blocks, *out_sent, *moved_out[0])
+    for _ in range(grid.Z - 3):
+        held = list(last) + list(swapped[3])
+        held = held
+        blocks = ring_on(blocks, *held)
+    mine = jnp.concatenate(blocks, 0)
+    pieces = [mine] + [grid.to_c(mine, k) for k in range(1, grid.C)]
+    held = []
+    pieces[-1] = after(pieces[-1], *held)
+    attn_grad = order_tokens(grid, pieces)
+    out_sum = core_sum(layers[0][2], moved_out[0] + out_y, BF16, 1)[0]
+    mlp_out = grid.scatter(after(out_sum, *[attn_grad]), "z")
     heads_grad = dot(attn_grad, w_o).astype(BF16)
     out_units = weight_grad(grid, attn_grad, heads)
 
-    heads_grad = after(heads_grad, *out_units)
+    held = list(out_units) + [out_sum]
+    heads_grad = after(heads_grad, *held)
     query_grad, *kv_parts = attend_back(
         grid, rows, group, prefix, qkv, kv_others, heads_grad, stats
     )
     kv_moved = [grid.to_x(kv_parts[k], -k) for k in others]
-    kv_grad = kv_parts[0]
+    out_moved = grid.send_xy(out_units)
+    held = list(out_moved[1:]) + list([arrived[order[2]]])
+    held = held
+    kv_grad = after(kv_parts[0], *held)
     for part in kv_moved:
-        kv_grad = kv_grad + part
+        kv_grad = kv_grad + part.astype(F32)
     qkv_grad = jnp.concatenate(
         [query_grad, kv_grad.astype(BF16)], 1
     )
-    qkv_grad = after(qkv_grad, arrived[order[1]], *swapped[3])
-    attn_in_grad = grid.scatter(contract_last(qkv_grad, w_qkv).astype(BF16), "zc")
-    qkv_moved = grid.send_xy(weight_grad(grid, attn_in, qkv_grad))
-    out_moved = grid.send_xy([after(unit, *qkv_moved[1:]) for unit in out_units])
-    ready = after(attn_in_grad, arrived[order[2]], *qkv_moved[1:])
+
+    def spread_y(value):
+        return [value] + [grid.to_y(value, k) for k in range(1, grid.Y)]
+
+    def spread_c(ys):
+        cs = [grid.to_c(part, k) for k in range(1, grid.C) for part in ys]
+        return place_rows(grid, ys + cs)
+
+    qkv_units = weight_grad(grid, attn_in, qkv_grad)
+    qkv_moved = grid.send_xy(qkv_units)
+    out_sums = unit_sum([after(unit) for unit in out_moved])
+    out_parts = grid.exchange_z(out_sums)
+    held = list(qkv_units) + list(out_parts[1:]) + list([arrived[order[2]]])
+    held = held
+    partial = contract_last(after(qkv_grad, *held), w_qkv).astype(BF16)
+    attn_in_grad = grid.scatter(partial, "zc")
+    gate_wgrad, up_wgrad, down_wgrad = unpack_hidden(
+        grid, [after(part, *[partial]) for part in arrived]
+    )
+    out_wgrad = grid.return_heads(out_parts, (q_cols,))[0]
+    result_low = (hidden + after(mlp_out, *[partial]).astype(F32)).astype(BF16)
+    result = spread_c(spread_y(result_low))
+    held = [gate_wgrad]
+    held = held
+    qkv_sums = unit_sum([after(unit, *held) for unit in qkv_moved])
+    qkv_parts = grid.exchange_z(qkv_sums)
+    qkv_wgrad = grid.return_heads(qkv_parts, (q_cols, HEAD_DIM, HEAD_DIM))
+    held = list(qkv_sums) + [out_wgrad] + list(qkv_wgrad)
+    held = held
+    ready = after(attn_in_grad, *held)
     _, input_low, gain_one_term = norm_back([ready], flat, hidden_grad, gain_one)
-    rows_y = [input_low] + [grid.to_y(input_low, k) for k in range(1, grid.Y)]
-    rows_c = [grid.to_c(part, k) for k in range(1, grid.C) for part in rows_y]
-    input_grad = place_rows(grid, rows_y + rows_c)
-    gain_sum = grid.sum_gains(jnp.concatenate([gain_one_term, gain_two_term], 0))
-
-    out_wgrad = grid.return_heads([after(unit, *rows_y[1:]) for unit in out_moved])
-    qkv_wgrad = grid.return_heads([after(unit, input_low) for unit in qkv_moved])
-    gate_wgrad, up_wgrad, down_wgrad = unpack_hidden(
-        grid, [after(a, *qkv_moved[1:]) for a in arrived]
+    input_ys = spread_y(input_low)
+    input_grad = spread_c(input_ys)
+    gain_sum = grid.sum_gains(
+        jnp.concatenate([gain_one_term, gain_two_term], 0),
+        [],
     )
     down_wgrad = down_wgrad.T
-    result = hidden + mlp_out.astype(F32)
-    result = grid.gather(after(result, attn_in_grad), "yc").reshape(seqs, rows, width)
 
     return (
         result,
         input_grad,
         gain_sum[0],
-        jnp.concatenate([w[:, :q_cols] for w in qkv_wgrad], 1).astype(F32),
-        jnp.concatenate([w[:, q_cols : q_cols + HEAD_DIM] for w in qkv_wgrad], 1).astype(F32),
-        jnp.concatenate([w[:, q_cols + HEAD_DIM :] for w in qkv_wgrad], 1).astype(F32),
-        jnp.concatenate(out_wgrad, 1).T.astype(F32),
+        qkv_wgrad[0],
+        qkv_wgrad[1],
+        qkv_wgrad[2],
+        out_wgrad.T,
         gain_sum[1],
         gate_wgrad,
         up_wgrad,

time: 649 us -> 623 us (0.960)
  waiting for transfers between devices: 325 us -> 353 us
  local copies, waits for them, and re-layouts: 47.6 us -> 22.8 us
  starting transfers between devices: 131 us -> 116 us
  other arithmetic: 12.2 us -> 3.56 us
    ppermute x79 -> x90, waiting for transfers between devices: 294 us -> 340 us  [move(): return lax.ppermute(value, AXES, pairs)]
    unnamed x189 -> x143, local copies, waits for them, and re-layouts: 41.6 us -> 19.1 us
    reduce_scatter x3, waiting for transfers between devices: 30.8 us -> 12.1 us  [scatter(): lax.psum_scatter(partial, AXES, scatter_dimension=0, tiled=True, axis_ind...]
    ppermute x79 -> x90, starting transfers between devices: 131 us -> 116 us  [move(): return lax.ppermute(value, AXES, pairs)]
    pallas_call x0 -> x8, Pallas kernels: none -> 8.14 us  [the longest x2 3.22 us: join_heads(): pl.pallas_call(functools.partial(join_kernel, U, grid.Y, sizes), out_shap...]
  transfers between devices with their start and end apart: 86 -> 94, of which waited for: 39 -> 46; matrix products, arithmetic and copies ran while one was open for 4% -> 2% of each run, Pallas kernels for 12% -> 15%
where the time goes in v3:
time: 623 us; the launch traced here: 617 us
  waiting for transfers between devices  353 us (57%)
  starting transfers between devices  116 us (19%)
  Pallas kernels  96.9 us (16%)
  local copies, waits for them, and re-layouts  22.8 us (4%)
  between operations  15.5 us (2%)
  matrix products  9.14 us (1%)
    ppermute x90, waiting for transfers between devices, move(): return lax.ppermute(value, AXES, pairs)  340 us
    ppermute x90, starting transfers between devices, move(): return lax.ppermute(value, AXES, pairs)  116 us
    pallas_call x2, Pallas kernels, hidden_layer(): pl.pallas_call(functools.partial(hidden_kernel, Z, X, C, tuple(grid.order...  29.5 us
    unnamed x143, local copies, waits for them, and re-layouts  19.1 us
    pallas_call x4, Pallas kernels, hidden_weight_grad(): pl.pallas_call(functools.partial(hidden_weight_kernel, X, tiles), out_sha...  13.5 us
  transfers between devices with their start and end apart: 94, of which 46 were waited for; matrix products, arithmetic and copies ran while one was open for 2% of the time, Pallas kernels for 15%

profile of v3, /device:TPU:0, one launch (start us, length us, event | category | flops | bytes accessed | tf_op | source)
XLA Modules:
  0.0 616.7 jit_solution(13760345477165311743)
XLA Ops:
  37.1 13.9 %collective-permute-done.5 = bf16[64,2560]{1,0:T(8,128)(2,1)S(1)} collective-permute-done((bf16[64,2560]{1,0:T(8,128)(2,1)S(1)}, bf16[64,2560]{1,0:T(8,128)(2,1)S(1)}, u32[]{:S(2)}, u32[]{:S(2)}) %collective-permute-start.5) | collective-permute-done | bytes 327712 | tf_op jit(solution)/shard_map/ppermute | solution.py:765
  80.1 8.2 %collective-permute-done.15 = bf16[160,384]{1,0:T(8,128)(2,1)S(1)} collective-permute-done((bf16[160,384]{1,0:T(8,128)(2,1)S(1)}, bf16[160,384]{1,0:T(8,128)(2,1)S(1)}, u32[]{:S(2)}, u32[]{:S(2)}) %collective-permute-start.15) | collective-permute-done | bytes 122912 | tf_op jit(solution)/shard_map/ppermute | solution.py:765
  95.8 10.4 %collective-permute-done.12.refs_2_ = bf16[4,160,512]{2,1,0:T(8,128)(2,1)S(1)} collective-permute-done((bf16[4,160,512]{2,1,0:T(8,128)(2,1)S(1)}, bf16[4,160,512]{2,1,0:T(8,128)(2,1)S(1)}, u32[]{:S(2)}, u32[]{:S(2)}) %collective-permute-start.12) | collective-permute-done | bytes 655392 | tf_op jit(solution)/shard_map/ppermute | solution.py:765
  111.3 19.2 %collective-permute-done.22 = bf16[320,1344]{1,0:T(8,128)(2,1)S(1)} collective-permute-done((bf16[320,1344]{1,0:T(8,128)(2,1)S(1)}, bf16[320,1344]{1,0:T(8,128)(2,1)S(1)}, u32[]{:S(2)}, u32[]{:S(2)}) %collective-permute-start.22) | collective-permute-done | bytes 860192 | tf_op jit(solution)/shard_map/ppermute | solution.py:765
  162.2 19.3 %collective-permute-done.27.refs_8_ = bf16[320,1344]{1,0:T(8,128)(2,1)S(1)} collective-permute-done((bf16[320,1344]{1,0:T(8,128)(2,1)}, bf16[320,1344]{1,0:T(8,128)(2,1)S(1)}, u32[]{:S(2)}, u32[]{:S(2)}) %collective-permute-start.27) | collective-permute-done | bytes 860192 | tf_op jit(solution)/shard_map/ppermute | solution.py:765
  183.1 22.9 %collective-permute-done.26.refs_5_ = bf16[320,1344]{1,0:T(8,128)(2,1)} collective-permute-done((bf16[320,1344]{1,0:T(8,128)(2,1)}, bf16[320,1344]{1,0:T(8,128)(2,1)}, u32[]{:S(2)}, u32[]{:S(2)}) %collective-permute-start.26) | collective-permute-done | bytes 860192 | tf_op jit(solution)/shard_map/ppermute | solution.py:765
  208.4 8.5 %reduce-scatter.4.cloned.1.call-done.more = bf16[64,2560]{1,0:T(8,128)(2,1)} async-done(((bf16[512,2560]{1,0:T(8,128)(2,1)}), bf16[64,2560]{1,0:T(8,128)(2,1)}) %reduce-scatter.4.cloned.1.call-update) | async-done | bytes 327696 | tf_op jit(solution)/shard_map/reduce_scatter | solution.py:819
  218.0 16.4 %collective-permute-start.29 = (bf16[64,2560]{1,0:T(8,128)(2,1)S(1)}, bf16[64,2560]{1,0:T(8,128)(2,1)S(1)}, u32[]{:S(2)}, u32[]{:S(2)}) collective-permute-start(bf16[64,2560]{1,0:T(8,128)(2,1)S(1)} %get-tuple-element.183), channel_id=1, source_target_pairs={{0,16},{1,17},{2,18},{3,19},{4,20},{5,21},{6,22},{7,23},{8,0},{9,1... | collective-permute-start | bytes 983048 | tf_op jit(solution)/shard_map/ppermute | solution.py:765
  260.9 10.9 %collective-permute-done.33 = bf16[128,2560]{1,0:T(8,128)(2,1)S(1)} collective-permute-done((bf16[128,2560]{1,0:T(8,128)(2,1)S(1)}, bf16[128,2560]{1,0:T(8,128)(2,1)S(1)}, u32[]{:S(2)}, u32[]{:S(2)}) %collective-permute-start.33) | collective-permute-done | bytes 655392 | tf_op jit(solution)/shard_map/ppermute | solution.py:765
  271.8 7.0 %collective-permute-done.36 = bf16[128,2560]{1,0:T(8,128)(2,1)S(1)} collective-permute-done((bf16[128,2560]{1,0:T(8,128)(2,1)S(1)}, bf16[128,2560]{1,0:T(8,128)(2,1)S(1)}, u32[]{:S(2)}, u32[]{:S(2)}) %collective-permute-start.36) | collective-permute-done | bytes 655392 | tf_op jit(solution)/shard_map/ppermute | solution.py:765
  282.0 14.7 %shard_map.213 = (f32[256,2560]{1,0:T(8,128)}, bf16[256,2560]{1,0:T(8,128)(2,1)S(1)}, f32[256,2560]{1,0:T(8,128)}, bf16[256,2560]{1,0:T(8,128)(2,1)S(1)}, bf16[5...) custom-call(s32[4]{0:T(128)S(1)} %pad_add_fusion.where, ...), custom_call_target="tpu_custom_call" | custom-call | flops 7046430720 | bytes 20971520 | tf_op jit(solution)/shard_map/pallas_call | solution.py:287
  303.3 14.8 %shard_map.215 = (f32[256,2560]{1,0:T(8,128)}, bf16[256,2560]{1,0:T(8,128)(2,1)S(1)}, f32[256,2560]{1,0:T(8,128)}, bf16[256,2560]{1,0:T(8,128)(2,1)S(1)}, bf16[5...) custom-call(s32[4]{0:T(128)S(1)} %pad_add_fusion.where, ...), custom_call_target="tpu_custom_call" | custom-call | flops 7046430720 | bytes 20971520 | tf_op jit(solution)/shard_map/pallas_call | solution.py:287
  334.1 11.5 %collective-permute-done.47.refs_0_ = bf16[320,1344]{1,0:T(8,128)(2,1)S(1)} collective-permute-done((bf16[320,1344]{1,0:T(8,128)(2,1)S(1)}, bf16[320,1344]{1,0:T(8,128)(2,1)S(1)}, u32[]{:S(2)}, u32[]{:S(2)}) %collective-permute-start.47) | collective-permute-done | bytes 860192 | tf_op jit(solution)/shard_map/ppermute | solution.py:765
  349.3 18.0 %collective-permute-done.49.refs_0_ = bf16[320,1344]{1,0:T(8,128)(2,1)S(1)} collective-permute-done((bf16[320,1344]{1,0:T(8,128)(2,1)S(1)}, bf16[320,1344]{1,0:T(8,128)(2,1)S(1)}, u32[]{:S(2)}, u32[]{:S(2)}) %collective-permute-start.49) | collective-permute-done | bytes 860192 | tf_op jit(solution)/shard_map/ppermute | solution.py:765
  379.2 24.5 %collective-permute-done.48.refs_0_ = bf16[64,2560]{1,0:T(8,128)(2,1)S(1)} collective-permute-done((bf16[64,2560]{1,0:T(8,128)(2,1)S(1)}, bf16[64,2560]{1,0:T(8,128)(2,1)S(1)}, u32[]{:S(2)}, u32[]{:S(2)}) %collective-permute-start.48) | collective-permute-done | bytes 327712 | tf_op jit(solution)/shard_map/ppermute | solution.py:765
  412.5 7.7 %collective-permute-done.56 = bf16[64,2560]{1,0:T(8,128)(2,1)S(1)} collective-permute-done((bf16[64,2560]{1,0:T(8,128)(2,1)S(1)}, bf16[64,2560]{1,0:T(8,128)(2,1)S(1)}, u32[]{:S(2)}, u32[]{:S(2)}) %collective-permute-start.56) | collective-permute-done | bytes 327712 | tf_op jit(solution)/shard_map/ppermute | solution.py:765
  422.5 8.1 %collective-permute-done.58.refs_0_ = bf16[320,1344]{1,0:T(8,128)(2,1)S(1)} collective-permute-done((bf16[320,1344]{1,0:T(8,128)(2,1)S(1)}, bf16[320,1344]{1,0:T(8,128)(2,1)S(1)}, u32[]{:S(2)}, u32[]{:S(2)}) %collective-permute-start.58) | collective-permute-done | bytes 860192 | tf_op jit(solution)/shard_map/ppermute | solution.py:765
  431.4 8.2 %collective-permute-done.59 = bf16[64,2560]{1,0:T(8,128)(2,1)S(1)} collective-permute-done((bf16[64,2560]{1,0:T(8,128)(2,1)S(1)}, bf16[64,2560]{1,0:T(8,128)(2,1)S(1)}, u32[]{:S(2)}, u32[]{:S(2)}) %collective-permute-start.59) | collective-permute-done | bytes 327712 | tf_op jit(solution)/shard_map/ppermute | solution.py:765
  441.7 22.5 %collective-permute-done.64.refs_1_ = bf16[320,1344]{1,0:T(8,128)(2,1)S(1)} collective-permute-done((bf16[320,1344]{1,0:T(8,128)(2,1)S(1)}, bf16[320,1344]{1,0:T(8,128)(2,1)S(1)}, u32[]{:S(2)}, u32[]{:S(2)}) %collective-permute-start.64) | collective-permute-done | bytes 860192 | tf_op jit(solution)/shard_map/ppermute | solution.py:765
  476.8 9.1 %shard_map.227 = (bf16[512,320]{1,0:T(8,128)(2,1)S(1)}, f32[512,160]{1,0:T(8,128)S(1)}, bf16[512,160]{1,0:T(8,128)(2,1)S(1)}) custom-call(s32[4]{0:T(128)S(1)} %pad_add_fusion.where, s32[2]{0:T(128)S(1)} %copy-done.53, bf16[512,480]{1,0:T(8,128)(2,1)S(1)} %copy-done.37, bf16[512,160]{1,0:T(8,128)(2,1)S(1)} %copy-done.52, ...), custom_call_target="tpu_custom_call" | custom-call | flops 4294967296 | bytes 4194304 | tf_op jit(solution)/shard_map/pallas_call | solution.py:715
  487.6 7.9 %collective-permute-done.62.refs_2_ = bf16[4,160,320]{2,1,0:T(8,128)(2,1)S(1)} collective-permute-done((bf16[4,160,320]{2,1,0:T(8,128)(2,1)S(1)}, bf16[4,160,320]{2,1,0:T(8,128)(2,1)S(1)}, u32[]{:S(2)}, u32[]{:S(2)}) %collective-permute-start.62) | collective-permute-done | bytes 409632 | tf_op jit(solution)/shard_map/ppermute | solution.py:765
  521.4 10.0 %collective-permute-done.75.refs_3_ = bf16[4,160,480]{2,1,0:T(8,128)(2,1)S(1)} collective-permute-done((bf16[4,160,480]{2,1,0:T(8,128)(2,1)}, bf16[4,160,480]{2,1,0:T(8,128)(2,1)S(1)}, u32[]{:S(2)}, u32[]{:S(2)}) %collective-permute-start.75) | collective-permute-done | bytes 614432 | tf_op jit(solution)/shard_map/ppermute | solution.py:765
  531.3 9.5 %collective-permute-done.74.refs_2_ = bf16[4,160,480]{2,1,0:T(8,128)(2,1)S(1)} collective-permute-done((bf16[4,160,480]{2,1,0:T(8,128)(2,1)}, bf16[4,160,480]{2,1,0:T(8,128)(2,1)S(1)}, u32[]{:S(2)}, u32[]{:S(2)}) %collective-permute-start.74) | collective-permute-done | bytes 614432 | tf_op jit(solution)/shard_map/ppermute | solution.py:765
  562.4 11.3 %collective-permute-done.76.refs_1_ = bf16[2,160,320]{2,1,0:T(8,128)(2,1)S(1)} collective-permute-done((bf16[2,160,320]{2,1,0:T(8,128)(2,1)}, bf16[2,160,320]{2,1,0:T(8,128)(2,1)S(1)}, u32[]{:S(2)}, u32[]{:S(2)}) %collective-permute-start.76) | collective-permute-done | bytes 204832 | tf_op jit(solution)/shard_map/ppermute | solution.py:765
  (404 shorter events, 286.7 us)
Async XLA Ops:
  7.2 64.5 %all-gather.3.cloned.1.call-start = ((), (), s32[]{:S(2)}) async-start(), calls=%async_computation.6 | async-start | bytes 1638400 | tf_op jit(solution)/shard_map/all_gather | solution.py:816
  13.0 203.8 %reduce-scatter.4.cloned.1.call-start = ((), (), s32[]{:S(2)}) async-start(), calls=%async_computation.3 | async-start | bytes 2949120 | tf_op jit(solution)/shard_map/reduce_scatter | solution.py:819
  76.5 29.6 %collective-permute-start.12 = (bf16[4,160,512]{2,1,0:T(8,128)(2,1)S(1)}, bf16[4,160,512]{2,1,0:T(8,128)(2,1)S(1)}, u32[]{:S(2)}, u32[]{:S(2)}) collective-permute-start(bf16[4,160,512]{2,1,0:T(8,128)(2,1)S(1)} %pad_maximum_fusion.1.refs_0_), channel_id=1, source_target_pairs={{0,2},{1,3},{2,0},{3,1},{4,6},{5,7},{6,4},{7,5},{8,10},{9,11},{10,... | collective-permute-start | bytes 1966088 | tf_op jit(solution)/shard_map/ppermute | solution.py:765
  77.0 29.4 %collective-permute-start.11 = (bf16[4,160,512]{2,1,0:T(8,128)(2,1)S(1)}, bf16[4,160,512]{2,1,0:T(8,128)(2,1)S(1)}, u32[]{:S(2)}, u32[]{:S(2)}) collective-permute-start(bf16[4,160,512]{2,1,0:T(8,128)(2,1)S(1)} %pad_maximum_fusion.1.refs_0_), channel_id=1, source_target_pairs={{0,4},{1,5},{2,6},{3,7},{4,0},{5,1},{6,2},{7,3},{8,12},{9,13},{10,... | collective-permute-start | bytes 1966088 | tf_op jit(solution)/shard_map/ppermute | solution.py:765
  106.3 27.7 %collective-permute-start.18 = (bf16[256,2560]{1,0:T(8,128)(2,1)S(1)}, bf16[256,2560]{1,0:T(8,128)(2,1)S(1)}, u32[]{:S(2)}, u32[]{:S(2)}) collective-permute-start(bf16[256,2560]{1,0:T(8,128)(2,1)S(1)} %pad_maximum_fusion.refs_0_), channel_id=1, source_target_pairs={{0,1},{1,0},{2,3},{3,2},{4,5},{5,4},{6,7},{7,6},{8,9},{9,8},{10,11... | collective-permute-start | bytes 3932168 | tf_op jit(solution)/shard_map/ppermute | solution.py:765
  160.2 416.7 %reduce-scatter.8.cloned.1.call-start = ((), (), s32[]{:S(2)}) async-start(), calls=%async_computation.5 | async-start | bytes 2949120 | tf_op jit(solution)/shard_map/reduce_scatter | solution.py:819
  161.5 46.9 %collective-permute-start.25 = (bf16[256,2560]{1,0:T(8,128)(2,1)S(1)}, bf16[256,2560]{1,0:T(8,128)(2,1)S(1)}, u32[]{:S(2)}, u32[]{:S(2)}) collective-permute-start(bf16[256,2560]{1,0:T(8,128)(2,1)S(1)} %bitcast.72), channel_id=1, source_target_pairs={{0,2},{1,3},{2,0},{3,1},{4,6},{5,7},{6,4},{7,5},{8,10},{9,11},{10,... | collective-permute-start | bytes 3932168 | tf_op jit(solution)/shard_map/ppermute | solution.py:765
  162.2 43.8 %collective-permute-start.26 = (bf16[320,1344]{1,0:T(8,128)(2,1)}, bf16[320,1344]{1,0:T(8,128)(2,1)}, u32[]{:S(2)}, u32[]{:S(2)}) collective-permute-start(bf16[320,1344]{1,0:T(8,128)(2,1)} %copy-done.41), channel_id=1, source_target_pairs={{0,8},{1,9},{2,10},{3,11},{4,12},{5,13},{6,14},{7,15},{8,16},{9,17... | collective-permute-start | bytes 2580488 | tf_op jit(solution)/shard_map/ppermute | solution.py:765
  206.0 38.1 %collective-permute-start.31 = (bf16[320,1344]{1,0:T(8,128)(2,1)}, bf16[320,1344]{1,0:T(8,128)(2,1)}, u32[]{:S(2)}, u32[]{:S(2)}) collective-permute-start(bf16[320,1344]{1,0:T(8,128)(2,1)} %copy-done.40), channel_id=1, source_target_pairs={{0,24},{1,25},{2,26},{3,27},{4,28},{5,29},{6,30},{7,31},{8,0},{9,1... | collective-permute-start | bytes 2580488 | tf_op jit(solution)/shard_map/ppermute | solution.py:765
  206.9 37.2 %collective-permute-start.34 = (bf16[320,1344]{1,0:T(8,128)(2,1)}, bf16[320,1344]{1,0:T(8,128)(2,1)}, u32[]{:S(2)}, u32[]{:S(2)}) collective-permute-start(bf16[320,1344]{1,0:T(8,128)(2,1)} %collective-permute-done.26.refs_5_), channel_id=1, source_target_pairs={{0,4},{1,5},{2,6},{3,7},{4,0},{5,1},{6,2},{7,3},{8,12},{9,13},{10,... | collective-permute-start | bytes 2580488 | tf_op jit(solution)/shard_map/ppermute | solution.py:765
  279.0 24.3 %collective-permute-start.41 = (bf16[256,2560]{1,0:T(8,128)(2,1)S(1)}, bf16[256,2560]{1,0:T(8,128)(2,1)S(1)}, u32[]{:S(2)}, u32[]{:S(2)}) collective-permute-start(bf16[256,2560]{1,0:T(8,128)(2,1)S(1)} %bitcast.73), channel_id=1, source_target_pairs={{0,1},{1,0},{2,3},{3,2},{4,5},{5,4},{6,7},{7,6},{8,9},{9,8},{10,11... | collective-permute-start | bytes 3932168 | tf_op jit(solution)/shard_map/ppermute | solution.py:765
  318.7 30.5 %collective-permute-start.46 = (bf16[128,2560]{1,0:T(8,128)(2,1)S(1)}, bf16[128,2560]{1,0:T(8,128)(2,1)S(1)}, u32[]{:S(2)}, u32[]{:S(2)}) collective-permute-start(bf16[128,2560]{1,0:T(8,128)(2,1)S(1)} %get-tuple-element.192), channel_id=1, source_target_pairs={{0,2},{1,3},{2,0},{3,1},{4,6},{5,7},{6,4},{7,5},{8,10},{9,11},{10,... | collective-permute-start | bytes 1966088 | tf_op jit(solution)/shard_map/ppermute | solution.py:765
  324.7 24.2 %collective-permute-start.44 = (bf16[64,2560]{1,0:T(8,128)(2,1)S(1)}, bf16[64,2560]{1,0:T(8,128)(2,1)S(1)}, u32[]{:S(2)}, u32[]{:S(2)}) collective-permute-start(bf16[64,2560]{1,0:T(8,128)(2,1)S(1)} %slice.81), channel_id=1, source_target_pairs={{0,8},{1,9},{2,10},{3,11},{4,12},{5,13},{6,14},{7,15},{8,24},{9,25... | collective-permute-start | bytes 983048 | tf_op jit(solution)/shard_map/ppermute | solution.py:765
  346.4 25.6 %collective-permute-start.51 = (bf16[320,1344]{1,0:T(8,128)(2,1)S(1)}, bf16[320,1344]{1,0:T(8,128)(2,1)S(1)}, u32[]{:S(2)}, u32[]{:S(2)}) collective-permute-start(bf16[320,1344]{1,0:T(8,128)(2,1)S(1)} %shard_map.220), channel_id=1, source_target_pairs={{0,8},{1,9},{2,10},{3,11},{4,12},{5,13},{6,14},{7,15},{8,16},{9,17... | collective-permute-start | bytes 2580488 | tf_op jit(solution)/shard_map/ppermute | solution.py:765
  349.0 29.9 %collective-permute-start.45 = (bf16[64,2560]{1,0:T(8,128)(2,1)S(1)}, bf16[64,2560]{1,0:T(8,128)(2,1)S(1)}, u32[]{:S(2)}, u32[]{:S(2)}) collective-permute-start(bf16[64,2560]{1,0:T(8,128)(2,1)S(1)} %fusion.16), channel_id=1, source_target_pairs={{0,8},{1,9},{2,10},{3,11},{4,12},{5,13},{6,14},{7,15},{8,24},{9,25... | collective-permute-start | bytes 983048 | tf_op jit(solution)/shard_map/ppermute | solution.py:765
  367.2 36.5 %collective-permute-start.50 = (bf16[320,1344]{1,0:T(8,128)(2,1)S(1)}, bf16[320,1344]{1,0:T(8,128)(2,1)S(1)}, u32[]{:S(2)}, u32[]{:S(2)}) collective-permute-start(bf16[320,1344]{1,0:T(8,128)(2,1)S(1)} %get-tuple-element.219), channel_id=1, source_target_pairs={{0,4},{1,5},{2,6},{3,7},{4,0},{5,1},{6,2},{7,3},{8,12},{9,13},{10,... | collective-permute-start | bytes 2580488 | tf_op jit(solution)/shard_map/ppermute | solution.py:765
  372.0 31.7 %collective-permute-start.52 = (bf16[320,1344]{1,0:T(8,128)(2,1)S(1)}, bf16[320,1344]{1,0:T(8,128)(2,1)S(1)}, u32[]{:S(2)}, u32[]{:S(2)}) collective-permute-start(bf16[320,1344]{1,0:T(8,128)(2,1)S(1)} %collective-permute-done.51), channel_id=1, source_target_pairs={{0,8},{1,9},{2,10},{3,11},{4,12},{5,13},{6,14},{7,15},{8,16},{9,17... | collective-permute-start | bytes 2580488 | tf_op jit(solution)/shard_map/ppermute | solution.py:765
  379.0 24.7 %collective-permute-start.48 = (bf16[64,2560]{1,0:T(8,128)(2,1)S(1)}, bf16[64,2560]{1,0:T(8,128)(2,1)S(1)}, u32[]{:S(2)}, u32[]{:S(2)}) collective-permute-start(bf16[64,2560]{1,0:T(8,128)(2,1)S(1)} %get-tuple-element.217), channel_id=1, source_target_pairs={{0,8},{1,9},{2,10},{3,11},{4,12},{5,13},{6,14},{7,15},{8,24},{9,25... | collective-permute-start | bytes 983048 | tf_op jit(solution)/shard_map/ppermute | solution.py:765
  421.8 43.4 %collective-permute-start.55 = (bf16[256,2560]{1,0:T(8,128)(2,1)S(1)}, bf16[256,2560]{1,0:T(8,128)(2,1)S(1)}, u32[]{:S(2)}, u32[]{:S(2)}) collective-permute-start(bf16[256,2560]{1,0:T(8,128)(2,1)S(1)} %shard_map.221), channel_id=1, source_target_pairs={{0,2},{1,3},{2,0},{3,1},{4,6},{5,7},{6,4},{7,5},{8,10},{9,11},{10,... | collective-permute-start | bytes 3932168 | tf_op jit(solution)/shard_map/ppermute | solution.py:765
  439.7 27.0 %collective-permute-start.60 = (bf16[256,2560]{1,0:T(8,128)(2,1)S(1)}, bf16[256,2560]{1,0:T(8,128)(2,1)}, u32[]{:S(2)}, u32[]{:S(2)}) collective-permute-start(bf16[256,2560]{1,0:T(8,128)(2,1)S(1)} %constant_dynamic-update-slice_fusion.6.refs_0_), channel_id=1, source_target_pairs={{0,1},{1,0},{2,3},{3,2},{4,5},{5,4},{6,7},{7,6},{8,9},{9,8},{10,11... | collective-permute-start | bytes 3932168 | tf_op jit(solution)/shard_map/ppermute | solution.py:765
  440.0 24.2 %collective-permute-start.64 = (bf16[320,1344]{1,0:T(8,128)(2,1)S(1)}, bf16[320,1344]{1,0:T(8,128)(2,1)S(1)}, u32[]{:S(2)}, u32[]{:S(2)}) collective-permute-start(bf16[320,1344]{1,0:T(8,128)(2,1)S(1)} %shard_map.229), channel_id=1, source_target_pairs={{0,8},{1,9},{2,10},{3,11},{4,12},{5,13},{6,14},{7,15},{8,16},{9,17... | collective-permute-start | bytes 2580488 | tf_op jit(solution)/shard_map/ppermute | solution.py:765
  511.9 71.1 %reduce-scatter.6.cloned.1.call-start = ((), (), s32[]{:S(2)}) async-start(), calls=%async_computation.4 | async-start | bytes 1638400 | tf_op jit(solution)/shard_map/reduce_scatter | solution.py:819
  514.1 26.7 %collective-permute-start.74 = (bf16[4,160,480]{2,1,0:T(8,128)(2,1)}, bf16[4,160,480]{2,1,0:T(8,128)(2,1)S(1)}, u32[]{:S(2)}, u32[]{:S(2)}) collective-permute-start(bf16[4,160,480]{2,1,0:T(8,128)(2,1)} %copy-done.49), channel_id=1, source_target_pairs={{0,2},{1,3},{2,0},{3,1},{4,6},{5,7},{6,4},{7,5},{8,10},{9,11},{10,... | collective-permute-start | bytes 1843208 | tf_op jit(solution)/shard_map/ppermute | solution.py:765
  514.8 26.1 %collective-permute-start.73 = (bf16[4,160,480]{2,1,0:T(8,128)(2,1)}, bf16[4,160,480]{2,1,0:T(8,128)(2,1)S(1)}, u32[]{:S(2)}, u32[]{:S(2)}) collective-permute-start(bf16[4,160,480]{2,1,0:T(8,128)(2,1)} %copy-done.48), channel_id=1, source_target_pairs={{0,4},{1,5},{2,6},{3,7},{4,0},{5,1},{6,2},{7,3},{8,12},{9,13},{10,... | collective-permute-start | bytes 1843208 | tf_op jit(solution)/shard_map/ppermute | solution.py:765
  (134 other events, 1660.8 us)
Sparse Core Ops, SparseCore 0:
  13.1 40.2 all-gather.2
  160.3 56.4 reduce-scatter.3
  512.0 38.0 reduce-scatter.7
  552.8 30.0 reduce-scatter.5

commit v4 on v3

--- a/solution.py
+++ b/solution.py
@@ -989,7 +989,7 @@
     for k in [0, middle] + ends:
         moved_x[k] = [grid.to_x(after(arrived[k], *first), x) for x in others]
         first = moved_x[k]
-    mlp_grad = grid.spread_yc(after(cot_all, *out_units[1:]))
+    mlp_grad = grid.spread_yc(after(cot_all, *out_units[1:], *[heads]))
     attn_partial = contract_last(after(heads, *[arrived[middle]]), w_o).astype(BF16)
     attn_out = grid.scatter(attn_partial, "zc")
     held = list(mlp_grad[: grid.Y]) + list([arrived[ends[0]]]) + list(moved_x[middle])
@@ -1044,7 +1044,7 @@
     last = holds[3]
     holds = [
         [],
-        list(holds[1]),
+        list(holds[1]) + list([hidden_parts[middle]]),
         list(holds[2]) + list([hidden_parts[middle]]),
     ]
     in_parts = grid.ring_sum(slots, holds)
@@ -1122,7 +1122,7 @@
     result_low = (hidden + after(mlp_out, *[partial]).astype(F32)).astype(BF16)
     result = spread_c(spread_y(result_low))
     held = [gate_wgrad]
-    held = held
+    held = held + list(out_parts[1:])
     qkv_sums = unit_sum([after(unit, *held) for unit in qkv_moved])
     qkv_parts = grid.exchange_z(qkv_sums)
     qkv_wgrad = grid.return_heads(qkv_parts, (q_cols, HEAD_DIM, HEAD_DIM))

time: 623 us -> 623 us (level)
  no operation moved by 1% of the time
where the time goes in v4:
time: 623 us; the launch traced here: 617 us
  waiting for transfers between devices  353 us (57%)
  starting transfers between devices  116 us (19%)
  Pallas kernels  96.9 us (16%)
  local copies, waits for them, and re-layouts  22.8 us (4%)
  between operations  15.5 us (2%)
  matrix products  9.14 us (1%)
    ppermute x90, waiting for transfers between devices, move(): return lax.ppermute(value, AXES, pairs)  340 us
    ppermute x90, starting transfers between devices, move(): return lax.ppermute(value, AXES, pairs)  116 us
    pallas_call x2, Pallas kernels, hidden_layer(): pl.pallas_call(functools.partial(hidden_kernel, Z, X, C, tuple(grid.order...  29.5 us
    unnamed x143, local copies, waits for them, and re-layouts  19.1 us
    pallas_call x4, Pallas kernels, hidden_weight_grad(): pl.pallas_call(functools.partial(hidden_weight_kernel, X, tiles), out_sha...  13.5 us
  transfers between devices with their start and end apart: 94, of which 46 were waited for; matrix products, arithmetic and copies ran while one was open for 2% of the time, Pallas kernels for 15%

profile of v4, /device:TPU:0, one launch (start us, length us, event | category | flops | bytes accessed | tf_op | source)
XLA Modules:
  0.0 616.7 jit_solution(13760345477165311743)
XLA Ops:
  37.1 13.9 %collective-permute-done.5 = bf16[64,2560]{1,0:T(8,128)(2,1)S(1)} collective-permute-done((bf16[64,2560]{1,0:T(8,128)(2,1)S(1)}, bf16[64,2560]{1,0:T(8,128)(2,1)S(1)}, u32[]{:S(2)}, u32[]{:S(2)}) %collective-permute-start.5) | collective-permute-done | bytes 327712 | tf_op jit(solution)/shard_map/ppermute | solution.py:765
  80.1 8.2 %collective-permute-done.15 = bf16[160,384]{1,0:T(8,128)(2,1)S(1)} collective-permute-done((bf16[160,384]{1,0:T(8,128)(2,1)S(1)}, bf16[160,384]{1,0:T(8,128)(2,1)S(1)}, u32[]{:S(2)}, u32[]{:S(2)}) %collective-permute-start.15) | collective-permute-done | bytes 122912 | tf_op jit(solution)/shard_map/ppermute | solution.py:765
  95.8 10.4 %collective-permute-done.12.refs_2_ = bf16[4,160,512]{2,1,0:T(8,128)(2,1)S(1)} collective-permute-done((bf16[4,160,512]{2,1,0:T(8,128)(2,1)S(1)}, bf16[4,160,512]{2,1,0:T(8,128)(2,1)S(1)}, u32[]{:S(2)}, u32[]{:S(2)}) %collective-permute-start.12) | collective-permute-done | bytes 655392 | tf_op jit(solution)/shard_map/ppermute | solution.py:765
  111.3 19.2 %collective-permute-done.22 = bf16[320,1344]{1,0:T(8,128)(2,1)S(1)} collective-permute-done((bf16[320,1344]{1,0:T(8,128)(2,1)S(1)}, bf16[320,1344]{1,0:T(8,128)(2,1)S(1)}, u32[]{:S(2)}, u32[]{:S(2)}) %collective-permute-start.22) | collective-permute-done | bytes 860192 | tf_op jit(solution)/shard_map/ppermute | solution.py:765
  162.2 19.3 %collective-permute-done.27.refs_8_ = bf16[320,1344]{1,0:T(8,128)(2,1)S(1)} collective-permute-done((bf16[320,1344]{1,0:T(8,128)(2,1)}, bf16[320,1344]{1,0:T(8,128)(2,1)S(1)}, u32[]{:S(2)}, u32[]{:S(2)}) %collective-permute-start.27) | collective-permute-done | bytes 860192 | tf_op jit(solution)/shard_map/ppermute | solution.py:765
  183.1 22.9 %collective-permute-done.26.refs_5_ = bf16[320,1344]{1,0:T(8,128)(2,1)} collective-permute-done((bf16[320,1344]{1,0:T(8,128)(2,1)}, bf16[320,1344]{1,0:T(8,128)(2,1)}, u32[]{:S(2)}, u32[]{:S(2)}) %collective-permute-start.26) | collective-permute-done | bytes 860192 | tf_op jit(solution)/shard_map/ppermute | solution.py:765
  208.4 8.5 %reduce-scatter.4.cloned.1.call-done.more = bf16[64,2560]{1,0:T(8,128)(2,1)} async-done(((bf16[512,2560]{1,0:T(8,128)(2,1)}), bf16[64,2560]{1,0:T(8,128)(2,1)}) %reduce-scatter.4.cloned.1.call-update) | async-done | bytes 327696 | tf_op jit(solution)/shard_map/reduce_scatter | solution.py:819
  218.0 16.4 %collective-permute-start.29 = (bf16[64,2560]{1,0:T(8,128)(2,1)S(1)}, bf16[64,2560]{1,0:T(8,128)(2,1)S(1)}, u32[]{:S(2)}, u32[]{:S(2)}) collective-permute-start(bf16[64,2560]{1,0:T(8,128)(2,1)S(1)} %get-tuple-element.183), channel_id=1, source_target_pairs={{0,16},{1,17},{2,18},{3,19},{4,20},{5,21},{6,22},{7,23},{8,0},{9,1... | collective-permute-start | bytes 983048 | tf_op jit(solution)/shard_map/ppermute | solution.py:765
  260.9 10.9 %collective-permute-done.33 = bf16[128,2560]{1,0:T(8,128)(2,1)S(1)} collective-permute-done((bf16[128,2560]{1,0:T(8,128)(2,1)S(1)}, bf16[128,2560]{1,0:T(8,128)(2,1)S(1)}, u32[]{:S(2)}, u32[]{:S(2)}) %collective-permute-start.33) | collective-permute-done | bytes 655392 | tf_op jit(solution)/shard_map/ppermute | solution.py:765
  271.8 7.0 %collective-permute-done.36 = bf16[128,2560]{1,0:T(8,128)(2,1)S(1)} collective-permute-done((bf16[128,2560]{1,0:T(8,128)(2,1)S(1)}, bf16[128,2560]{1,0:T(8,128)(2,1)S(1)}, u32[]{:S(2)}, u32[]{:S(2)}) %collective-permute-start.36) | collective-permute-done | bytes 655392 | tf_op jit(solution)/shard_map/ppermute | solution.py:765
  282.0 14.7 %shard_map.213 = (f32[256,2560]{1,0:T(8,128)}, bf16[256,2560]{1,0:T(8,128)(2,1)S(1)}, f32[256,2560]{1,0:T(8,128)}, bf16[256,2560]{1,0:T(8,128)(2,1)S(1)}, bf16[5...) custom-call(s32[4]{0:T(128)S(1)} %pad_add_fusion.where, ...), custom_call_target="tpu_custom_call" | custom-call | flops 7046430720 | bytes 20971520 | tf_op jit(solution)/shard_map/pallas_call | solution.py:287
  303.3 14.8 %shard_map.215 = (f32[256,2560]{1,0:T(8,128)}, bf16[256,2560]{1,0:T(8,128)(2,1)S(1)}, f32[256,2560]{1,0:T(8,128)}, bf16[256,2560]{1,0:T(8,128)(2,1)S(1)}, bf16[5...) custom-call(s32[4]{0:T(128)S(1)} %pad_add_fusion.where, ...), custom_call_target="tpu_custom_call" | custom-call | flops 7046430720 | bytes 20971520 | tf_op jit(solution)/shard_map/pallas_call | solution.py:287
  334.1 11.5 %collective-permute-done.45.refs_0_ = bf16[320,1344]{1,0:T(8,128)(2,1)S(1)} collective-permute-done((bf16[320,1344]{1,0:T(8,128)(2,1)S(1)}, bf16[320,1344]{1,0:T(8,128)(2,1)S(1)}, u32[]{:S(2)}, u32[]{:S(2)}) %collective-permute-start.45) | collective-permute-done | bytes 860192 | tf_op jit(solution)/shard_map/ppermute | solution.py:765
  349.3 18.0 %collective-permute-done.49.refs_0_ = bf16[320,1344]{1,0:T(8,128)(2,1)S(1)} collective-permute-done((bf16[320,1344]{1,0:T(8,128)(2,1)S(1)}, bf16[320,1344]{1,0:T(8,128)(2,1)S(1)}, u32[]{:S(2)}, u32[]{:S(2)}) %collective-permute-start.49) | collective-permute-done | bytes 860192 | tf_op jit(solution)/shard_map/ppermute | solution.py:765
  379.2 24.5 %collective-permute-done.48.refs_0_ = bf16[64,2560]{1,0:T(8,128)(2,1)S(1)} collective-permute-done((bf16[64,2560]{1,0:T(8,128)(2,1)S(1)}, bf16[64,2560]{1,0:T(8,128)(2,1)S(1)}, u32[]{:S(2)}, u32[]{:S(2)}) %collective-permute-start.48) | collective-permute-done | bytes 327712 | tf_op jit(solution)/shard_map/ppermute | solution.py:765
  412.5 7.7 %collective-permute-done.56 = bf16[64,2560]{1,0:T(8,128)(2,1)S(1)} collective-permute-done((bf16[64,2560]{1,0:T(8,128)(2,1)S(1)}, bf16[64,2560]{1,0:T(8,128)(2,1)S(1)}, u32[]{:S(2)}, u32[]{:S(2)}) %collective-permute-start.56) | collective-permute-done | bytes 327712 | tf_op jit(solution)/shard_map/ppermute | solution.py:765
  422.5 8.1 %collective-permute-done.58.refs_0_ = bf16[320,1344]{1,0:T(8,128)(2,1)S(1)} collective-permute-done((bf16[320,1344]{1,0:T(8,128)(2,1)S(1)}, bf16[320,1344]{1,0:T(8,128)(2,1)S(1)}, u32[]{:S(2)}, u32[]{:S(2)}) %collective-permute-start.58) | collective-permute-done | bytes 860192 | tf_op jit(solution)/shard_map/ppermute | solution.py:765
  431.4 8.2 %collective-permute-done.59 = bf16[64,2560]{1,0:T(8,128)(2,1)S(1)} collective-permute-done((bf16[64,2560]{1,0:T(8,128)(2,1)S(1)}, bf16[64,2560]{1,0:T(8,128)(2,1)S(1)}, u32[]{:S(2)}, u32[]{:S(2)}) %collective-permute-start.59) | collective-permute-done | bytes 327712 | tf_op jit(solution)/shard_map/ppermute | solution.py:765
  441.7 22.5 %collective-permute-done.64.refs_1_ = bf16[320,1344]{1,0:T(8,128)(2,1)S(1)} collective-permute-done((bf16[320,1344]{1,0:T(8,128)(2,1)S(1)}, bf16[320,1344]{1,0:T(8,128)(2,1)S(1)}, u32[]{:S(2)}, u32[]{:S(2)}) %collective-permute-start.64) | collective-permute-done | bytes 860192 | tf_op jit(solution)/shard_map/ppermute | solution.py:765
  476.8 9.1 %shard_map.227 = (bf16[512,320]{1,0:T(8,128)(2,1)S(1)}, f32[512,160]{1,0:T(8,128)S(1)}, bf16[512,160]{1,0:T(8,128)(2,1)S(1)}) custom-call(s32[4]{0:T(128)S(1)} %pad_add_fusion.where, s32[2]{0:T(128)S(1)} %copy-done.53, bf16[512,480]{1,0:T(8,128)(2,1)S(1)} %copy-done.37, bf16[512,160]{1,0:T(8,128)(2,1)S(1)} %copy-done.52, ...), custom_call_target="tpu_custom_call" | custom-call | flops 4294967296 | bytes 4194304 | tf_op jit(solution)/shard_map/pallas_call | solution.py:715
  487.6 7.9 %collective-permute-done.62.refs_2_ = bf16[4,160,320]{2,1,0:T(8,128)(2,1)S(1)} collective-permute-done((bf16[4,160,320]{2,1,0:T(8,128)(2,1)S(1)}, bf16[4,160,320]{2,1,0:T(8,128)(2,1)S(1)}, u32[]{:S(2)}, u32[]{:S(2)}) %collective-permute-start.62) | collective-permute-done | bytes 409632 | tf_op jit(solution)/shard_map/ppermute | solution.py:765
  521.4 10.0 %collective-permute-done.75.refs_3_ = bf16[4,160,480]{2,1,0:T(8,128)(2,1)S(1)} collective-permute-done((bf16[4,160,480]{2,1,0:T(8,128)(2,1)}, bf16[4,160,480]{2,1,0:T(8,128)(2,1)S(1)}, u32[]{:S(2)}, u32[]{:S(2)}) %collective-permute-start.75) | collective-permute-done | bytes 614432 | tf_op jit(solution)/shard_map/ppermute | solution.py:765
  531.3 9.5 %collective-permute-done.74.refs_2_ = bf16[4,160,480]{2,1,0:T(8,128)(2,1)S(1)} collective-permute-done((bf16[4,160,480]{2,1,0:T(8,128)(2,1)}, bf16[4,160,480]{2,1,0:T(8,128)(2,1)S(1)}, u32[]{:S(2)}, u32[]{:S(2)}) %collective-permute-start.74) | collective-permute-done | bytes 614432 | tf_op jit(solution)/shard_map/ppermute | solution.py:765
  562.4 11.3 %collective-permute-done.76.refs_1_ = bf16[2,160,320]{2,1,0:T(8,128)(2,1)S(1)} collective-permute-done((bf16[2,160,320]{2,1,0:T(8,128)(2,1)}, bf16[2,160,320]{2,1,0:T(8,128)(2,1)S(1)}, u32[]{:S(2)}, u32[]{:S(2)}) %collective-permute-start.76) | collective-permute-done | bytes 204832 | tf_op jit(solution)/shard_map/ppermute | solution.py:765
  (404 shorter events, 286.7 us)
Async XLA Ops:
  7.2 64.5 %all-gather.3.cloned.1.call-start = ((), (), s32[]{:S(2)}) async-start(), calls=%async_computation.6 | async-start | bytes 1638400 | tf_op jit(solution)/shard_map/all_gather | solution.py:816
  13.0 203.8 %reduce-scatter.4.cloned.1.call-start = ((), (), s32[]{:S(2)}) async-start(), calls=%async_computation.3 | async-start | bytes 2949120 | tf_op jit(solution)/shard_map/reduce_scatter | solution.py:819
  76.5 29.6 %collective-permute-start.12 = (bf16[4,160,512]{2,1,0:T(8,128)(2,1)S(1)}, bf16[4,160,512]{2,1,0:T(8,128)(2,1)S(1)}, u32[]{:S(2)}, u32[]{:S(2)}) collective-permute-start(bf16[4,160,512]{2,1,0:T(8,128)(2,1)S(1)} %pad_maximum_fusion.1.refs_0_), channel_id=1, source_target_pairs={{0,2},{1,3},{2,0},{3,1},{4,6},{5,7},{6,4},{7,5},{8,10},{9,11},{10,... | collective-permute-start | bytes 1966088 | tf_op jit(solution)/shard_map/ppermute | solution.py:765
  77.0 29.4 %collective-permute-start.11 = (bf16[4,160,512]{2,1,0:T(8,128)(2,1)S(1)}, bf16[4,160,512]{2,1,0:T(8,128)(2,1)S(1)}, u32[]{:S(2)}, u32[]{:S(2)}) collective-permute-start(bf16[4,160,512]{2,1,0:T(8,128)(2,1)S(1)} %pad_maximum_fusion.1.refs_0_), channel_id=1, source_target_pairs={{0,4},{1,5},{2,6},{3,7},{4,0},{5,1},{6,2},{7,3},{8,12},{9,13},{10,... | collective-permute-start | bytes 1966088 | tf_op jit(solution)/shard_map/ppermute | solution.py:765
  106.3 27.7 %collective-permute-start.18 = (bf16[256,2560]{1,0:T(8,128)(2,1)S(1)}, bf16[256,2560]{1,0:T(8,128)(2,1)S(1)}, u32[]{:S(2)}, u32[]{:S(2)}) collective-permute-start(bf16[256,2560]{1,0:T(8,128)(2,1)S(1)} %pad_maximum_fusion.refs_0_), channel_id=1, source_target_pairs={{0,1},{1,0},{2,3},{3,2},{4,5},{5,4},{6,7},{7,6},{8,9},{9,8},{10,11... | collective-permute-start | bytes 3932168 | tf_op jit(solution)/shard_map/ppermute | solution.py:765
  160.2 416.7 %reduce-scatter.8.cloned.1.call-start = ((), (), s32[]{:S(2)}) async-start(), calls=%async_computation.5 | async-start | bytes 2949120 | tf_op jit(solution)/shard_map/reduce_scatter | solution.py:819
  161.5 46.9 %collective-permute-start.25 = (bf16[256,2560]{1,0:T(8,128)(2,1)S(1)}, bf16[256,2560]{1,0:T(8,128)(2,1)S(1)}, u32[]{:S(2)}, u32[]{:S(2)}) collective-permute-start(bf16[256,2560]{1,0:T(8,128)(2,1)S(1)} %bitcast.72), channel_id=1, source_target_pairs={{0,2},{1,3},{2,0},{3,1},{4,6},{5,7},{6,4},{7,5},{8,10},{9,11},{10,... | collective-permute-start | bytes 3932168 | tf_op jit(solution)/shard_map/ppermute | solution.py:765
  162.2 43.8 %collective-permute-start.26 = (bf16[320,1344]{1,0:T(8,128)(2,1)}, bf16[320,1344]{1,0:T(8,128)(2,1)}, u32[]{:S(2)}, u32[]{:S(2)}) collective-permute-start(bf16[320,1344]{1,0:T(8,128)(2,1)} %copy-done.41), channel_id=1, source_target_pairs={{0,8},{1,9},{2,10},{3,11},{4,12},{5,13},{6,14},{7,15},{8,16},{9,17... | collective-permute-start | bytes 2580488 | tf_op jit(solution)/shard_map/ppermute | solution.py:765
  206.0 38.1 %collective-permute-start.31 = (bf16[320,1344]{1,0:T(8,128)(2,1)}, bf16[320,1344]{1,0:T(8,128)(2,1)}, u32[]{:S(2)}, u32[]{:S(2)}) collective-permute-start(bf16[320,1344]{1,0:T(8,128)(2,1)} %copy-done.40), channel_id=1, source_target_pairs={{0,24},{1,25},{2,26},{3,27},{4,28},{5,29},{6,30},{7,31},{8,0},{9,1... | collective-permute-start | bytes 2580488 | tf_op jit(solution)/shard_map/ppermute | solution.py:765
  206.9 37.2 %collective-permute-start.34 = (bf16[320,1344]{1,0:T(8,128)(2,1)}, bf16[320,1344]{1,0:T(8,128)(2,1)}, u32[]{:S(2)}, u32[]{:S(2)}) collective-permute-start(bf16[320,1344]{1,0:T(8,128)(2,1)} %collective-permute-done.26.refs_5_), channel_id=1, source_target_pairs={{0,4},{1,5},{2,6},{3,7},{4,0},{5,1},{6,2},{7,3},{8,12},{9,13},{10,... | collective-permute-start | bytes 2580488 | tf_op jit(solution)/shard_map/ppermute | solution.py:765
  279.0 24.3 %collective-permute-start.41 = (bf16[256,2560]{1,0:T(8,128)(2,1)S(1)}, bf16[256,2560]{1,0:T(8,128)(2,1)S(1)}, u32[]{:S(2)}, u32[]{:S(2)}) collective-permute-start(bf16[256,2560]{1,0:T(8,128)(2,1)S(1)} %bitcast.73), channel_id=1, source_target_pairs={{0,1},{1,0},{2,3},{3,2},{4,5},{5,4},{6,7},{7,6},{8,9},{9,8},{10,11... | collective-permute-start | bytes 3932168 | tf_op jit(solution)/shard_map/ppermute | solution.py:765
  318.7 30.5 %collective-permute-start.47 = (bf16[128,2560]{1,0:T(8,128)(2,1)S(1)}, bf16[128,2560]{1,0:T(8,128)(2,1)S(1)}, u32[]{:S(2)}, u32[]{:S(2)}) collective-permute-start(bf16[128,2560]{1,0:T(8,128)(2,1)S(1)} %get-tuple-element.192), channel_id=1, source_target_pairs={{0,2},{1,3},{2,0},{3,1},{4,6},{5,7},{6,4},{7,5},{8,10},{9,11},{10,... | collective-permute-start | bytes 1966088 | tf_op jit(solution)/shard_map/ppermute | solution.py:765
  324.7 24.2 %collective-permute-start.44 = (bf16[64,2560]{1,0:T(8,128)(2,1)S(1)}, bf16[64,2560]{1,0:T(8,128)(2,1)S(1)}, u32[]{:S(2)}, u32[]{:S(2)}) collective-permute-start(bf16[64,2560]{1,0:T(8,128)(2,1)S(1)} %slice.81), channel_id=1, source_target_pairs={{0,8},{1,9},{2,10},{3,11},{4,12},{5,13},{6,14},{7,15},{8,24},{9,25... | collective-permute-start | bytes 983048 | tf_op jit(solution)/shard_map/ppermute | solution.py:765
  346.4 25.6 %collective-permute-start.51 = (bf16[320,1344]{1,0:T(8,128)(2,1)S(1)}, bf16[320,1344]{1,0:T(8,128)(2,1)S(1)}, u32[]{:S(2)}, u32[]{:S(2)}) collective-permute-start(bf16[320,1344]{1,0:T(8,128)(2,1)S(1)} %shard_map.220), channel_id=1, source_target_pairs={{0,8},{1,9},{2,10},{3,11},{4,12},{5,13},{6,14},{7,15},{8,16},{9,17... | collective-permute-start | bytes 2580488 | tf_op jit(solution)/shard_map/ppermute | solution.py:765
  349.0 29.9 %collective-permute-start.46 = (bf16[64,2560]{1,0:T(8,128)(2,1)S(1)}, bf16[64,2560]{1,0:T(8,128)(2,1)S(1)}, u32[]{:S(2)}, u32[]{:S(2)}) collective-permute-start(bf16[64,2560]{1,0:T(8,128)(2,1)S(1)} %fusion.16), channel_id=1, source_target_pairs={{0,8},{1,9},{2,10},{3,11},{4,12},{5,13},{6,14},{7,15},{8,24},{9,25... | collective-permute-start | bytes 983048 | tf_op jit(solution)/shard_map/ppermute | solution.py:765
  367.2 36.5 %collective-permute-start.50 = (bf16[320,1344]{1,0:T(8,128)(2,1)S(1)}, bf16[320,1344]{1,0:T(8,128)(2,1)S(1)}, u32[]{:S(2)}, u32[]{:S(2)}) collective-permute-start(bf16[320,1344]{1,0:T(8,128)(2,1)S(1)} %get-tuple-element.219), channel_id=1, source_target_pairs={{0,4},{1,5},{2,6},{3,7},{4,0},{5,1},{6,2},{7,3},{8,12},{9,13},{10,... | collective-permute-start | bytes 2580488 | tf_op jit(solution)/shard_map/ppermute | solution.py:765
  372.0 31.7 %collective-permute-start.52 = (bf16[320,1344]{1,0:T(8,128)(2,1)S(1)}, bf16[320,1344]{1,0:T(8,128)(2,1)S(1)}, u32[]{:S(2)}, u32[]{:S(2)}) collective-permute-start(bf16[320,1344]{1,0:T(8,128)(2,1)S(1)} %collective-permute-done.51), channel_id=1, source_target_pairs={{0,8},{1,9},{2,10},{3,11},{4,12},{5,13},{6,14},{7,15},{8,16},{9,17... | collective-permute-start | bytes 2580488 | tf_op jit(solution)/shard_map/ppermute | solution.py:765
  379.0 24.7 %collective-permute-start.48 = (bf16[64,2560]{1,0:T(8,128)(2,1)S(1)}, bf16[64,2560]{1,0:T(8,128)(2,1)S(1)}, u32[]{:S(2)}, u32[]{:S(2)}) collective-permute-start(bf16[64,2560]{1,0:T(8,128)(2,1)S(1)} %get-tuple-element.217), channel_id=1, source_target_pairs={{0,8},{1,9},{2,10},{3,11},{4,12},{5,13},{6,14},{7,15},{8,24},{9,25... | collective-permute-start | bytes 983048 | tf_op jit(solution)/shard_map/ppermute | solution.py:765
  421.8 43.4 %collective-permute-start.55 = (bf16[256,2560]{1,0:T(8,128)(2,1)S(1)}, bf16[256,2560]{1,0:T(8,128)(2,1)S(1)}, u32[]{:S(2)}, u32[]{:S(2)}) collective-permute-start(bf16[256,2560]{1,0:T(8,128)(2,1)S(1)} %shard_map.221), channel_id=1, source_target_pairs={{0,2},{1,3},{2,0},{3,1},{4,6},{5,7},{6,4},{7,5},{8,10},{9,11},{10,... | collective-permute-start | bytes 3932168 | tf_op jit(solution)/shard_map/ppermute | solution.py:765
  439.7 27.0 %collective-permute-start.60 = (bf16[256,2560]{1,0:T(8,128)(2,1)S(1)}, bf16[256,2560]{1,0:T(8,128)(2,1)}, u32[]{:S(2)}, u32[]{:S(2)}) collective-permute-start(bf16[256,2560]{1,0:T(8,128)(2,1)S(1)} %constant_dynamic-update-slice_fusion.6.refs_0_), channel_id=1, source_target_pairs={{0,1},{1,0},{2,3},{3,2},{4,5},{5,4},{6,7},{7,6},{8,9},{9,8},{10,11... | collective-permute-start | bytes 3932168 | tf_op jit(solution)/shard_map/ppermute | solution.py:765
  440.0 24.2 %collective-permute-start.64 = (bf16[320,1344]{1,0:T(8,128)(2,1)S(1)}, bf16[320,1344]{1,0:T(8,128)(2,1)S(1)}, u32[]{:S(2)}, u32[]{:S(2)}) collective-permute-start(bf16[320,1344]{1,0:T(8,128)(2,1)S(1)} %shard_map.229), channel_id=1, source_target_pairs={{0,8},{1,9},{2,10},{3,11},{4,12},{5,13},{6,14},{7,15},{8,16},{9,17... | collective-permute-start | bytes 2580488 | tf_op jit(solution)/shard_map/ppermute | solution.py:765
  511.9 71.1 %reduce-scatter.6.cloned.1.call-start = ((), (), s32[]{:S(2)}) async-start(), calls=%async_computation.4 | async-start | bytes 1638400 | tf_op jit(solution)/shard_map/reduce_scatter | solution.py:819
  514.1 26.7 %collective-permute-start.74 = (bf16[4,160,480]{2,1,0:T(8,128)(2,1)}, bf16[4,160,480]{2,1,0:T(8,128)(2,1)S(1)}, u32[]{:S(2)}, u32[]{:S(2)}) collective-permute-start(bf16[4,160,480]{2,1,0:T(8,128)(2,1)} %copy-done.49), channel_id=1, source_target_pairs={{0,2},{1,3},{2,0},{3,1},{4,6},{5,7},{6,4},{7,5},{8,10},{9,11},{10,... | collective-permute-start | bytes 1843208 | tf_op jit(solution)/shard_map/ppermute | solution.py:765
  514.8 26.1 %collective-permute-start.73 = (bf16[4,160,480]{2,1,0:T(8,128)(2,1)}, bf16[4,160,480]{2,1,0:T(8,128)(2,1)S(1)}, u32[]{:S(2)}, u32[]{:S(2)}) collective-permute-start(bf16[4,160,480]{2,1,0:T(8,128)(2,1)} %copy-done.48), channel_id=1, source_target_pairs={{0,4},{1,5},{2,6},{3,7},{4,0},{5,1},{6,2},{7,3},{8,12},{9,13},{10,... | collective-permute-start | bytes 1843208 | tf_op jit(solution)/shard_map/ppermute | solution.py:765
  (134 other events, 1660.8 us)
Sparse Core Ops, SparseCore 0:
  13.1 40.2 all-gather.2
  160.3 56.4 reduce-scatter.3
  512.0 38.0 reduce-scatter.7
  552.8 30.0 reduce-scatter.5
